TPU v7x, 128 devices: a whole 4x4x4 slice. The times are simulated.
128 devices in a mesh: seq: 16 (over x, z_hi, core), win: 8 (over y, z_lo).
Axes of the slice: x: 4, y: 4, z: 4 (z_hi: 2, z_lo: 2; z = z_hi * 2 + z_lo), core: 2. Of those that a mesh axis runs over, the one named last changes fastest.
Arguments:
- tokens: bfloat16 [16, 2048, 512], P('win', 'seq'), may hold values from -6 to 6
- lengths: int32 [16], P('win'), may hold values from 1536 to 2048, as said below
- gain_one: float32 [512], replicated, may hold values from 0.1 to 1.9
- bias_one: float32 [512], replicated, may hold values from -3 to 3
- weight_query: bfloat16 [512, 512], replicated, may hold values from -0.25 to 0.25
- weight_key: bfloat16 [512, 512], replicated, may hold values from -0.25 to 0.25
- weight_value: bfloat16 [512, 512], replicated, may hold values from -0.25 to 0.25
- weight_out: bfloat16 [512, 512], replicated, may hold values from -2 to 2
- gain_two: float32 [512], replicated, may hold values from 0.1 to 1.9
- bias_two: float32 [512], replicated, may hold values from -3 to 3
- weight_gate: bfloat16 [512, 2048], replicated, may hold values from -0.25 to 0.25
- weight_up: bfloat16 [512, 2048], replicated, may hold values from -0.25 to 0.25
- weight_down: bfloat16 [2048, 512], replicated, may hold values from -0.25 to 0.25
- cotangent: bfloat16 [16, 2048, 512], P('win', 'seq'), may hold values from -6 to 6
Outputs:
- output: float32 [16, 2048, 512], P('win', 'seq')
- grad_tokens: float32 [16, 2048, 512], P('win', 'seq')
- grad_gain_one: float32 [512], replicated
- grad_bias_one: float32 [512], replicated
- grad_query: float32 [512, 512], replicated
- grad_key: float32 [512, 512], replicated
- grad_value: float32 [512, 512], replicated
- grad_out: float32 [512, 512], replicated
- grad_gain_two: float32 [512], replicated
- grad_bias_two: float32 [512], replicated
- grad_gate: float32 [512, 2048], replicated
- grad_up: float32 [512, 2048], replicated
- grad_down: float32 [2048, 512], replicated
Inputs may be any that keep to these rules, and one draw needn't show every extreme that they name: `lengths`: of the 2 consecutive windows that share an index of win, one, drawn from the seed, is longer than 1920; at least one window of all, drawn from the seed, has length 2048.
All inputs are finite; a program needn't handle non-finite values.
Results may differ from a plain program's by a relative error of at most 0.017.
Values may be sent and summed in bfloat16 or wider, within the bound.
No kernel may reach another device: no remote copies, remote signals or barrier semaphores. Data moves between devices by JAX's collectives and lax.ppermute only.
A program may use at most 192 MiB of HBM per device.

v0:
```python
import math

import jax
import jax.numpy as jnp
from jax import lax
from jax.sharding import PartitionSpec as P

HEADS = 16
HEAD_DIM = 32


epsilon = 1e-05
masked_score = -1e30


def in_one_piece(arrays, axis, dim, along):
    widths = [a.shape[along] for a in arrays]
    both = jnp.concatenate(arrays, axis=along)
    out = lax.all_gather(both, axis, axis=dim, tiled=True)
    return tuple(jnp.split(out, [sum(widths[:k]) for k in range(1, len(widths))], axis=along))


def layer_norm(values, gain, shift):
    center = values - jnp.mean(values, -1, keepdims=True)
    spread = jnp.mean(center * center, -1, keepdims=True)
    return center * lax.rsqrt(spread + epsilon) * gain + shift


def rotary(values, positions, direction):
    halves = values.reshape(values.shape[:-1] + (HEADS, 2, HEAD_DIM // 2))
    inverse = 10000.0 ** (-jnp.arange(HEAD_DIM // 2, dtype=jnp.float32) * (2.0 / HEAD_DIM))
    angles = positions.astype(jnp.float32)[:, None] * inverse[None, :]
    cosine = jnp.cos(angles)[:, None, :]
    sine = direction * jnp.sin(angles)[:, None, :]
    first = halves[..., 0, :]
    second = halves[..., 1, :]
    turned = jnp.stack([first * cosine - second * sine, second * cosine + first * sine], -2)
    return turned.reshape(values.shape)


def attend(carry_state, query_heads, key_part, value_part, key_start, lengths):
    row_peak, row_total, weighted = carry_state
    win_count, key_count, model_width = key_part.shape
    key_heads = key_part.reshape(win_count, key_count, HEADS, HEAD_DIM)
    value_heads = value_part.reshape(win_count, key_count, HEADS, HEAD_DIM)
    scores = jnp.einsum(
        "wqhd,wkhd->wqhk", query_heads, key_heads, preferred_element_type=jnp.float32
    ) * HEAD_DIM ** (-0.5)
    places = key_start + jnp.arange(key_count, dtype=jnp.int32)
    usable = places[None, :] < lengths[:, None]
    scores = jnp.where(usable[:, None, None, :], scores, masked_score)
    new_peak = jnp.maximum(row_peak, jnp.max(scores, -1))
    factor = jnp.exp(row_peak - new_peak)
    weight = jnp.exp(scores - new_peak[..., None])
    row_total = row_total * factor + jnp.sum(weight, -1)
    weighted = weighted * factor[..., None] + jnp.einsum(
        "wqhk,wkhd->wqhd",
        weight.astype(jnp.bfloat16),
        value_heads,
        preferred_element_type=jnp.float32,
    )
    return (new_peak, row_total, weighted)


def attend_piece(carry_state, query_heads, key_part, value_part, key_start, lengths):
    key_count = key_part.shape[1]
    block_size = math.gcd(key_count, 512)

    def attend_advance(state_now, number):
        offset = number * block_size
        key_block = lax.dynamic_slice_in_dim(key_part, offset, block_size, 1)
        value_block = lax.dynamic_slice_in_dim(value_part, offset, block_size, 1)
        return (
            attend(state_now, query_heads, key_block, value_block, key_start + offset, lengths),
            None,
        )

    carry_state, unused = lax.scan(
        attend_advance, carry_state, jnp.arange(key_count // block_size, dtype=jnp.int32)
    )
    return carry_state


def local(
    tokens,
    lengths,
    gain_one,
    bias_one,
    weight_query,
    weight_key,
    weight_value,
    weight_out,
    gain_two,
    bias_two,
    weight_gate,
    weight_up,
    weight_down,
    cotangent,
):
    win_count, seq_rows, model_width = tokens.shape
    tok_rows = win_count * seq_rows
    positions = lax.axis_index("seq") * seq_rows + jnp.arange(seq_rows, dtype=jnp.int32)
    inputs = tokens.astype(jnp.float32).reshape(tok_rows, model_width)
    normed_one, pull_one = jax.vjp(layer_norm, inputs, gain_one, bias_one)
    normed_low = normed_one.astype(jnp.bfloat16)
    query_raw = jnp.dot(normed_low, weight_query, preferred_element_type=jnp.float32).reshape(
        win_count, seq_rows, model_width
    )
    key_raw = jnp.dot(normed_low, weight_key, preferred_element_type=jnp.float32).reshape(
        win_count, seq_rows, model_width
    )
    value_raw = jnp.dot(normed_low, weight_value, preferred_element_type=jnp.float32).reshape(
        win_count, seq_rows, model_width
    )
    queries = rotary(query_raw, positions, 1.0).astype(jnp.bfloat16)
    keys_low = rotary(key_raw, positions, 1.0).astype(jnp.bfloat16)
    values_low = value_raw.astype(jnp.bfloat16)
    query_heads = queries.reshape(win_count, seq_rows, HEADS, HEAD_DIM)
    start_state = (
        jnp.full((win_count, seq_rows, HEADS), masked_score, jnp.float32),
        jnp.zeros((win_count, seq_rows, HEADS), jnp.float32),
        jnp.zeros((win_count, seq_rows, HEADS, HEAD_DIM), jnp.float32),
    )
    keys_all, values_all = in_one_piece((keys_low, values_low), "seq", 1, 0)
    row_peak, row_total, weighted = attend_piece(
        start_state, query_heads, keys_all, values_all, 0, lengths
    )
    log_total = row_peak + jnp.log(row_total)
    mixed = weighted / row_total[..., None]
    mixed_low = mixed.reshape(tok_rows, model_width).astype(jnp.bfloat16)
    residual = inputs + jnp.dot(mixed_low, weight_out, preferred_element_type=jnp.float32)
    normed_two, pull_two = jax.vjp(layer_norm, residual, gain_two, bias_two)
    normed_two_low = normed_two.astype(jnp.bfloat16)
    gate_pre = jnp.dot(normed_two_low, weight_gate, preferred_element_type=jnp.float32)
    up_pre = jnp.dot(normed_two_low, weight_up, preferred_element_type=jnp.float32)
    hidden = (gate_pre * jax.nn.sigmoid(gate_pre) * up_pre).astype(jnp.bfloat16)
    output = residual + jnp.dot(hidden, weight_down, preferred_element_type=jnp.float32)
    cot_rows = cotangent.reshape(tok_rows, model_width)
    grad_down = jnp.dot(hidden.T, cot_rows, preferred_element_type=jnp.float32)
    grad_hidden = jnp.dot(cot_rows, weight_down.T, preferred_element_type=jnp.float32)
    gate_sigmoid = jax.nn.sigmoid(gate_pre)
    grad_gate_pre = (
        grad_hidden * up_pre * gate_sigmoid * (1.0 + gate_pre * (1.0 - gate_sigmoid))
    ).astype(jnp.bfloat16)
    grad_up_pre = (grad_hidden * gate_pre * gate_sigmoid).astype(jnp.bfloat16)
    grad_gate = jnp.dot(normed_two_low.T, grad_gate_pre, preferred_element_type=jnp.float32)
    grad_up = jnp.dot(normed_two_low.T, grad_up_pre, preferred_element_type=jnp.float32)
    grad_normed_two = jnp.dot(
        grad_gate_pre, weight_gate.T, preferred_element_type=jnp.float32
    ) + jnp.dot(grad_up_pre, weight_up.T, preferred_element_type=jnp.float32)
    grad_resid_norm, grad_gain_two, grad_bias_two = pull_two(grad_normed_two)
    grad_residual = cot_rows.astype(jnp.float32) + grad_resid_norm
    grad_attended = grad_residual.astype(jnp.bfloat16)
    grad_out = jnp.dot(mixed_low.T, grad_attended, preferred_element_type=jnp.float32)
    grad_mixed = (
        jnp.dot(grad_attended, weight_out.T, preferred_element_type=jnp.float32)
        .astype(jnp.bfloat16)
        .reshape(win_count, seq_rows, HEADS, HEAD_DIM)
    )
    correction = jnp.sum(grad_mixed.astype(jnp.float32) * mixed, -1)
    key_count = keys_all.shape[1]
    block_size = math.gcd(key_count, 512)
    scale = HEAD_DIM ** (-0.5)

    def score_terms(
        query_block,
        grad_block,
        total_block,
        correct_block,
        key_heads,
        value_heads,
        key_offset,
        key_width,
    ):
        scores = (
            jnp.einsum(
                "wqhd,wkhd->wqhk", query_block, key_heads, preferred_element_type=jnp.float32
            )
            * scale
        )
        usable = (key_offset + jnp.arange(key_width, dtype=jnp.int32))[None, :] < lengths[:, None]
        scores = jnp.where(usable[:, None, None, :], scores, masked_score)
        probs = jnp.exp(scores - total_block[..., None])
        grad_probs = jnp.einsum(
            "wqhd,wkhd->wqhk", grad_block, value_heads, preferred_element_type=jnp.float32
        )
        grad_scores = (probs * (grad_probs - correct_block[..., None])).astype(jnp.bfloat16)
        return (probs, grad_scores)

    def query_block_grads(number, grad_queries):
        offset = number * block_size
        key_heads = lax.dynamic_slice_in_dim(keys_all, offset, block_size, 1).reshape(
            win_count, block_size, HEADS, HEAD_DIM
        )
        value_heads = lax.dynamic_slice_in_dim(values_all, offset, block_size, 1).reshape(
            win_count, block_size, HEADS, HEAD_DIM
        )
        probs, grad_scores = score_terms(
            query_heads,
            grad_mixed,
            log_total,
            correction,
            key_heads,
            value_heads,
            offset,
            block_size,
        )
        return (
            grad_queries
            + jnp.einsum(
                "wqhk,wkhd->wqhd", grad_scores, key_heads, preferred_element_type=jnp.float32
            )
            * scale
        )

    grad_queries = lax.fori_loop(
        0,
        key_count // block_size,
        query_block_grads,
        jnp.zeros((win_count, seq_rows, HEADS, HEAD_DIM), jnp.float32),
    )
    totals_all, corrects_all = in_one_piece((log_total, correction), "seq", 1, 0)
    own_key_heads = keys_low.reshape(win_count, seq_rows, HEADS, HEAD_DIM)
    own_value_heads = values_low.reshape(win_count, seq_rows, HEADS, HEAD_DIM)
    own_start = lax.axis_index("seq") * seq_rows
    empty_heads = jnp.zeros((win_count, seq_rows, HEADS, HEAD_DIM), jnp.float32)
    carry_state = (empty_heads, empty_heads)
    query_piece, grad_piece = in_one_piece((query_heads, grad_mixed), "seq", 1, 0)
    piece_rows = query_piece.shape[1]
    piece_block = math.gcd(piece_rows, 512)

    def fold_advance(state_now, number):
        grad_keys, grad_values = state_now
        offset = number * piece_block
        query_block = lax.dynamic_slice_in_dim(query_piece, offset, piece_block, 1)
        grad_block = lax.dynamic_slice_in_dim(grad_piece, offset, piece_block, 1)
        total_block = lax.dynamic_slice_in_dim(totals_all, offset, piece_block, 1)
        correct_block = lax.dynamic_slice_in_dim(corrects_all, offset, piece_block, 1)
        probs, grad_scores = score_terms(
            query_block,
            grad_block,
            total_block,
            correct_block,
            own_key_heads,
            own_value_heads,
            own_start,
            seq_rows,
        )
        grad_values = grad_values + jnp.einsum(
            "wqhk,wqhd->wkhd",
            probs.astype(jnp.bfloat16),
            grad_block,
            preferred_element_type=jnp.float32,
        )
        grad_keys = (
            grad_keys
            + jnp.einsum(
                "wqhk,wqhd->wkhd", grad_scores, query_block, preferred_element_type=jnp.float32
            )
            * scale
        )
        return ((grad_keys, grad_values), None)

    carry_state, unused = lax.scan(
        fold_advance, carry_state, jnp.arange(piece_rows // piece_block, dtype=jnp.int32)
    )
    own_grad_keys, own_grad_values = carry_state
    summed = jnp.concatenate(
        [
            own_grad_keys.reshape(win_count, seq_rows, model_width),
            own_grad_values.reshape(win_count, seq_rows, model_width),
        ],
        -1,
    )
    grad_query_raw = (
        rotary(grad_queries.reshape(win_count, seq_rows, model_width), positions, -1.0)
        .astype(jnp.bfloat16)
        .reshape(tok_rows, model_width)
    )
    grad_key_raw = (
        rotary(summed[..., :model_width], positions, -1.0)
        .astype(jnp.bfloat16)
        .reshape(tok_rows, model_width)
    )
    grad_value_raw = summed[..., model_width:].astype(jnp.bfloat16).reshape(tok_rows, model_width)
    grad_query = jnp.dot(normed_low.T, grad_query_raw, preferred_element_type=jnp.float32)
    grad_key = jnp.dot(normed_low.T, grad_key_raw, preferred_element_type=jnp.float32)
    grad_value = jnp.dot(normed_low.T, grad_value_raw, preferred_element_type=jnp.float32)
    grad_normed_one = (
        jnp.dot(grad_query_raw, weight_query.T, preferred_element_type=jnp.float32)
        + jnp.dot(grad_key_raw, weight_key.T, preferred_element_type=jnp.float32)
        + jnp.dot(grad_value_raw, weight_value.T, preferred_element_type=jnp.float32)
    )
    grad_input_norm, grad_gain_one, grad_bias_one = pull_one(grad_normed_one)
    grad_tokens = (grad_residual + grad_input_norm).reshape(win_count, seq_rows, model_width)
    (
        grad_query,
        grad_key,
        grad_value,
        grad_out,
        grad_gain_one,
        grad_bias_one,
        grad_gate,
        grad_up,
        grad_down,
        grad_gain_two,
        grad_bias_two,
    ) = lax.psum(
        (
            grad_query,
            grad_key,
            grad_value,
            grad_out,
            grad_gain_one,
            grad_bias_one,
            grad_gate,
            grad_up,
            grad_down,
            grad_gain_two,
            grad_bias_two,
        ),
        ("seq", "win"),
    )
    output_rows = output.reshape(win_count, seq_rows, model_width)
    return (
        output_rows,
        grad_tokens,
        grad_gain_one,
        grad_bias_one,
        grad_query,
        grad_key,
        grad_value,
        grad_out,
        grad_gain_two,
        grad_bias_two,
        grad_gate,
        grad_up,
        grad_down,
    )


def solution(mesh):
    return jax.shard_map(
        local,
        mesh=mesh,
        in_specs=(
            P("win", "seq", None),
            P("win"),
            P(),
            P(),
            P(),
            P(),
            P(),
            P(),
            P(),
            P(),
            P(),
            P(),
            P(),
            P("win", "seq", None),
        ),
        out_specs=(
            P("win", "seq", None),
            P("win", "seq", None),
            P(),
            P(),
            P(),
            P(),
            P(),
            P(),
            P(),
            P(),
            P(),
            P(),
            P(),
        ),
        check_vma=False,
    )
```

profile of v0, /device:TPU:1, one launch (start us, length us, event | category | flops | bytes accessed | tf_op | source)
XLA Modules:
  0.0 648.0 jit_solution(8732592033628694594)
XLA Ops:
  19.6 73.8 %all-gather.3.cloned.1.call-done = bf16[4,2048,512]{2,1,0:T(8,128)(2,1)} async-done(((bf16[4,128,512]{2,1,0:T(8,128)(2,1)}), bf16[4,2048,512]{2,1,0:T(8,128)(2,1)}) %all-gather.3.cloned.1.call-update) | async-done | bytes 8388624 | tf_op jit(solution)/shard_map/all_gather | solution.py:19
  93.4 6.3 fusion.106
  99.7 6.2 copy.65
  105.9 6.2 copy.64
  112.2 40.4 %while.42 = (s32[]{:T(128)}, f32[2,128,16]{1,2,0:T(8,128)S(1)}, f32[2,128,16]{1,2,0:T(8,128)S(1)}, f32[2,128,16,32]{1,3,2,0:T(8,128)}, s32[4]{0:T(128)S(1)}, /*i...) while((s32[]{:T(128)}, f32[2,128,16]{1,2,0:T(8,128)S(1)}, ...), condition=%wide.region_5.6_spmd.clone, body=%wide.region_2.5_spmd.clone.sunk | while | flops 291919360 | bytes 37232912 | solution.py:78
  152.6 2.5 fusion.104
  157.4 2.4 multiply_convert_fusion
  171.8 22.4 %all_gather.11 = f32[4,2048,16]{1,0,2:T(4,128)S(1)} all-gather(f32[4,128,16]{1,0,2:T(4,128)S(1)} %pad_maximum_fusion.3), channel_id=1, replica_groups=mesh['seq'=16,'win'=8] {'seq'}, dimensions={1}, use_global_device_ids=true | all-gather | bytes 557056 | tf_op jit(solution)/shard_map/all_gather | solution.py:19
  194.2 2.3 fusion.83
  196.5 2.8 fusion.114
  199.3 2.7 fusion.113
  202.0 2.8 fusion.115
  205.8 62.8 %while.43 = (s32[]{:T(128)}, f32[2,128,16,32]{1,3,2,0:T(8,128)}, bf16[2,2048,512]{1,2,0:T(8,128)(2,1)}, s32[2]{0:T(128)S(1)}, bf16[2,128,16,32]{1,3,2,0:T(8,128)...) while((s32[]{:T(128)}, f32[2,128,16,32]{1,3,2,0:T(8,128)}, ...), condition=%wide.region_12.13_spmd.clone, body=%wide.region_11.12_spmd.clone.sunk | while | flops 415630848 | bytes 25729228 | solution.py:216
  205.9 2.7 constant_dynamic-slice_fusion.13
  208.6 4.9 fusion.196
  213.5 8.2 %fusion.197 = f32[2,128,16,32]{1,3,2,0:T(8,128)} fusion(bf16[2,512,16,32]{1,3,2,0:T(8,128)(2,1)S(1)} %bitcast.289, f32[2,16,512,128]{3,2,1,0:T(8,128)} %fusion.196, f32[2,128,16]{1,2,0:T(8,128)S(1)} %get-tuple-element.918, f32[2,128,16]{1,2,0:T(8,128)S(1)} %get-tuple-element.915, pred[2,512]{1,0:T(4,128)(4,1)S(1)} %broadcast_compare_fusion.7, ...), kind=kOutput, calls=%fused_computation.31.clone.1 | convolution fusion | flops 281411584 | bytes 11830273 | tf_op jit(solution)/shard_map/while/body/eval_jaxpr/wqhk,wkhd->wqhd/dot_general | solution.py:210
  221.8 2.7 constant_dynamic-slice_fusion.13
  224.5 4.6 fusion.196
  229.1 8.0 %fusion.197 = f32[2,128,16,32]{1,3,2,0:T(8,128)} fusion(bf16[2,512,16,32]{1,3,2,0:T(8,128)(2,1)S(1)} %bitcast.289, f32[2,16,512,128]{3,2,1,0:T(8,128)} %fusion.196, f32[2,128,16]{1,2,0:T(8,128)S(1)} %get-tuple-element.918, f32[2,128,16]{1,2,0:T(8,128)S(1)} %get-tuple-element.915, pred[2,512]{1,0:T(4,128)(4,1)S(1)} %broadcast_compare_fusion.7, ...), kind=kOutput, calls=%fused_computation.31.clone.1 | convolution fusion | flops 281411584 | bytes 11830273 | tf_op jit(solution)/shard_map/while/body/eval_jaxpr/wqhk,wkhd->wqhd/dot_general | solution.py:210
  237.2 2.7 constant_dynamic-slice_fusion.13
  239.9 4.6 fusion.196
  244.5 8.0 %fusion.197 = f32[2,128,16,32]{1,3,2,0:T(8,128)} fusion(bf16[2,512,16,32]{1,3,2,0:T(8,128)(2,1)S(1)} %bitcast.289, f32[2,16,512,128]{3,2,1,0:T(8,128)} %fusion.196, f32[2,128,16]{1,2,0:T(8,128)S(1)} %get-tuple-element.918, f32[2,128,16]{1,2,0:T(8,128)S(1)} %get-tuple-element.915, pred[2,512]{1,0:T(4,128)(4,1)S(1)} %broadcast_compare_fusion.7, ...), kind=kOutput, calls=%fused_computation.31.clone.1 | convolution fusion | flops 281411584 | bytes 11830273 | tf_op jit(solution)/shard_map/while/body/eval_jaxpr/wqhk,wkhd->wqhd/dot_general | solution.py:210
  252.6 2.7 constant_dynamic-slice_fusion.13
  255.3 4.6 fusion.196
  259.9 8.7 %fusion.197 = f32[2,128,16,32]{1,3,2,0:T(8,128)} fusion(bf16[2,512,16,32]{1,3,2,0:T(8,128)(2,1)S(1)} %bitcast.289, f32[2,16,512,128]{3,2,1,0:T(8,128)} %fusion.196, f32[2,128,16]{1,2,0:T(8,128)S(1)} %get-tuple-element.918, f32[2,128,16]{1,2,0:T(8,128)S(1)} %get-tuple-element.915, pred[2,512]{1,0:T(4,128)(4,1)S(1)} %broadcast_compare_fusion.7, ...), kind=kOutput, calls=%fused_computation.31.clone.1 | convolution fusion | flops 281411584 | bytes 11830273 | tf_op jit(solution)/shard_map/while/body/eval_jaxpr/wqhk,wkhd->wqhd/dot_general | solution.py:210
  268.7 12.0 %fusion.105 = (bf16[2,2048,16,32]{1,0,3,2:T(2,128)(2,1)}, bf16[2,2048,16,32]{1,0,3,2:T(2,128)(2,1)}) fusion(bf16[4,2048,16,32]{1,0,3,2:T(4,128)(2,1)} %all-gather.5.cloned.1.call-done), kind=kLoop, calls=%fused_computation.161 | loop fusion | bytes 16777216 | tf_op jit(solution)/shard_map/split | solution.py:20
  281.1 115.6 %while.44 = (s32[]{:T(128)}, f32[2,128,16,32]{1,3,2,0:T(8,128)}, f32[2,128,16,32]{1,3,2,0:T(8,128)}, s32[4]{0:T(128)}, bf16[2,2048,16,32]{1,0,3,2:T(2,128)(2,1)}...) while((s32[]{:T(128)}, f32[2,128,16,32]{1,3,2,0:T(8,128)}, ...), condition=%wide.region_14.15_spmd.clone, body=%wide.region_13.14_spmd.clone.sunk | while | flops 558498176 | bytes 36898804 | solution.py:264
  284.8 4.6 constant_dynamic-slice_fusion.14
  289.4 4.6 fusion.206
  294.0 10.2 %fusion.207 = f32[2,128,16,32]{1,3,2,0:T(8,128)} fusion(f32[2,16,512,128]{3,2,1,0:T(8,128)} %fusion.206, f32[2,512,16]{1,2,0:T(8,128)S(1)} %copy.156, f32[2,512,16]{1,2,0:T(8,128)S(1)} %copy.157, pred[2,128]{1,0:T(4,128)(4,1)} %broadcast_compare_fusion.8, bf16[2,128,16,32]{1,3,2,0:T(8,128)(2,1)} %get-tuple-element.878, ...), kind=kOutput, calls=%fused_computation.52.clone.1 | convolution fusion | flops 281411584 | bytes 11927809 | tf_op jit(solution)/shard_map/while/body/eval_jaxpr/wqhk,wqhd->wkhd/dot_general | solution.py:257
  304.2 5.8 fusion.208
  313.5 4.6 constant_dynamic-slice_fusion.14
  318.1 4.6 fusion.206
  322.7 10.3 %fusion.207 = f32[2,128,16,32]{1,3,2,0:T(8,128)} fusion(f32[2,16,512,128]{3,2,1,0:T(8,128)} %fusion.206, f32[2,512,16]{1,2,0:T(8,128)S(1)} %copy.156, f32[2,512,16]{1,2,0:T(8,128)S(1)} %copy.157, pred[2,128]{1,0:T(4,128)(4,1)} %broadcast_compare_fusion.8, bf16[2,128,16,32]{1,3,2,0:T(8,128)(2,1)} %get-tuple-element.878, ...), kind=kOutput, calls=%fused_computation.52.clone.1 | convolution fusion | flops 281411584 | bytes 11927809 | tf_op jit(solution)/shard_map/while/body/eval_jaxpr/wqhk,wqhd->wkhd/dot_general | solution.py:257
  333.0 5.9 fusion.208
  342.3 4.6 constant_dynamic-slice_fusion.14
  346.9 4.6 fusion.206
  351.5 10.3 %fusion.207 = f32[2,128,16,32]{1,3,2,0:T(8,128)} fusion(f32[2,16,512,128]{3,2,1,0:T(8,128)} %fusion.206, f32[2,512,16]{1,2,0:T(8,128)S(1)} %copy.156, f32[2,512,16]{1,2,0:T(8,128)S(1)} %copy.157, pred[2,128]{1,0:T(4,128)(4,1)} %broadcast_compare_fusion.8, bf16[2,128,16,32]{1,3,2,0:T(8,128)(2,1)} %get-tuple-element.878, ...), kind=kOutput, calls=%fused_computation.52.clone.1 | convolution fusion | flops 281411584 | bytes 11927809 | tf_op jit(solution)/shard_map/while/body/eval_jaxpr/wqhk,wqhd->wkhd/dot_general | solution.py:257
  361.8 5.9 fusion.208
  371.1 4.6 constant_dynamic-slice_fusion.14
  375.7 4.6 fusion.206
  380.3 10.3 %fusion.207 = f32[2,128,16,32]{1,3,2,0:T(8,128)} fusion(f32[2,16,512,128]{3,2,1,0:T(8,128)} %fusion.206, f32[2,512,16]{1,2,0:T(8,128)S(1)} %copy.156, f32[2,512,16]{1,2,0:T(8,128)S(1)} %copy.157, pred[2,128]{1,0:T(4,128)(4,1)} %broadcast_compare_fusion.8, bf16[2,128,16,32]{1,3,2,0:T(8,128)(2,1)} %get-tuple-element.878, ...), kind=kOutput, calls=%fused_computation.52.clone.1 | convolution fusion | flops 281411584 | bytes 11927809 | tf_op jit(solution)/shard_map/while/body/eval_jaxpr/wqhk,wqhd->wkhd/dot_general | solution.py:257
  390.6 5.9 fusion.208
  405.4 2.9 convolution_add_fusion.1
  409.9 65.1 %all-reduce = (f32[512]{0:T(512)}, f32[512]{0:T(512)}, f32[512]{0:T(512)}, f32[512]{0:T(512)}) all-reduce(f32[512]{0:T(512)S(1)} %get-tuple-element.464, f32[512]{0:T(512)S(1)} %get-tuple-element.467, f32[512]{0:T(512)S(1)} %copy-done.50, f32[512]{0:T(512)S(1)} %copy-done.51), channel_id=1, replica_groups=mesh['seq'=16,'win'=8] {'seq','win'}, use_global_device_ids=true, to_apply=%region_18.19 | all-reduce | flops 2048 | bytes 16384 | tf_op jit(solution)/shard_map/psum | solution.py:308
  477.0 148.0 %all-reduce.4.cloned.1.call-done = (f32[512,512]{1,0:T(8,128)}, f32[512,512]{1,0:T(8,128)}, f32[512,512]{1,0:T(8,128)}, f32[512,512]{1,0:T(8,128)}, f32[512,2048...) async-done(((f32[512,512]{1,0:T(8,128)}, f32[512,512]{1,0:T(8,128)}, f32[512,512]{1,0:T(8,128)}, f32[512,512]{1,0:T(8,128)}, f32[512,2048]{1,0:T(8,128)}, ...) | async-done | bytes 16777232 | tf_op jit(solution)/shard_map/psum | solution.py:308
  625.1 2.4 copy.192
  627.5 2.4 copy.193
  (269 shorter events, 100.4 us)
Async XLA Ops:
  7.2 150.2 %copy-start = (bf16[2048,512]{1,0:T(8,128)(2,1)S(1)}, bf16[2048,512]{1,0:T(8,128)(2,1)}, u32[]{:S(2)}) copy-start(bf16[2048,512]{1,0:T(8,128)(2,1)} %param.32) | copy-start | bytes 6291460
  7.2 86.2 %all-gather.3.cloned.1.call-start = ((), (), s32[]{:S(2)}) async-start(), calls=%async_computation | async-start | bytes 8912896 | tf_op jit(solution)/shard_map/all_gather | solution.py:19
  13.2 5.3 copy-start.7
  14.6 3.9 copy-start.24
  15.7 3.9 copy-start.41
  15.8 83.9 %copy-start.3 = (bf16[2,128,16,2,16]{1,4,3,2,0:T(8,128)(2,1)}, bf16[2,128,16,2,16]{1,4,3,2,0:T(8,128)(2,1)S(1)}, u32[]{:S(2)}) copy-start(bf16[2,128,16,2,16]{1,4,3,2,0:T(8,128)(2,1)S(1)} %maximum_convert_fusion) | copy-start | bytes 786436
  16.8 251.8 %all-gather.5.cloned.1.call-start = ((), (), s32[]{:S(2)}) async-start(), calls=%async_computation.1 | async-start | bytes 8912896 | tf_op jit(solution)/shard_map/all_gather | solution.py:19
  105.9 6.2 copy-start.43
  112.1 43.0 %copy-start.5 = (bf16[2,128,512]{2,1,0:T(8,128)(2,1)S(1)}, bf16[2,128,512]{2,1,0:T(8,128)(2,1)}, u32[]{:S(2)}) copy-start(bf16[2,128,512]{2,1,0:T(8,128)(2,1)} %param.20) | copy-start | bytes 786436
  112.1 43.0 %copy-start.31 = (bf16[512,512]{1,0:T(8,128)(2,1)S(1)}, bf16[512,512]{1,0:T(8,128)(2,1)}, u32[]{:S(2)}) copy-start(bf16[512,512]{1,0:T(8,128)(2,1)} %param.27) | copy-start | bytes 1572868
  112.1 43.6 %copy-start.48 = (f32[512]{0:T(512)S(1)}, f32[512]{0:T(512)}, u32[]{:S(2)}) copy-start(f32[512]{0:T(512)} %param.28) | copy-start | bytes 6148
  112.1 43.6 %copy-start.49 = (f32[512]{0:T(512)S(1)}, f32[512]{0:T(512)}, u32[]{:S(2)}) copy-start(f32[512]{0:T(512)} %param.29) | copy-start | bytes 6148
  152.5 3.4 copy-start.29
  152.5 4.1 copy-start.28
  155.1 2.3 copy-start.25
  155.5 6.5 copy-start.1
  159.8 2.2 copy-start.35
  159.8 2.2 copy-start.37
  160.5 2.6 copy-start.32
  162.3 34.2 %copy-start.10 = (f32[256,512]{1,0:T(8,128)}, f32[256,512]{1,0:T(8,128)S(1)}, u32[]{:S(2)}) copy-start(f32[256,512]{1,0:T(8,128)S(1)} %get-tuple-element.543) | copy-start | bytes 1572868
  167.7 457.4 %all-reduce.4.cloned.1.call-start = ((), (), s32[]{:S(2)}) async-start(), calls=%async_computation.2 | async-start | bytes 33554432 | tf_op jit(solution)/shard_map/psum | solution.py:308
  169.7 26.8 %copy-start.38 = (bf16[256,2048]{1,0:T(8,128)(2,1)S(1)}, bf16[256,2048]{1,0:T(8,128)(2,1)}, u32[]{:S(2)}) copy-start(bf16[256,2048]{1,0:T(8,128)(2,1)} %copy-done.37) | copy-start | bytes 3145732
  196.5 2.8 copy-start.36
  199.3 2.7 copy-start.9
  199.3 2.7 copy-start.16
  268.7 12.5 %copy-start.4 = (bf16[2,128,16,2,16]{1,4,3,2,0:T(8,128)(2,1)S(1)}, bf16[2,128,16,2,16]{1,4,3,2,0:T(8,128)(2,1)}, u32[]{:S(2)}) copy-start(bf16[2,128,16,2,16]{1,4,3,2,0:T(8,128)(2,1)} %copy-done.3) | copy-start | bytes 786436
  281.1 117.0 %copy-start.42 = (f32[128,16]{0,1:T(8,128)S(1)}, f32[128,16]{0,1:T(8,128)}, u32[]{:S(2)}) copy-start(f32[128,16]{0,1:T(8,128)} %copy-done.41) | copy-start | bytes 24580
  396.7 3.5 copy-start.8
  398.1 2.1 copy-start.17
  399.9 3.0 copy-start.19
  405.3 3.0 copy-start.20
  405.3 3.0 copy-start.30
  405.3 3.3 copy-start.22
  405.3 3.4 copy-start.26
  405.3 3.7 copy-start.6
  405.3 3.7 copy-start.18
  405.3 3.7 copy-start.27
  405.3 3.7 copy-start.44
  405.3 3.7 copy-start.45
  405.3 4.2 copy-start.47
  405.4 4.5 copy-start.50
  405.4 4.5 copy-start.51
  405.4 69.6 %copy-start.11 = (f32[256,512]{1,0:T(8,128)S(1)}, f32[256,512]{1,0:T(8,128)}, u32[]{:S(2)}) copy-start(f32[256,512]{1,0:T(8,128)} %copy-done.10) | copy-start | bytes 1572868
  625.1 4.8 copy-start.34
  625.1 5.8 copy-start.33
  625.1 6.7 %copy-start.14 = (f32[512,2048]{1,0:T(8,128)S(1)}, f32[512,2048]{1,0:T(8,128)}, u32[]{:S(2)}) copy-start(f32[512,2048]{1,0:T(8,128)} %get-tuple-element.933) | copy-start | bytes 12582916
  631.8 3.7 copy-start.13
  635.5 3.7 copy-start.12
  (13 other events, 16.1 us)
Sparse Core Ops, SparseCore 0:
  16.9 76.3 all-gather.2
  167.8 98.5 all-gather.4
  404.4 220.6 all-reduce.3
where the time goes:
time: 652 us; the launch traced here: 648 us
  waiting for transfers between devices  222 us (34%)
  matrix products  179 us (27%)
  local copies, waits for them, and re-layouts  110 us (17%)
  blocking collectives  87.4 us (13%)
  other arithmetic  28.8 us (4%)
  between operations  14.7 us (2%)
    psum x1, waiting for transfers between devices, local(): lax.psum((grad_query, grad_key, grad_value, grad_out, grad_gain_one, grad...  148 us
    all_gather x2, waiting for transfers between devices, in_one_piece(): out = lax.all_gather(both, axis, axis=dim, tiled=True)  73.8 us
    psum x1, blocking collectives, local(): lax.psum((grad_query, grad_key, grad_value, grad_out, grad_gain_one, grad...  65.1 us
    dot_general x4, matrix products, fold_advance(): jnp.einsum('wqhk,wqhd->wkhd', grad_scores, query_block, preferred_element...  41 us
    dot_general x8, matrix products, score_terms(): jnp.einsum('wqhd,wkhd->wqhk', query_block, key_heads, preferred_element_t...  37.1 us
    unnamed x114, local copies, waits for them, and re-layouts  34.3 us
    dot_general x4, matrix products, query_block_grads(): jnp.einsum('wqhk,wkhd->wqhd', grad_scores, key_heads, preferred_element_t...  33 us
    dot_general x4, matrix products, fold_advance(): jnp.einsum('wqhk,wqhd->wkhd', probs.astype(jnp.bfloat16), grad_block, pre...  23.5 us
  transfers between devices with their start and end apart: 3, of which 2 were waited for; matrix products, arithmetic and copies ran while one was open for 13% of the time, Pallas kernels for 0%

commit v1 on v0

v1 whole, which is shorter than its diff:
```python
import functools
import math

import jax
import jax.numpy as jnp
import numpy as np
from jax import lax
from jax.experimental import pallas as pl
from jax.experimental.pallas import tpu as pltpu
from jax.sharding import Mesh
from jax.sharding import PartitionSpec as P

HEADS = 16
HEAD_DIM = 32
HALF = HEAD_DIM // 2
PARTS = 3 * HEAD_DIM
LENGTH = 2048
epsilon = 1e-05
masked_score = -1e30
BF = jnp.bfloat16
F32 = jnp.float32
inv_root = HEAD_DIM ** (-0.5)
score_scale = inv_root * math.log2(math.e)
VMEM_LIMIT = 60 * 1024 * 1024


def mm(a, b):
    return jnp.dot(a, b, preferred_element_type=F32)


def mm_nt(a, b):
    return lax.dot_general(a, b, (((1,), (1,)), ((), ())), preferred_element_type=F32)


def mm_tn(a, b):
    return lax.dot_general(a, b, (((0,), (0,)), ((), ())), preferred_element_type=F32)


def normalize(x):
    center = x - jnp.mean(x, -1, keepdims=True)
    rstd = lax.rsqrt(jnp.mean(center * center, -1, keepdims=True) + epsilon)
    return center * rstd, rstd


def norm_back(dh, gain, xhat, rstd):
    dxhat = dh * gain
    a = jnp.mean(dxhat, -1, keepdims=True)
    b = jnp.mean(dxhat * xhat, -1, keepdims=True)
    return rstd * (dxhat - a - xhat * b)


def rotate(block, cosine, sine):
    a, b = block[:HALF], block[HALF:]
    return jnp.concatenate([a * cosine - b * sine, b * cosine + a * sine], 0)


def qkv_kernel(place, tok, gain, bias, wq, wk, wv, cosine, sine, out, normed):
    xhat, _ = normalize(tok[...].astype(F32))
    normed[...] = xhat.astype(BF)
    h1 = (xhat * gain[...] + bias[...]).astype(BF)
    cos = jnp.concatenate([cosine[...]] * 2, 1)
    sin = jnp.concatenate([sine[...]] * 2, 1)
    for n, w in enumerate((wq, wk, wv)):
        t = mm(h1, w[...]).T
        for h in range(HEADS):
            block = t[h * HEAD_DIM : (h + 1) * HEAD_DIM]
            if n < 2:
                block = rotate(block, cos, sin)
            block = block.astype(BF)
            for k in range(2):
                out[h, k, n * HEAD_DIM : (n + 1) * HEAD_DIM, :] = block[:, k * 128 : (k + 1) * 128]


def whole(*shape):
    return pl.BlockSpec(shape, lambda *_: (0,) * len(shape))


def qkv_call(place, tok, gain, bias, wq, wk, wv, cos, sin):
    rows, width = tok.shape
    table = pl.BlockSpec((HALF, 128), lambda i, p: (0, p[0]))
    return pl.pallas_call(
        qkv_kernel,
        grid_spec=pltpu.PrefetchScalarGridSpec(
            num_scalar_prefetch=1,
            grid=(1,),
            in_specs=[whole(rows, width)]
            + [whole(1, width)] * 2
            + [whole(width, width)] * 3
            + [table, table],
            out_specs=(whole(HEADS, 2, PARTS, 128), whole(rows, width)),
        ),
        out_shape=(
            jax.ShapeDtypeStruct((HEADS, 2, PARTS, 128), BF),
            jax.ShapeDtypeStruct((rows, width), BF),
        ),
        compiler_params=pltpu.CompilerParams(vmem_limit_bytes=VMEM_LIMIT),
        name="qkv_forward",
    )(place, tok, gain, bias, wq, wk, wv, cos, sin)


def gather_rows(ref, w, lo, n):
    return jnp.concatenate([ref[s, w, lo : lo + n, :] for s in range(HEADS)], axis=1)


def split2(x):
    hi = x.astype(BF)
    return hi, (x - hi.astype(F32)).astype(BF)


def split3(x):
    hi = x.astype(BF)
    rest = x - hi.astype(F32)
    mid = rest.astype(BF)
    return hi, mid, (rest - mid.astype(F32)).astype(BF)


def key_rows(kt, length):
    place = lax.broadcasted_iota(jnp.int32, (16, LENGTH), 1)
    row = lax.broadcasted_iota(jnp.int32, (16, LENGTH), 0)
    mask = jnp.where(place < length, 0.0, masked_score)
    extra = jnp.where(row == 0, mask, jnp.where(row < 4, 1.0, 0.0)).astype(BF)
    zeros = jnp.zeros((48, LENGTH), BF)
    return jnp.concatenate([kt, kt, extra, zeros], 0).T


TQ = 256


def attend_kernel(lengths, qkv, out, mixed, total, kaug, qaug, vaug):
    for w in range(2):
        kt = gather_rows(qkv, w, 32, 32)
        kaug[...] = key_rows(kt, lengths[w])
        qs = gather_rows(qkv, w, 0, 32).astype(F32) * score_scale
        hi, lo = split2(qs)
        row = lax.broadcasted_iota(jnp.int32, (64, LENGTH), 0)
        qaug[...] = jnp.concatenate([hi, lo, jnp.where(row == 0, 1.0, 0.0).astype(BF)], 0)
        row = lax.broadcasted_iota(jnp.int32, (16, LENGTH), 0)
        vaug[...] = jnp.concatenate(
            [gather_rows(qkv, w, 64, 32), jnp.where(row == 0, 1.0, 0.0).astype(BF)], 0
        )

        def tile(t, carry):
            cols = pl.ds(pl.multiple_of(t * TQ, TQ), TQ)
            st = mm(kaug[...], qaug[:, cols])
            peak = jnp.max(st, 0, keepdims=True)
            p = jnp.exp2(st - peak).astype(BF)
            o = mm(vaug[...], p)
            norm = o[32:33]
            ot = o[:32] / norm
            mixed[w, :, cols] = ot
            total[w, :, cols] = peak + jnp.log2(norm)
            for j in range(TQ // 128):
                out[t * (TQ // 128) + j, w] = ot[:, j * 128 : (j + 1) * 128].astype(BF)
            return carry

        lax.fori_loop(0, LENGTH // TQ, tile, 0)


SMEM = pl.BlockSpec(memory_space=pltpu.SMEM)
VM = pl.BlockSpec(memory_space=pltpu.VMEM)


def attend_call(lengths, qkv):
    return pl.pallas_call(
        attend_kernel,
        out_shape=(
            jax.ShapeDtypeStruct((HEADS, 2, HEAD_DIM, 128), BF),
            jax.ShapeDtypeStruct((2, HEAD_DIM, LENGTH), F32),
            jax.ShapeDtypeStruct((2, 1, LENGTH), F32),
        ),
        in_specs=[SMEM, VM],
        out_specs=(VM, VM, VM),
        scratch_shapes=[
            pltpu.VMEM((LENGTH, 128), BF),
            pltpu.VMEM((128, LENGTH), BF),
            pltpu.VMEM((48, LENGTH), BF),
        ],
        compiler_params=pltpu.CompilerParams(vmem_limit_bytes=VMEM_LIMIT),
        name="attend_forward",
    )(lengths, qkv)


def attend_back_kernel(
    lengths, qkv, dot_in, mixed, total, cosine, sine, normed, wt, gain, bias, vec_in,
    out, grads, kaug, qaug, vaug, doaug, right, dkv, dqs,
):
    projected = None
    sums = None
    for w in range(2):
        kt = gather_rows(qkv, w, 32, 32)
        kaug[...] = key_rows(kt, lengths[w])
        qt = gather_rows(qkv, w, 0, 32)
        hi, lo = split2(qt.astype(F32) * score_scale)
        row = lax.broadcasted_iota(jnp.int32, (16, LENGTH), 0)

        def rows_of(first, second, third, fourth):
            return jnp.where(
                row == 0,
                first,
                jnp.where(
                    row == 1, second, jnp.where(row == 2, third, jnp.where(row == 3, fourth, 0.0))
                ),
            ).astype(BF)

        l1, l2, l3 = (v.astype(F32) for v in split3(-total[w]))
        qaug[...] = jnp.concatenate(
            [hi, lo, rows_of(1.0, l1, l2, l3), jnp.zeros((48, LENGTH), BF)], 0
        )
        do = gather_rows(dot_in, w, 0, 32)
        delta = jnp.sum(do.astype(F32) * mixed[w], 0, keepdims=True)
        d1, d2, d3 = (v.astype(F32) for v in split3(-delta))
        doaug[...] = jnp.concatenate(
            [do, rows_of(d1, d2, d3, 0.0), jnp.zeros((80, LENGTH), BF)], 0
        )
        vaug[...] = jnp.concatenate(
            [
                gather_rows(qkv, w, 64, 32),
                jnp.where(row < 3, 1.0, 0.0).astype(BF),
                jnp.zeros((80, LENGTH), BF),
            ],
            0,
        ).T
        right[...] = jnp.concatenate([qt, do, jnp.zeros((64, LENGTH), BF)], 0).T
        dkv[...] = jnp.zeros_like(dkv)
        lane = lax.broadcasted_iota(jnp.int32, (TQ, 128), 1)

        def tile(t, carry):
            cols = pl.ds(pl.multiple_of(t * TQ, TQ), TQ)
            st = mm(kaug[...], qaug[:, cols])
            probs = jnp.exp2(st)
            ds = (probs * mm(vaug[...], doaug[:, cols])).astype(BF)
            both = jnp.concatenate([ds, probs.astype(BF)], 1)
            r = right[cols, :]
            zero = jnp.zeros_like(r)
            pair = jnp.concatenate(
                [jnp.where(lane < 32, r, zero), jnp.where(lane < 32, zero, r)], 0
            )
            dkv[...] += mm(both, pair)
            dq = mm(kt, ds) * inv_root
            dq = rotate(dq, cosine[:, cols], -sine[:, cols])
            dq = dq.astype(BF)
            dqs[:, cols] = dq
            for j in range(TQ // 128):
                out[t * (TQ // 128) + j, w, 0:32, :] = dq[:, j * 128 : (j + 1) * 128]
            return carry

        lax.fori_loop(0, LENGTH // TQ, tile, 0)
        back = dkv[...].T
        dk = rotate(back[:32] * inv_root, cosine[...], -sine[...]).astype(BF)
        dv = back[32:64].astype(BF)
        for s in range(HEADS):
            out[s, w, 32:64, :] = dk[:, s * 128 : (s + 1) * 128]
            out[s, w, 64:96, :] = dv[:, s * 128 : (s + 1) * 128]
        d = jnp.concatenate([dqs[...], dk, dv], 0)
        x = jnp.concatenate([normed[s, w * 128 : (w + 1) * 128, :] for s in range(HEADS)], 0)
        part = mm(d, x)
        part_sum = jnp.sum(d.astype(F32), 1, keepdims=True)
        projected = part if w == 0 else projected + part
        sums = part_sum if w == 0 else sums + part_sum
    columns = wt[...].astype(F32)
    grads[0:PARTS] = (projected * gain[...] + sums * bias[...]).astype(BF)
    row = lax.broadcasted_iota(jnp.int32, (32, 512), 0)
    dgain = jnp.sum(columns * projected, 0, keepdims=True)
    dbias = jnp.sum(columns * sums, 0, keepdims=True)
    tail = jnp.where(
        row == 0,
        dgain,
        jnp.where(
            row == 1,
            dbias,
            jnp.where(row == 2, vec_in[0:1], jnp.where(row == 3, vec_in[1:2], 0.0)),
        ),
    )
    grads[PARTS:128] = tail.astype(BF)


def attend_back_call(lengths, qkv, do, mixed, total, cos, sin, normed, wt, gain, bias, vecs):
    return pl.pallas_call(
        attend_back_kernel,
        out_shape=(
            jax.ShapeDtypeStruct((HEADS, 2, PARTS, 128), BF),
            jax.ShapeDtypeStruct((128, 512), BF),
        ),
        in_specs=[SMEM] + [VM] * 11,
        out_specs=(VM, VM),
        scratch_shapes=[
            pltpu.VMEM((LENGTH, 128), BF),
            pltpu.VMEM((128, LENGTH), BF),
            pltpu.VMEM((LENGTH, 128), BF),
            pltpu.VMEM((128, LENGTH), BF),
            pltpu.VMEM((LENGTH, 128), BF),
            pltpu.VMEM((LENGTH, 128), F32),
            pltpu.VMEM((32, LENGTH), BF),
        ],
        compiler_params=pltpu.CompilerParams(vmem_limit_bytes=VMEM_LIMIT),
        name="attend_backward",
    )(lengths, qkv, do, mixed, total, cos, sin, normed, wt, gain, bias, vecs)


FC = 512


def ff_kernel(
    tok, ob, wout, gain, bias, wg, wu, wd, cot,
    output, gwg, gwu, gwd, gwout, vecs, dres, dot_out,
    res, h2, h2t, dh2, obt,
):
    step = pl.program_id(0)
    last = pl.num_programs(0) - 1

    @pl.when(step == 0)
    def first():
        for k in range(2):
            obt[:, k * 128 : (k + 1) * 128] = ob[:, k].reshape(512, 128)
        r = tok[...].astype(F32) + mm(obt[...].T, wout[...])
        xhat, _ = normalize(r)
        h = (xhat * gain[...] + bias[...]).astype(BF)
        res[...] = r
        h2[...] = h
        h2t[...] = h.T
        output[...] = r
        dh2[...] = jnp.zeros_like(dh2)

    gate = mm(h2[...], wg[...])
    up = mm(h2[...], wu[...])
    dm = mm_nt(cot[...], wd[...])
    sg = jax.nn.sigmoid(gate)
    act = gate * sg
    m = (act * up).astype(BF)
    dgate = (dm * up * (sg * (1.0 + gate - act))).astype(BF)
    dup = (dm * act).astype(BF)
    output[...] += mm(m, wd[...])
    gwd[...] = mm(m.T, cot[...])
    gwg[...] = mm(h2t[...], dgate)
    gwu[...] = mm(h2t[...], dup)
    dh2[...] += mm_nt(dgate, wg[...]) + mm_nt(dup, wu[...])

    @pl.when(step == last)
    def final():
        xhat, rstd = normalize(res[...])
        dh = dh2[...]
        vecs[0:1] = jnp.sum(dh * xhat, 0, keepdims=True)
        vecs[1:2] = jnp.sum(dh, 0, keepdims=True)
        dr = cot[...].astype(F32) + norm_back(dh, gain[...], xhat, rstd)
        dres[...] = dr
        da = dr.astype(BF)
        gwout[...] = mm(obt[...], da)
        do = mm_nt(wout[...], da).astype(BF)
        for k in range(2):
            dot_out[:, k] = do[:, k * 128 : (k + 1) * 128].reshape(HEADS, HEAD_DIM, 128)


def ff_call(tok, ob, wout, gain, bias, wg, wu, wd, cot):
    rows, width = tok.shape
    ff = wg.shape[1]

    return pl.pallas_call(
        ff_kernel,
        grid=(ff // FC,),
        in_specs=[
            whole(rows, width),
            whole(HEADS, 2, HEAD_DIM, 128),
            whole(width, width),
            whole(1, width),
            whole(1, width),
            pl.BlockSpec((width, FC), lambda i: (0, i)),
            pl.BlockSpec((width, FC), lambda i: (0, i)),
            pl.BlockSpec((FC, width), lambda i: (i, 0)),
            whole(rows, width),
        ],
        out_specs=(
            whole(rows, width),
            pl.BlockSpec((width, FC), lambda i: (0, i)),
            pl.BlockSpec((width, FC), lambda i: (0, i)),
            pl.BlockSpec((FC, width), lambda i: (i, 0)),
            whole(width, width),
            whole(2, width),
            whole(rows, width),
            whole(HEADS, 2, HEAD_DIM, 128),
        ),
        out_shape=(
            jax.ShapeDtypeStruct((rows, width), F32),
            jax.ShapeDtypeStruct((width, ff), F32),
            jax.ShapeDtypeStruct((width, ff), F32),
            jax.ShapeDtypeStruct((ff, width), F32),
            jax.ShapeDtypeStruct((width, width), F32),
            jax.ShapeDtypeStruct((2, width), F32),
            jax.ShapeDtypeStruct((rows, width), F32),
            jax.ShapeDtypeStruct((HEADS, 2, HEAD_DIM, 128), BF),
        ),
        scratch_shapes=[
            pltpu.VMEM((rows, width), F32),
            pltpu.VMEM((rows, width), BF),
            pltpu.VMEM((width, rows), BF),
            pltpu.VMEM((rows, width), F32),
            pltpu.VMEM((width, rows), BF),
        ],
        compiler_params=pltpu.CompilerParams(vmem_limit_bytes=VMEM_LIMIT),
        name="feed_forward",
    )(tok, ob, wout, gain, bias, wg, wu, wd, cot)


def proj_back_kernel(tok, dres, dqkv, wq, wk, wv, gain, gtok):
    xhat, rstd = normalize(tok[...].astype(F32))
    total = None
    for n, w in enumerate((wq, wk, wv)):
        lo = n * HEAD_DIM
        d = jnp.concatenate(
            [dqkv[:, k, lo : lo + HEAD_DIM, :].reshape(512, 128) for k in range(2)], 1
        )
        part = mm(w[...], d)
        total = part if total is None else total + part
    gtok[...] = dres[...] + norm_back(total.T, gain[...], xhat, rstd)


def proj_back_call(tok, dres, dqkv, wq, wk, wv, gain):
    rows, width = tok.shape
    return pl.pallas_call(
        proj_back_kernel,
        out_shape=jax.ShapeDtypeStruct((rows, width), F32),
        compiler_params=pltpu.CompilerParams(vmem_limit_bytes=VMEM_LIMIT),
        name="projection_backward",
    )(tok, dres, dqkv, wq, wk, wv, gain)


def unpack_kernel(core, mine, other, gwq, gwk, gwv, vecs):
    first = core[0] == 0
    even = jnp.where(first, mine[...], other[...])
    odd = jnp.where(first, other[...], mine[...])
    for n, g in enumerate((gwq, gwk, gwv)):
        lo = n * HEAD_DIM
        rows = []
        for i in range(HEADS // 2):
            rows += [even[i, lo : lo + HEAD_DIM], odd[i, lo : lo + HEAD_DIM]]
        g[...] = jnp.concatenate(rows, 0).astype(F32).T
    total = even[0, PARTS:128].astype(F32) + odd[0, PARTS:128].astype(F32)
    for i in range(1, HEADS // 2):
        total += even[i, PARTS:128].astype(F32) + odd[i, PARTS:128].astype(F32)
    vecs[...] = total[:8]


def unpack_call(core, mine, other):
    width = mine.shape[-1]
    square = jax.ShapeDtypeStruct((width, width), F32)
    return pl.pallas_call(
        unpack_kernel,
        out_shape=(square, square, square, jax.ShapeDtypeStruct((8, width), F32)),
        in_specs=[SMEM, VM, VM],
        out_specs=(VM, VM, VM, VM),
        compiler_params=pltpu.CompilerParams(vmem_limit_bytes=VMEM_LIMIT),
        name="unpack_projections",
    )(core, mine, other)


def angles():
    inverse = np.float32(10000.0) ** (-np.arange(HALF, dtype=np.float32) * np.float32(2.0 / HEAD_DIM))
    turn = inverse[:, None] * np.arange(LENGTH, dtype=np.float32)[None, :]
    turn = turn.astype(np.float64)
    return np.cos(turn).astype(np.float32), np.sin(turn).astype(np.float32)


SEQ = ("x", "zh", "c")
WIN = ("y", "zl")
CHIPS = ("x", "zh")


def exchange(x, axes):
    return lax.all_to_all(x, axes, 0, 0, tiled=True)


def spread(x, axes, n):
    return exchange(jnp.broadcast_to(x[None], (n,) + x.shape), axes)


def local(
    tokens, lengths, gain_one, bias_one, weight_query, weight_key, weight_value, weight_out,
    gain_two, bias_two, weight_gate, weight_up, weight_down, cotangent,
):
    win_count, seq_rows, width = tokens.shape
    rows = win_count * seq_rows
    tok = tokens.reshape(rows, width)
    cot = cotangent.reshape(rows, width)
    g1, b1, g2, b2 = (v.reshape(1, width) for v in (gain_one, bias_one, gain_two, bias_two))
    cos, sin = angles()
    head = lax.axis_index(SEQ)
    core = lax.axis_index("c").reshape(1)
    columns = jnp.concatenate(
        [
            lax.dynamic_slice_in_dim(w, head * HEAD_DIM, HEAD_DIM, 1)
            for w in (weight_query, weight_key, weight_value)
        ],
        1,
    ).T

    sent, normed = qkv_call(
        head.reshape(1), tok, g1, b1, weight_query, weight_key, weight_value, cos, sin
    )
    qkv = exchange(sent, SEQ)
    normed = lax.all_gather(normed, SEQ, axis=0)
    mixed_low, mixed, total = attend_call(lengths, qkv)
    ob = exchange(mixed_low, SEQ)
    output, gwg, gwu, gwd, gwout, vecs, dres, dot_out = ff_call(
        tok, ob, weight_out, g2, b2, weight_gate, weight_up, weight_down, cot
    )
    gwg, gwu, gwd, gwout = lax.psum((gwg, gwu, gwd, gwout), SEQ + WIN)
    do = exchange(dot_out, SEQ)
    dqkv, grads = attend_back_call(
        lengths, qkv, do, mixed, total, cos, sin, normed, columns, g1, b1, vecs
    )
    dqkv = exchange(dqkv, SEQ)
    gtok = proj_back_call(tok, dres, dqkv, weight_query, weight_key, weight_value, g1)
    parts = exchange(grads.reshape(8, 16, width), WIN)
    part = jnp.sum(parts.astype(F32), 0).astype(BF)
    grads = spread(part, WIN, 8).reshape(128, width)
    mine = spread(grads, CHIPS, 8)
    other = lax.ppermute(mine, "c", [(0, 1), (1, 0)])
    gwq, gwk, gwv, vecs = unpack_call(core, mine, other)
    return (
        output.reshape(tokens.shape),
        gtok.reshape(tokens.shape),
        vecs[0],
        vecs[1],
        gwq,
        gwk,
        gwv,
        gwout,
        vecs[2],
        vecs[3],
        gwg,
        gwu,
        gwd,
    )


def solution(mesh):
    fine = Mesh(mesh.devices.reshape(4, 2, 2, 4, 2), SEQ + WIN)
    sharded = P(WIN, SEQ, None)
    return jax.shard_map(
        local,
        mesh=fine,
        in_specs=(sharded, P(WIN)) + (P(),) * 11 + (sharded,),
        out_specs=(sharded, sharded) + (P(),) * 11,
        check_vma=False,
    )
```

time: 652 us -> 281 us (0.43)
  matrix products: 179 us -> 0 us
  waiting for transfers between devices: 222 us -> 67.9 us
  local copies, waits for them, and re-layouts: 110 us -> 18.4 us
  Pallas kernels: 0 us -> 72.6 us
  other arithmetic: 28.8 us -> 0.67 us
  blocking collectives: 87.4 us -> 97.2 us
  starting transfers between devices: 0.29 us -> 7.68 us
    dot_general x49 -> x0, matrix products: 179 us -> none  [the longest x4 41 us: fold_advance(): jnp.einsum('wqhk,wqhd->wkhd', grad_scores, query_block, preferred_element...]
    all_to_all x0 -> x6, blocking collectives: none -> 97.2 us  [exchange(): return lax.all_to_all(x, axes, 0, 0, tiled=True)]
    psum x1, waiting for transfers between devices: 148 us -> 61.8 us  [local(): gwg, gwu, gwd, gwout = lax.psum((gwg, gwu, gwd, gwout), SEQ + WIN)]
    all_gather x2 -> x1, waiting for transfers between devices: 73.8 us -> 0.01 us  [local(): normed = lax.all_gather(normed, SEQ, axis=0)]
    pallas_call x0 -> x6, Pallas kernels: none -> 72.6 us  [the longest x1 28.3 us: attend_back_call(): pl.pallas_call(attend_back_kernel, out_shape=(jax.ShapeDtypeStruct((HEADS...]
    psum x1 -> x0, blocking collectives: 65.1 us -> none  [local(): lax.psum((grad_query, grad_key, grad_value, grad_out, grad_gain_one, grad...]
    dynamic_slice x32 -> x2, local copies, waits for them, and re-layouts: 46.8 us -> 2.12 us  [local(): lax.dynamic_slice_in_dim(w, head * HEAD_DIM, HEAD_DIM, 1)]
    all_gather x1 -> x0, blocking collectives: 22.4 us -> none  [in_one_piece(): out = lax.all_gather(both, axis, axis=dim, tiled=True)]
  transfers between devices with their start and end apart: 3 -> 4, of which waited for: 2 -> 2; matrix products, arithmetic and copies ran while one was open for 13% -> 2% of each run, Pallas kernels for 0% -> 25%
where the time goes in v1:
time: 281 us; the launch traced here: 280 us
  blocking collectives  97.2 us (35%)
  Pallas kernels  72.6 us (26%)
  waiting for transfers between devices  67.9 us (24%)
  local copies, waits for them, and re-layouts  18.4 us (7%)
  between operations  15.6 us (6%)
  starting transfers between devices  7.68 us (3%)
    all_to_all x6, blocking collectives, exchange(): return lax.all_to_all(x, axes, 0, 0, tiled=True)  97.2 us
    psum x1, waiting for transfers between devices, local(): gwg, gwu, gwd, gwout = lax.psum((gwg, gwu, gwd, gwout), SEQ + WIN)  61.8 us
    pallas_call x1, Pallas kernels, attend_back_call(): pl.pallas_call(attend_back_kernel, out_shape=(jax.ShapeDtypeStruct((HEADS...  28.3 us
    pallas_call x1, Pallas kernels, attend_call(): pl.pallas_call(attend_kernel, out_shape=(jax.ShapeDtypeStruct((HEADS, 2,...  21.2 us
    unnamed x19, local copies, waits for them, and re-layouts  14.7 us
    pallas_call x1, Pallas kernels, ff_call(): pl.pallas_call(ff_kernel, grid=(ff // FC,), in_specs=[whole(rows, width),...  13 us
    all_to_all x1, waiting for transfers between devices, exchange(): return lax.all_to_all(x, axes, 0, 0, tiled=True)  6.06 us
  transfers between devices with their start and end apart: 4, of which 2 were waited for; matrix products, arithmetic and copies ran while one was open for 2% of the time, Pallas kernels for 25%

profile of v1, /device:TPU:1, one launch (start us, length us, event | category | flops | bytes accessed | tf_op | source)
XLA Modules:
  0.0 280.0 jit_solution(13969350966617182637)
XLA Ops:
  8.0 0.0 all-gather.3.cloned.1.call-start
  8.1 3.2 %qkv_forward.1 = (bf16[16,2,96,128]{3,2,1,0:T(8,128)(2,1)}, bf16[256,512]{1,0:T(8,128)(2,1)}) custom-call(s32[1]{0:T(128)} %bitcast.1.place, bf16[256,512]{1,0:T(8,128)(2,1)} %bitcast.20, f32[1,512]{1,0:T(1,128)} %bitcast.27, f32[1,512]{1,0:T(1,128)} %bitcast.30, bf16[512,512]{1,0:T(8,128)(2,1)} %wq.3, bf16[512,512]{1,0:T(8,128)(2,1)} %wk.3, ...), custom_call_target="tpu_custom_call" | custom-call | tf_op jit(solution)/shard_map/qkv_forward/pallas_call | solution.py:81
  11.3 0.0 all-gather.3.cloned.1.call-update
  11.3 0.0 all-reduce.3.cloned.1.call-start
  11.4 25.9 %all_to_all.35.qkv = bf16[16,2,96,128]{3,2,1,0:T(8,128)(2,1)} all-to-all(bf16[16,2,96,128]{3,2,1,0:T(8,128)(2,1)} %get-tuple-element.32), channel_id=1, replica_groups=mesh['x'=4,'zh'=2,'c'=2,'y'=4,'zl'=2] {'x','zh','c'}, dimensions={0} | all-to-all | bytes 1572864 | tf_op jit(solution)/shard_map/all_to_all | solution.py:468
  37.2 21.2 %attend_forward.1 = (bf16[16,2,32,128]{3,2,1,0:T(8,128)(2,1)}, f32[2,32,2048]{2,1,0:T(8,128)}, f32[2,1,2048]{2,1,0:T(1,128)}) custom-call(s32[2]{0:T(128)} %lengths.3, bf16[16,2,96,128]{3,2,1,0:T(8,128)(2,1)} %all_to_all.35.qkv), custom_call_target="tpu_custom_call" | custom-call | tf_op jit(solution)/shard_map/attend_forward/pallas_call | solution.py:164
  58.5 15.2 %all_to_all.36.ob = bf16[16,2,32,128]{3,2,1,0:T(8,128)(2,1)} all-to-all(bf16[16,2,32,128]{3,2,1,0:T(8,128)(2,1)} %get-tuple-element.33), channel_id=1, replica_groups=mesh['x'=4,'zh'=2,'c'=2,'y'=4,'zl'=2] {'x','zh','c'}, dimensions={0} | all-to-all | bytes 524288 | tf_op jit(solution)/shard_map/all_to_all | solution.py:468
  73.6 13.0 %feed_forward.1 = (f32[256,512]{1,0:T(8,128)}, f32[512,2048]{1,0:T(8,128)}, f32[512,2048]{1,0:T(8,128)}, f32[2048,512]{1,0:T(8,128)}, f32[512,512]{1,0:T(8,128)}...) custom-call(bf16[256,512]{1,0:T(8,128)(2,1)} %bitcast.21, ...), custom_call_target="tpu_custom_call" | custom-call | tf_op jit(solution)/shard_map/feed_forward/pallas_call | solution.py:357
  86.6 0.0 all-reduce.3.cloned.1.call-update
  86.7 3.9 %all-to-all-start.2 = ((bf16[16,2,32,128]{3,2,1,0:T(8,128)(2,1)}), bf16[16,2,32,128]{3,2,1,0:T(8,128)(2,1)S(1)}, u32[]{:S(2)}, u32[]{:S(2)}) async-start(bf16[16,2,32,128]{3,2,1,0:T(8,128)(2,1)} %get-tuple-element.36), calls=%async_computation.2 | async-start | bytes 524288 | tf_op jit(solution)/shard_map/all_to_all | solution.py:468
  90.5 1.1 constant_dynamic-slice_fusion
  91.6 0.1 copy.33
  91.7 0.1 copy.34
  91.8 1.0 constant_dynamic-slice_fusion.2
  92.8 0.1 copy.32
  92.9 0.6 maximum_bitcast_fusion.wt
  93.6 6.1 %all-to-all-done.2.dot_in = bf16[16,2,32,128]{3,2,1,0:T(8,128)(2,1)S(1)} async-done(((bf16[16,2,32,128]{3,2,1,0:T(8,128)(2,1)}), bf16[16,2,32,128]{3,2,1,0:T(8,128)(2,1)S(1)}, u32[]{:S(2)}, u32[]{:S(2)}) %all-to-all-start.2) | async-done | bytes 262176 | tf_op jit(solution)/shard_map/all_to_all | solution.py:468
  99.6 0.0 copy-start.4
  99.6 0.0 all-gather.3.cloned.1.call-done
  99.6 0.7 copy-done.4
  100.3 28.3 %attend_backward.1 = (bf16[16,2,96,128]{3,2,1,0:T(8,128)(2,1)}, bf16[128,512]{1,0:T(8,128)(2,1)}) custom-call(s32[2]{0:T(128)} %lengths.3, bf16[16,2,96,128]{3,2,1,0:T(8,128)(2,1)} %all_to_all.35.qkv, bf16[16,2,32,128]{3,2,1,0:T(8,128)(2,1)} %copy-done.4, f32[2,32,2048]{2,1,0:T(8,128)} %get-tuple-element.37.mixed, f32[2,1,2048]{2,1,0:T(1,128)} %get-tuple-element.38.total, ...), custom_call_target="tpu_custom_call" | custom-call | tf_op jit(solution)/shard_map/attend_backward/pallas_call | solution.py:278
  128.6 0.0 copy-start.5
  128.6 10.9 %all_to_all.37 = bf16[8,16,512]{2,1,0:T(8,128)(2,1)S(1)} all-to-all(bf16[8,16,512]{2,1,0:T(8,128)(2,1)} %bitcast.26), channel_id=1, replica_groups=mesh['x'=4,'zh'=2,'c'=2,'y'=4,'zl'=2] {'y','zl'}, dimensions={0} | all-to-all | bytes 262144 | tf_op jit(solution)/shard_map/all_to_all | solution.py:468
  139.6 8.0 %all_to_all.38 = bf16[8,16,512]{2,1,0:T(8,128)(2,1)S(1)} all-to-all(bf16[8,16,512]{2,1,0:T(8,128)(2,1)S(1)} %broadcast_in_dim.6), channel_id=1, replica_groups=mesh['x'=4,'zh'=2,'c'=2,'y'=4,'zl'=2] {'y','zl'}, dimensions={0} | all-to-all | bytes 262144 | tf_op jit(solution)/shard_map/all_to_all | solution.py:468
  147.5 0.1 broadcast_in_dim.15
  147.6 19.6 %all_to_all.39.mine = bf16[8,128,512]{2,1,0:T(8,128)(2,1)S(1)} all-to-all(bf16[8,128,512]{2,1,0:T(8,128)(2,1)S(1)} %broadcast_in_dim.15), channel_id=1, replica_groups=mesh['x'=4,'zh'=2,'c'=2,'y'=4,'zl'=2] {'x','zh'}, dimensions={0} | all-to-all | bytes 2097152 | tf_op jit(solution)/shard_map/all_to_all | solution.py:468
  167.2 0.0 copy-start
  167.2 3.7 %collective-permute-start = (bf16[8,128,512]{2,1,0:T(8,128)(2,1)S(1)}, bf16[8,128,512]{2,1,0:T(8,128)(2,1)S(1)}, u32[]{:S(2)}, u32[]{:S(2)}) collective-permute-start(bf16[8,128,512]{2,1,0:T(8,128)(2,1)S(1)} %all_to_all.39.mine), channel_id=1, source_target_pairs={{0,8},{8,0},{1,9},{9,1},{2,10},{10,2},{3,11},{11,3},{4,12},{12,4},... | collective-permute-start | bytes 3145736 | tf_op jit(solution)/shard_map/ppermute | solution.py:516
  170.9 0.0 copy-done.5
  170.9 17.7 %all_to_all.40.dqkv = bf16[16,2,96,128]{3,2,1,0:T(8,128)(2,1)} all-to-all(bf16[16,2,96,128]{3,2,1,0:T(8,128)(2,1)S(1)} %copy-done.5), channel_id=1, replica_groups=mesh['x'=4,'zh'=2,'c'=2,'y'=4,'zl'=2] {'x','zh','c'}, dimensions={0} | all-to-all | bytes 1572864 | tf_op jit(solution)/shard_map/all_to_all | solution.py:468
  188.6 3.4 %projection_backward.1 = f32[256,512]{1,0:T(8,128)} custom-call(bf16[256,512]{1,0:T(8,128)(2,1)} %bitcast.22, f32[256,512]{1,0:T(8,128)} %get-tuple-element.35.dres, bf16[16,2,96,128]{3,2,1,0:T(8,128)(2,1)} %all_to_all.40.dqkv, bf16[512,512]{1,0:T(8,128)(2,1)} %wq.3, bf16[512,512]{1,0:T(8,128)(2,1)} %wk.3, bf16[512,512]{1,0:T(8,128)(2,1)} %wv.3, ...), custom_call_target="tpu_custom_call" | custom-call | tf_op jit(solution)/shard_map/projection_backward/pallas_call | solution.py:418
  192.1 0.0 collective-permute-done.other
  192.1 0.0 copy-start.3
  192.1 0.0 copy-done
  192.1 1.0 copy-done.3
  193.1 3.4 %unpack_projections.1 = (f32[512,512]{1,0:T(8,128)}, f32[512,512]{1,0:T(8,128)}, f32[512,512]{1,0:T(8,128)}, f32[8,512]{1,0:T(8,128)}) custom-call(s32[1]{0:T(128)} %bitcast.11.core, bf16[8,128,512]{2,1,0:T(8,128)(2,1)} %copy-done, bf16[8,128,512]{2,1,0:T(8,128)(2,1)} %copy-done.3), custom_call_target="tpu_custom_call" | custom-call | tf_op jit(solution)/shard_map/unpack_projections/pallas_call | solution.py:445
  196.5 1.5 fusion
  198.0 61.8 %all-reduce.3.cloned.1.call-done = (f32[512,512]{1,0:T(8,128)}, f32[512,2048]{1,0:T(8,128)}, f32[512,2048]{1,0:T(8,128)}, f32[2048,512]{1,0:T(8,128)}) async-done(((f32[512,512]{1,0:T(8,128)}, f32[512,2048]{1,0:T(8,128)}, f32[512,2048]{1,0:T(8,128)}, f32[2048,512]{1,0:T(8,128)}), (f32[512,512]{1,0:T(8,128)}, f32[512,2048]{1,0:T(8,128)}, f32[512,2048]{1,0:T(8,128)}, ...) | async-done | bytes 13631504 | tf_op jit(solution)/shard_map/psum | solution.py:505
  259.7 2.3 copy.39
  262.0 0.0 copy-start.2
  262.0 4.8 %copy.40 = f32[512,2048]{1,0:T(8,128)} copy(f32[512,2048]{1,0:T(8,128)} %get-tuple-element.71) | data formatting | bytes 8388608
  266.8 0.0 copy-done.2
  266.8 0.0 copy-start.1
  266.8 2.1 copy.41
  269.0 1.6 copy-done.1
  270.5 2.0 copy.42
  (2 shorter events, 0.0 us)
Async XLA Ops:
  8.0 91.6 %all-gather.3.cloned.1.call-start = ((), (), s32[]{:S(2)}) async-start(), calls=%async_computation.7 | async-start | bytes 4456448 | tf_op jit(solution)/shard_map/all_gather | solution.py:499
  11.3 248.4 %all-reduce.3.cloned.1.call-start = ((), (), s32[]{:S(2)}) async-start(), calls=%async_computation.8 | async-start | bytes 27262976 | tf_op jit(solution)/shard_map/psum | solution.py:505
  86.7 13.0 %all-to-all-start.2 = ((bf16[16,2,32,128]{3,2,1,0:T(8,128)(2,1)}), bf16[16,2,32,128]{3,2,1,0:T(8,128)(2,1)S(1)}, u32[]{:S(2)}, u32[]{:S(2)}) async-start(bf16[16,2,32,128]{3,2,1,0:T(8,128)(2,1)} %get-tuple-element.36), calls=%async_computation.2 | async-start | bytes 524288 | tf_op jit(solution)/shard_map/all_to_all | solution.py:468
  99.6 0.7 copy-start.4
  128.6 42.3 %copy-start.5 = (bf16[16,2,96,128]{3,2,1,0:T(8,128)(2,1)S(1)}, bf16[16,2,96,128]{3,2,1,0:T(8,128)(2,1)}, u32[]{:S(2)}) copy-start(bf16[16,2,96,128]{3,2,1,0:T(8,128)(2,1)} %get-tuple-element.41) | copy-start | bytes 2359300
  167.2 24.9 %copy-start = (bf16[8,128,512]{2,1,0:T(8,128)(2,1)}, bf16[8,128,512]{2,1,0:T(8,128)(2,1)S(1)}, u32[]{:S(2)}) copy-start(bf16[8,128,512]{2,1,0:T(8,128)(2,1)S(1)} %all_to_all.39.mine) | copy-start | bytes 3145732
  167.2 24.9 %collective-permute-start = (bf16[8,128,512]{2,1,0:T(8,128)(2,1)S(1)}, bf16[8,128,512]{2,1,0:T(8,128)(2,1)S(1)}, u32[]{:S(2)}, u32[]{:S(2)}) collective-permute-start(bf16[8,128,512]{2,1,0:T(8,128)(2,1)S(1)} %all_to_all.39.mine), channel_id=1, source_target_pairs={{0,8},{8,0},{1,9},{9,1},{2,10},{10,2},{3,11},{11,3},{4,12},{12,4},... | collective-permute-start | bytes 3145736 | tf_op jit(solution)/shard_map/ppermute | solution.py:516
  192.1 1.0 copy-start.3
  262.0 4.9 %copy-start.2 = (f32[512,2048]{1,0:T(8,128)S(1)}, f32[512,2048]{1,0:T(8,128)}, u32[]{:S(2)}) copy-start(f32[512,2048]{1,0:T(8,128)} %get-tuple-element.72) | copy-start | bytes 12582916
  266.8 3.7 %copy-start.1 = (f32[2048,512]{1,0:T(8,128)S(1)}, f32[2048,512]{1,0:T(8,128)}, u32[]{:S(2)}) copy-start(f32[2048,512]{1,0:T(8,128)} %get-tuple-element.73) | copy-start | bytes 12582916
Sparse Core Ops, SparseCore 0:
  11.8 63.2 all-gather.2
Sparse Core Ops, SparseCore 1:
  86.8 172.9 all-reduce.2

commit v2 on v1

v2 whole, which is shorter than its diff:
```python
import functools
import math

import jax
import jax.numpy as jnp
import numpy as np
from jax import lax
from jax.experimental import pallas as pl
from jax.experimental.pallas import tpu as pltpu
from jax.sharding import Mesh
from jax.sharding import PartitionSpec as P

HEADS = 16
HEAD_DIM = 32
HALF = HEAD_DIM // 2
PARTS = 3 * HEAD_DIM
LENGTH = 2048
epsilon = 1e-05
masked_score = -1e30
BF = jnp.bfloat16
F32 = jnp.float32
inv_root = HEAD_DIM ** (-0.5)
score_scale = inv_root * math.log2(math.e)
VMEM_LIMIT = 60 * 1024 * 1024


def cost(flops, nbytes=1 << 20):
    return pl.CostEstimate(flops=flops, bytes_accessed=nbytes, transcendentals=0)


def mm(a, b):
    return jnp.dot(a, b, preferred_element_type=F32)


def mm_nt(a, b):
    return lax.dot_general(a, b, (((1,), (1,)), ((), ())), preferred_element_type=F32)


def mm_tn(a, b):
    return lax.dot_general(a, b, (((0,), (0,)), ((), ())), preferred_element_type=F32)


def normalize(x):
    center = x - jnp.mean(x, -1, keepdims=True)
    rstd = lax.rsqrt(jnp.mean(center * center, -1, keepdims=True) + epsilon)
    return center * rstd, rstd


def norm_back(dh, gain, xhat, rstd):
    dxhat = dh * gain
    a = jnp.mean(dxhat, -1, keepdims=True)
    b = jnp.mean(dxhat * xhat, -1, keepdims=True)
    return rstd * (dxhat - a - xhat * b)


def rotate(block, cosine, sine):
    a, b = block[:HALF], block[HALF:]
    return jnp.concatenate([a * cosine - b * sine, b * cosine + a * sine], 0)


def head_of(number):
    return number // 8


def core_of(number):
    return number // 8 % 2


def y_of(number):
    return number // 2 % 4


def qkv_kernel(place, tok, gain, bias, wq, wk, wv, cosine, sine, out):
    xhat, _ = normalize(tok[...].astype(F32))
    h1 = (xhat * gain[...] + bias[...]).astype(BF)
    cos = jnp.concatenate([cosine[...]] * 2, 1)
    sin = jnp.concatenate([sine[...]] * 2, 1)
    for n, w in enumerate((wq, wk, wv)):
        t = mm(h1, w[...]).T
        for h in range(HEADS):
            block = t[h * HEAD_DIM : (h + 1) * HEAD_DIM]
            if n < 2:
                block = rotate(block, cos, sin)
            block = block.astype(BF)
            for k in range(2):
                out[h, k, n * HEAD_DIM : (n + 1) * HEAD_DIM, :] = block[:, k * 128 : (k + 1) * 128]


def whole(*shape):
    return pl.BlockSpec(shape, lambda *_: (0,) * len(shape))


def qkv_call(place, tok, gain, bias, wq, wk, wv, cos, sin):
    rows, width = tok.shape
    table = pl.BlockSpec((HALF, 128), lambda i, p: (0, head_of(p[0])))
    return pl.pallas_call(
        qkv_kernel,
        grid_spec=pltpu.PrefetchScalarGridSpec(
            num_scalar_prefetch=1,
            grid=(1,),
            in_specs=[whole(rows, width)]
            + [whole(1, width)] * 2
            + [whole(width, width)] * 3
            + [table, table],
            out_specs=whole(HEADS, 2, PARTS, 128),
        ),
        out_shape=jax.ShapeDtypeStruct((HEADS, 2, PARTS, 128), BF),
        cost_estimate=cost(2 * rows * width * width * 3),
        compiler_params=pltpu.CompilerParams(vmem_limit_bytes=VMEM_LIMIT),
        name="qkv_forward",
    )(place, tok, gain, bias, wq, wk, wv, cos, sin)


def gather_rows(ref, w, lo, n):
    return jnp.concatenate([ref[s, w, lo : lo + n, :] for s in range(HEADS)], axis=1)


def split2(x):
    hi = x.astype(BF)
    return hi, (x - hi.astype(F32)).astype(BF)


def split3(x):
    hi = x.astype(BF)
    rest = x - hi.astype(F32)
    mid = rest.astype(BF)
    return hi, mid, (rest - mid.astype(F32)).astype(BF)


def key_rows(kt, length):
    place = lax.broadcasted_iota(jnp.int32, (16, LENGTH), 1)
    row = lax.broadcasted_iota(jnp.int32, (16, LENGTH), 0)
    mask = jnp.where(place < length, 0.0, masked_score)
    extra = jnp.where(row == 0, mask, jnp.where(row < 4, 1.0, 0.0)).astype(BF)
    zeros = jnp.zeros((48, LENGTH), BF)
    return jnp.concatenate([kt, kt, extra, zeros], 0).T


TQ = 1024
TB = 512


def attend_kernel(lengths, qkv, out, mixed, total, kaug, qaug, vaug):
    for w in range(2):
        kt = gather_rows(qkv, w, 32, 32)
        kaug[...] = key_rows(kt, lengths[w])
        qs = gather_rows(qkv, w, 0, 32).astype(F32) * score_scale
        hi, lo = split2(qs)
        row = lax.broadcasted_iota(jnp.int32, (64, LENGTH), 0)
        qaug[...] = jnp.concatenate([hi, lo, jnp.where(row == 0, 1.0, 0.0).astype(BF)], 0)
        row = lax.broadcasted_iota(jnp.int32, (16, LENGTH), 0)
        vaug[...] = jnp.concatenate(
            [gather_rows(qkv, w, 64, 32), jnp.where(row == 0, 1.0, 0.0).astype(BF)], 0
        )

        def tile(t, carry):
            cols = pl.ds(pl.multiple_of(t * TQ, TQ), TQ)
            st = mm(kaug[...], qaug[:, cols])
            peak = jnp.max(st, 0, keepdims=True)
            p = jnp.exp2(st - peak).astype(BF)
            o = mm(vaug[...], p)
            norm = o[32:33]
            ot = o[:32] / norm
            mixed[w, :, cols] = ot
            total[w, :, cols] = peak + jnp.log2(norm)
            for j in range(TQ // 128):
                out[t * (TQ // 128) + j, w] = ot[:, j * 128 : (j + 1) * 128].astype(BF)
            return carry

        lax.fori_loop(0, LENGTH // TQ, tile, 0)


SMEM = pl.BlockSpec(memory_space=pltpu.SMEM)
VM = pl.BlockSpec(memory_space=pltpu.VMEM)


def attend_call(lengths, qkv):
    return pl.pallas_call(
        attend_kernel,
        out_shape=(
            jax.ShapeDtypeStruct((HEADS, 2, HEAD_DIM, 128), BF),
            jax.ShapeDtypeStruct((2, HEAD_DIM, LENGTH), F32),
            jax.ShapeDtypeStruct((2, 1, LENGTH), F32),
        ),
        in_specs=[SMEM, VM],
        out_specs=(VM, VM, VM),
        scratch_shapes=[
            pltpu.VMEM((LENGTH, 128), BF),
            pltpu.VMEM((128, LENGTH), BF),
            pltpu.VMEM((48, LENGTH), BF),
        ],
        cost_estimate=cost(1 << 34),
        compiler_params=pltpu.CompilerParams(vmem_limit_bytes=VMEM_LIMIT),
        name="attend_forward",
    )(lengths, qkv)


def attend_back_kernel(
    lengths, qkv, dot_in, mixed, total, cosine, sine, out, kaug, qaug, vaug, doaug, right, dkv
):
    for w in range(2):
        kt = gather_rows(qkv, w, 32, 32)
        kaug[...] = key_rows(kt, lengths[w])
        qt = gather_rows(qkv, w, 0, 32)
        hi, lo = split2(qt.astype(F32) * score_scale)
        row = lax.broadcasted_iota(jnp.int32, (16, LENGTH), 0)

        def rows_of(first, second, third, fourth):
            return jnp.where(
                row == 0,
                first,
                jnp.where(
                    row == 1, second, jnp.where(row == 2, third, jnp.where(row == 3, fourth, 0.0))
                ),
            ).astype(BF)

        l1, l2, l3 = (v.astype(F32) for v in split3(-total[w]))
        qaug[...] = jnp.concatenate(
            [hi, lo, rows_of(1.0, l1, l2, l3), jnp.zeros((48, LENGTH), BF)], 0
        )
        do = gather_rows(dot_in, w, 0, 32)
        delta = jnp.sum(do.astype(F32) * mixed[w], 0, keepdims=True)
        d1, d2, d3 = (v.astype(F32) for v in split3(-delta))
        doaug[...] = jnp.concatenate(
            [do, rows_of(d1, d2, d3, 0.0), jnp.zeros((80, LENGTH), BF)], 0
        )
        vaug[...] = jnp.concatenate(
            [
                gather_rows(qkv, w, 64, 32),
                jnp.where(row < 3, 1.0, 0.0).astype(BF),
                jnp.zeros((80, LENGTH), BF),
            ],
            0,
        ).T
        right[...] = jnp.concatenate([qt, do, jnp.zeros((64, LENGTH), BF)], 0).T
        dkv[...] = jnp.zeros_like(dkv)
        lane = lax.broadcasted_iota(jnp.int32, (TB, 128), 1)

        def tile(t, carry):
            cols = pl.ds(pl.multiple_of(t * TB, TB), TB)
            st = mm(kaug[...], qaug[:, cols])
            probs = jnp.exp2(st)
            ds = (probs * mm(vaug[...], doaug[:, cols])).astype(BF)
            both = jnp.concatenate([ds, probs.astype(BF)], 1)
            r = right[cols, :]
            zero = jnp.zeros_like(r)
            pair = jnp.concatenate(
                [jnp.where(lane < 32, r, zero), jnp.where(lane < 32, zero, r)], 0
            )
            dkv[...] += mm(both, pair)
            dq = mm(kt, ds) * inv_root
            dq = rotate(dq, cosine[:, cols], -sine[:, cols])
            dq = dq.astype(BF)
            for j in range(TB // 128):
                out[t * (TB // 128) + j, w, 0:32, :] = dq[:, j * 128 : (j + 1) * 128]
            return carry

        lax.fori_loop(0, LENGTH // TB, tile, 0)
        back = dkv[...].T
        dk = rotate(back[:32] * inv_root, cosine[...], -sine[...]).astype(BF)
        dv = back[32:64].astype(BF)
        for s in range(HEADS):
            out[s, w, 32:64, :] = dk[:, s * 128 : (s + 1) * 128]
            out[s, w, 64:96, :] = dv[:, s * 128 : (s + 1) * 128]


def attend_back_call(lengths, qkv, do, mixed, total, cos, sin):
    return pl.pallas_call(
        attend_back_kernel,
        out_shape=jax.ShapeDtypeStruct((HEADS, 2, PARTS, 128), BF),
        in_specs=[SMEM] + [VM] * 6,
        out_specs=VM,
        scratch_shapes=[
            pltpu.VMEM((LENGTH, 128), BF),
            pltpu.VMEM((128, LENGTH), BF),
            pltpu.VMEM((LENGTH, 128), BF),
            pltpu.VMEM((128, LENGTH), BF),
            pltpu.VMEM((LENGTH, 128), BF),
            pltpu.VMEM((LENGTH, 128), F32),
        ],
        cost_estimate=cost(1 << 34),
        compiler_params=pltpu.CompilerParams(vmem_limit_bytes=VMEM_LIMIT),
        name="attend_backward",
    )(lengths, qkv, do, mixed, total, cos, sin)


def ordered(ref, core, y):
    rows = []
    for o in range(2):
        for d in range(4):
            start = (core + o) % 2 * 256 + (y + d) % 4 * 64
            rows.append(ref[pl.ds(pl.multiple_of(start, 64), 64), :])
    return jnp.concatenate(rows, 0)


def pack(refs, index, value):
    for o in range(2):
        for d in range(4):
            for j in range(4):
                for l in range(4):
                    lo = o * 256 + d * 64 + j * 16
                    refs[o * 4 + d][(4 * j + l,) + index] = value[
                        lo : lo + 16, l * 128 : (l + 1) * 128
                    ].astype(BF)


def unpack(ref, index, out, where):
    for j in range(4):
        for l in range(4):
            out[where + (slice(j * 16, j * 16 + 16), slice(l * 128, l * 128 + 128))] = ref[
                (4 * j + l,) + index
            ].astype(F32)


FC = 512


def ff_kernel(
    place, tok, ob, wout, gain, bias, wg, wu, wd, cot,
    output, k0, k1, k2, k3, s0, s1, s2, s3, gwout, vecs, dres, dot_out,
    res, h2, h2t, dh2, obt, mt,
):
    pieces = (k0, k1, k2, k3, s0, s1, s2, s3)
    core, y = core_of(place[0]), y_of(place[0])
    step = pl.program_id(0)
    last = pl.num_programs(0) - 1

    @pl.when(step == 0)
    def first():
        for k in range(2):
            obt[:, k * 128 : (k + 1) * 128] = ob[:, k].reshape(512, 128)
        r = tok[...].astype(F32) + mm(obt[...].T, wout[...])
        xhat, _ = normalize(r)
        h = (xhat * gain[...] + bias[...]).astype(BF)
        res[...] = r
        h2[...] = h
        mt[...] = h.T
        h2t[...] = ordered(mt, core, y)
        output[...] = r
        dh2[...] = jnp.zeros_like(dh2)

    gate = mm(h2[...], wg[...])
    up = mm(h2[...], wu[...])
    dm = mm_nt(cot[...], wd[...])
    sg = jax.nn.sigmoid(gate)
    act = gate * sg
    m = (act * up).astype(BF)
    dgate = (dm * up * (sg * (1.0 + gate - act))).astype(BF)
    dup = (dm * act).astype(BF)
    output[...] += mm(m, wd[...])
    mt[...] = m.T
    pack(pieces, (0, 0), mm(h2t[...], dgate))
    pack(pieces, (1, 0), mm(h2t[...], dup))
    pack(pieces, (2, 0), mm(ordered(mt, core, y), cot[...]))
    dh2[...] += mm_nt(dgate, wg[...]) + mm_nt(dup, wu[...])

    @pl.when(step == last)
    def final():
        xhat, rstd = normalize(res[...])
        dh = dh2[...]
        vecs[0:1] = jnp.sum(dh * xhat, 0, keepdims=True)
        vecs[1:2] = jnp.sum(dh, 0, keepdims=True)
        dr = cot[...].astype(F32) + norm_back(dh, gain[...], xhat, rstd)
        dres[...] = dr
        da = dr.astype(BF)
        gwout[...] = mm(ordered(obt, core, y), da)
        do = mm_nt(wout[...], da).astype(BF)
        for k in range(2):
            dot_out[:, k] = do[:, k * 128 : (k + 1) * 128].reshape(HEADS, HEAD_DIM, 128)


def ff_call(place, tok, ob, wout, gain, bias, wg, wu, wd, cot):
    rows, width = tok.shape
    ff = wg.shape[1]

    return pl.pallas_call(
        ff_kernel,
        grid_spec=pltpu.PrefetchScalarGridSpec(
            num_scalar_prefetch=1,
            grid=(ff // FC,),
            in_specs=[
                whole(rows, width),
                whole(HEADS, 2, HEAD_DIM, 128),
                whole(width, width),
                whole(1, width),
                whole(1, width),
                pl.BlockSpec((width, FC), lambda i, c: (0, i)),
                pl.BlockSpec((width, FC), lambda i, c: (0, i)),
                pl.BlockSpec((FC, width), lambda i, c: (i, 0)),
                whole(rows, width),
            ],
            out_specs=(
                whole(rows, width),
            )
            + (pl.BlockSpec((16, 3, 1, 16, 128), lambda i, c: (0, 0, i, 0, 0)),) * 8
            + (
                whole(width, width),
                whole(2, width),
                whole(rows, width),
                whole(HEADS, 2, HEAD_DIM, 128),
            ),
            scratch_shapes=[
                pltpu.VMEM((rows, width), F32),
                pltpu.VMEM((rows, width), BF),
                pltpu.VMEM((width, rows), BF),
                pltpu.VMEM((rows, width), F32),
                pltpu.VMEM((width, rows), BF),
                pltpu.VMEM((FC, rows), BF),
            ],
        ),
        out_shape=(
            jax.ShapeDtypeStruct((rows, width), F32),
        )
        + (jax.ShapeDtypeStruct((16, 3, 4, 16, 128), BF),) * 8
        + (
            jax.ShapeDtypeStruct((width, width), F32),
            jax.ShapeDtypeStruct((2, width), F32),
            jax.ShapeDtypeStruct((rows, width), F32),
            jax.ShapeDtypeStruct((HEADS, 2, HEAD_DIM, 128), BF),
        ),
        cost_estimate=cost(2 * rows * width * ff * 9),
        compiler_params=pltpu.CompilerParams(vmem_limit_bytes=VMEM_LIMIT),
        name="feed_forward",
    )(place, tok, ob, wout, gain, bias, wg, wu, wd, cot)


def proj_back_kernel(place, tok, dres, dqkv, wq, wk, wv, gain, bias, gwout, vecs, gtok, *rest):
    pieces, h1t = rest[:8], rest[8]
    xhat, rstd = normalize(tok[...].astype(F32))
    h1t[...] = (xhat * gain[...] + bias[...]).astype(BF).T
    h = ordered(h1t, core_of(place[0]), y_of(place[0]))
    total = None
    for n, w in enumerate((wq, wk, wv)):
        lo = n * HEAD_DIM
        d = jnp.concatenate(
            [dqkv[:, k, lo : lo + HEAD_DIM, :].reshape(512, 128) for k in range(2)], 1
        )
        part = mm(w[...], d)
        total = part if total is None else total + part
        pack(pieces, (n,), mm_nt(h, d))
    pack(pieces, (3,), gwout[...])
    dh = total.T
    four = jnp.concatenate(
        [jnp.sum(dh * xhat, 0, keepdims=True), jnp.sum(dh, 0, keepdims=True), vecs[...]], 0
    )
    block = jnp.concatenate([four[:, l * 128 : (l + 1) * 128] for l in range(4)], 0).astype(BF)
    for ref in pieces:
        for j in range(16):
            ref[j, 4] = block
    gtok[...] = dres[...] + norm_back(dh, gain[...], xhat, rstd)


def proj_back_call(place, tok, dres, dqkv, wq, wk, wv, gain, bias, gwout, vecs):
    rows, width = tok.shape
    piece = jax.ShapeDtypeStruct((16, 5, 16, 128), BF)
    return pl.pallas_call(
        proj_back_kernel,
        out_shape=(jax.ShapeDtypeStruct((rows, width), F32),) + (piece,) * 8,
        in_specs=[SMEM] + [VM] * 10,
        out_specs=(VM,) * 9,
        scratch_shapes=[pltpu.VMEM((width, rows), BF)],
        cost_estimate=cost(2 * rows * width * width * 6),
        compiler_params=pltpu.CompilerParams(vmem_limit_bytes=VMEM_LIMIT),
        name="projection_backward",
    )(place, tok, dres, dqkv, wq, wk, wv, gain, bias, gwout, vecs)


def put_pieces(number, core, refs, write):
    for d, ref in enumerate(refs):
        write(ref, core, pl.multiple_of((y_of(number) + 4 - d) % 4 * 64, 64))


def wide_rows(ref, n, out, start):
    for j in range(4):
        rows = pl.ds(start + j * 16, 16)
        for i in range(4):
            for l in range(4):
                lo = i * 512 + l * 128
                out[0, rows, lo : lo + 128] = ref[4 * j + l, n, i].astype(F32)


def unpack_ff_kernel(place, *refs):
    gwg, gwu, gwd = refs[-3:]
    number = place[0]

    def write(ref, core, start):
        wide_rows(ref, 0, gwg, start)
        wide_rows(ref, 1, gwu, start)
        for j in range(4):
            rows = pl.ds(start + j * 16, 16)
            for i in range(4):
                for l in range(4):
                    gwd[i, 0, rows, l * 128 : (l + 1) * 128] = ref[4 * j + l, 2, i].astype(F32)

    put_pieces(number, None, refs[:4], write)


def unpack_ff_call(place, pieces, other, before):
    def spec(block, axis):
        def index(i, p):
            at = [0] * len(block)
            at[axis] = (core_of(p[0]) + other) % 2
            return tuple(at)

        return pl.BlockSpec(block, index)

    shapes = ((2, 256, 2048), (2, 256, 2048), (4, 2, 256, 512))
    return pl.pallas_call(
        unpack_ff_kernel,
        grid_spec=pltpu.PrefetchScalarGridSpec(
            num_scalar_prefetch=1,
            grid=(1,),
            in_specs=[whole(*pieces[0].shape)] * 4
            + [pl.BlockSpec(memory_space=pl.ANY)] * len(before),
            out_specs=(
                spec((1, 256, 2048), 0),
                spec((1, 256, 2048), 0),
                spec((4, 1, 256, 512), 1),
            ),
        ),
        out_shape=tuple(jax.ShapeDtypeStruct(shape, F32) for shape in shapes),
        input_output_aliases={5 + k: k for k in range(3)} if before else {},
        cost_estimate=cost(1 << 20, 9 << 20),
        compiler_params=pltpu.CompilerParams(vmem_limit_bytes=VMEM_LIMIT),
        name="unpack_feed_forward",
    )(place, *pieces, *before)


def unpack_kernel(place, *refs):
    outs = refs[-4:]
    number = place[0]

    def write(ref, core, start):
        for n, g in enumerate(outs):
            for j in range(4):
                rows = pl.ds(pl.multiple_of(core * 256 + start + j * 16, 16), 16)
                for l in range(4):
                    g[rows, l * 128 : (l + 1) * 128] = ref[4 * j + l, n].astype(F32)

    put_pieces(number, core_of(number), refs[:4], write)
    put_pieces(number, 1 - core_of(number), refs[4:8], write)


def unpack_call(place, mine, others):
    square = jax.ShapeDtypeStruct((512, 512), F32)
    return pl.pallas_call(
        unpack_kernel,
        out_shape=(square,) * 4,
        in_specs=[SMEM] + [VM] * 8,
        out_specs=(VM,) * 4,
        cost_estimate=cost(1 << 20, 6 << 20),
        compiler_params=pltpu.CompilerParams(vmem_limit_bytes=VMEM_LIMIT),
        name="unpack_projections",
    )(place, *mine, *others)


def angles():
    inverse = np.float32(10000.0) ** (-np.arange(HALF, dtype=np.float32) * np.float32(2.0 / HEAD_DIM))
    turn = inverse[:, None] * np.arange(LENGTH, dtype=np.float32)[None, :]
    turn = turn.astype(np.float64)
    return np.cos(turn).astype(np.float32), np.sin(turn).astype(np.float32)


SEQ = ("x", "zh", "c")
WIN = ("y", "zl")
REST = ("x", "zh", "zl")
SWAP = [(0, 1), (1, 0)]


def exchange(x, axes):
    return lax.all_to_all(x, axes, 0, 0, tiled=True)


def spread(x, axes, n):
    return exchange(jnp.broadcast_to(x[None], (n,) + x.shape), axes)


def add_up(*terms):
    return sum(t.astype(F32) for t in terms).astype(BF)


def along_y(x, d):
    return lax.ppermute(x, "y", [(i, (i + d) % 4) for i in range(4)])


def reduce_y(pieces):
    got = [lax.ppermute(p, "c", SWAP) for p in pieces[4:]]
    there = [along_y(add_up(pieces[d], got[d]), d) for d in (1, 2, 3)]
    return add_up(pieces[0], got[0], *there)


def reduce_rest(x):
    return jnp.sum(exchange(x, REST).astype(F32), 0).astype(BF)


def collect(whole_piece):
    mine = [whole_piece] + [along_y(whole_piece, d) for d in (1, 2, 3)]
    return mine, [lax.ppermute(m, "c", SWAP) for m in mine]


def after(x, *others):
    return lax.optimization_barrier((x,) + others)[0]


def local(
    tokens, lengths, gain_one, bias_one, weight_query, weight_key, weight_value, weight_out,
    gain_two, bias_two, weight_gate, weight_up, weight_down, cotangent,
):
    win_count, seq_rows, width = tokens.shape
    rows = win_count * seq_rows
    tok = tokens.reshape(rows, width)
    cot = cotangent.reshape(rows, width)
    g1, b1, g2, b2 = (v.reshape(1, width) for v in (gain_one, bias_one, gain_two, bias_two))
    cos, sin = angles()
    place = lax.axis_index(SEQ + WIN).reshape(1)

    sent = qkv_call(place, tok, g1, b1, weight_query, weight_key, weight_value, cos, sin)
    qkv = exchange(sent, SEQ)
    mixed_low, mixed, total = attend_call(lengths, qkv)
    ob = exchange(mixed_low, SEQ)
    output, *pieces, gwout, vecs, dres, dot_out = ff_call(
        place, tok, ob, weight_out, g2, b2, weight_gate, weight_up, weight_down, cot
    )
    do = exchange(dot_out, SEQ)
    ff = reduce_y(pieces)
    dqkv = exchange(attend_back_call(lengths, qkv, do, mixed, total, cos, sin), SEQ)
    ff = reduce_rest(after(ff, dqkv))
    gtok, *pieces = proj_back_call(
        place, tok, dres, dqkv, weight_query, weight_key, weight_value, g1, b1, gwout, vecs
    )
    ff = spread(ff, REST, 16)
    mine, others = collect(ff)
    gwg, gwu, gwd = unpack_ff_call(place, others, 1, unpack_ff_call(place, mine, 0, ()))
    part = reduce_rest(after(reduce_y(pieces), ff))
    four = part[4].reshape(4, 4, 128).transpose(1, 0, 2).reshape(4, width).astype(F32)
    gwq, gwk, gwv, gwout = unpack_call(place, *collect(spread(part[:4], REST, 16)))
    return (
        output.reshape(tokens.shape),
        gtok.reshape(tokens.shape),
        four[0],
        four[1],
        gwq,
        gwk,
        gwv,
        gwout,
        four[2],
        four[3],
        gwg.reshape(width, 2048),
        gwu.reshape(width, 2048),
        gwd.reshape(2048, width),
    )


def solution(mesh):
    fine = Mesh(mesh.devices.reshape(4, 2, 2, 4, 2), SEQ + WIN)
    sharded = P(WIN, SEQ, None)
    return jax.shard_map(
        local,
        mesh=fine,
        in_specs=(sharded, P(WIN)) + (P(),) * 11 + (sharded,),
        out_specs=(sharded, sharded) + (P(),) * 11,
        check_vma=False,
    )
```

time: 281 us -> 237 us (0.84)
  starting transfers between devices: 7.68 us -> 65.8 us
  blocking collectives: 97.2 us -> 47.9 us
  waiting for transfers between devices: 67.9 us -> 30.7 us
  between operations: 15.6 us -> 0.92 us
  local copies, waits for them, and re-layouts: 18.4 us -> 5.35 us
  other arithmetic: 0.67 us -> 12.3 us
    psum x1 -> x0, waiting for transfers between devices: 61.8 us -> none  [local(): gwg, gwu, gwd, gwout = lax.psum((gwg, gwu, gwd, gwout), SEQ + WIN)]
    all_to_all x6 -> x3, blocking collectives: 97.2 us -> 47.9 us  [exchange(): return lax.all_to_all(x, axes, 0, 0, tiled=True)]
    ppermute x1 -> x28, starting transfers between devices: 3.74 us -> 39.4 us  [the longest x12 24.7 us: along_y(): return lax.ppermute(x, 'y', [(i, (i + d) % 4) for i in range(4)])]
    all_to_all x1 -> x5, starting transfers between devices: 3.86 us -> 26.5 us  [exchange(): return lax.all_to_all(x, axes, 0, 0, tiled=True)]
    all_to_all x1 -> x5, waiting for transfers between devices: 6.06 us -> 25.3 us  [exchange(): return lax.all_to_all(x, axes, 0, 0, tiled=True)]
    convert_element_type x0 -> x9, other arithmetic: none -> 12.1 us  [the longest x8 12.1 us: add_up(): return sum((t.astype(F32) for t in terms)).astype(BF)]
    unnamed x19 -> x40, local copies, waits for them, and re-layouts: 14.7 us -> 3.64 us
    pallas_call x4 -> x6, Pallas kernels: 48.1 us -> 56 us  [the longest x1 25.2 us: attend_back_call(): pl.pallas_call(attend_back_kernel, out_shape=jax.ShapeDtypeStruct((HEADS,...]
  transfers between devices with their start and end apart: 4 -> 33, of which waited for: 2 -> 7; matrix products, arithmetic and copies ran while one was open for 2% -> 6% of each run, Pallas kernels for 25% -> 17%
where the time goes in v2:
time: 237 us; the launch traced here: 236 us
  Pallas kernels  73.1 us (31%)
  starting transfers between devices  65.8 us (28%)
  blocking collectives  47.9 us (20%)
  waiting for transfers between devices  30.7 us (13%)
  other arithmetic  12.3 us (5%)
  local copies, waits for them, and re-layouts  5.35 us (2%)
    all_to_all x3, blocking collectives, exchange(): return lax.all_to_all(x, axes, 0, 0, tiled=True)  47.9 us
    all_to_all x5, starting transfers between devices, exchange(): return lax.all_to_all(x, axes, 0, 0, tiled=True)  26.5 us
    all_to_all x5, waiting for transfers between devices, exchange(): return lax.all_to_all(x, axes, 0, 0, tiled=True)  25.3 us
    pallas_call x1, Pallas kernels, attend_back_call(): pl.pallas_call(attend_back_kernel, out_shape=jax.ShapeDtypeStruct((HEADS,...  25.2 us
    ppermute x12, starting transfers between devices, along_y(): return lax.ppermute(x, 'y', [(i, (i + d) % 4) for i in range(4)])  24.7 us
    pallas_call x1, Pallas kernels, attend_call(): pl.pallas_call(attend_kernel, out_shape=(jax.ShapeDtypeStruct((HEADS, 2,...  13.9 us
    convert_element_type x8, other arithmetic, add_up(): return sum((t.astype(F32) for t in terms)).astype(BF)  12.1 us
    pallas_call x1, Pallas kernels, ff_call(): pl.pallas_call(ff_kernel, grid_spec=pltpu.PrefetchScalarGridSpec(num_scal...  11.9 us
  transfers between devices with their start and end apart: 33, of which 7 were waited for; matrix products, arithmetic and copies ran while one was open for 6% of the time, Pallas kernels for 17%

profile of v2, /device:TPU:1, one launch (start us, length us, event | category | flops | bytes accessed | tf_op | source)
XLA Modules:
  0.0 236.1 jit_solution(8187302988354082680)
XLA Ops:
  0.7 3.2 %qkv_forward.1 = bf16[16,2,96,128]{3,2,1,0:T(8,128)(2,1)} custom-call(s32[1]{0:T(128)} %bitcast.place, bf16[256,512]{1,0:T(8,128)(2,1)} %bitcast.24, f32[1,512]{1,0:T(1,128)} %bitcast.28, f32[1,512]{1,0:T(1,128)} %bitcast.30, bf16[512,512]{1,0:T(8,128)(2,1)} %wq.3, bf16[512,512]{1,0:T(8,128)(2,1)} %wk.3, bf16[512,512]{1,0:T(8,128)(2,1)} %wv.3, ...), custom_call_target="tpu_custom_call" | custom-call | flops 402653184 | bytes 1048576 | tf_op jit(solution)/shard_map/qkv_forward/pallas_call | solution.py:96
  3.9 23.7 %all_to_all.40.qkv = bf16[16,2,96,128]{3,2,1,0:T(8,128)(2,1)} all-to-all(bf16[16,2,96,128]{3,2,1,0:T(8,128)(2,1)} %qkv_forward.1), channel_id=1, replica_groups=mesh['x'=4,'zh'=2,'c'=2,'y'=4,'zl'=2] {'x','zh','c'}, dimensions={0} | all-to-all | bytes 1572864 | tf_op jit(solution)/shard_map/all_to_all | solution.py:571
  27.6 13.9 %attend_forward.1 = (bf16[16,2,32,128]{3,2,1,0:T(8,128)(2,1)}, f32[2,32,2048]{2,1,0:T(8,128)}, f32[2,1,2048]{2,1,0:T(1,128)}) custom-call(s32[2]{0:T(128)} %lengths.3, bf16[16,2,96,128]{3,2,1,0:T(8,128)(2,1)} %all_to_all.40.qkv), custom_call_target="tpu_custom_call" | custom-call | flops 17179869184 | bytes 1048576 | tf_op jit(solution)/shard_map/attend_forward/pallas_call | solution.py:178
  41.6 13.4 %all_to_all.41.ob = bf16[16,2,32,128]{3,2,1,0:T(8,128)(2,1)} all-to-all(bf16[16,2,32,128]{3,2,1,0:T(8,128)(2,1)} %get-tuple-element.50), channel_id=1, replica_groups=mesh['x'=4,'zh'=2,'c'=2,'y'=4,'zl'=2] {'x','zh','c'}, dimensions={0} | all-to-all | bytes 524288 | tf_op jit(solution)/shard_map/all_to_all | solution.py:571
  54.9 11.9 %feed_forward.1 = (f32[256,512]{1,0:T(8,128)}, bf16[16,3,4,16,128]{4,3,2,1,0:T(8,128)(2,1)}, bf16[16,3,4,16,128]{4,3,2,1,0:T(8,128)(2,1)}, bf16[16,3,4,16,128]{4...) custom-call(s32[1]{0:T(128)} %bitcast.place, ...), custom_call_target="tpu_custom_call" | custom-call | flops 4831838208 | bytes 1048576 | tf_op jit(solution)/shard_map/feed_forward/pallas_call | solution.py:376
  68.0 3.7 %all-to-all-start.2 = ((bf16[16,2,32,128]{3,2,1,0:T(8,128)(2,1)}), bf16[16,2,32,128]{3,2,1,0:T(8,128)(2,1)S(1)}, u32[]{:S(2)}, u32[]{:S(2)}) async-start(bf16[16,2,32,128]{3,2,1,0:T(8,128)(2,1)} %get-tuple-element.53), calls=%async_computation.2 | async-start | bytes 524288 | tf_op jit(solution)/shard_map/all_to_all | solution.py:571
  71.7 2.3 add_convert_fusion.3
  74.0 1.3 collective-permute-start.9
  75.3 2.3 add_convert_fusion.2
  77.7 2.6 %collective-permute-start.11 = (bf16[16,3,4,16,128]{4,3,2,1,0:T(8,128)(2,1)}, bf16[16,3,4,16,128]{4,3,2,1,0:T(8,128)(2,1)}, u32[]{:S(2)}, u32[]{:S(2)}) collective-permute-start(bf16[16,3,4,16,128]{4,3,2,1,0:T(8,128)(2,1)} %add_convert_fusion.2), channel_id=1, source_target_pairs={{0,4},{2,6},{4,0},{6,2},{1,5},{3,7},{5,1},{7,3},{8,12},{10,14},{12... | collective-permute-start | bytes 2359304 | tf_op jit(solution)/shard_map/ppermute | solution.py:583
  80.3 1.2 add_convert_fusion.1
  81.5 1.1 collective-permute-start.13
  82.5 0.7 copy-done.19
  83.2 25.2 %attend_backward.1 = bf16[16,2,96,128]{3,2,1,0:T(8,128)(2,1)} custom-call(s32[2]{0:T(128)} %lengths.3, bf16[16,2,96,128]{3,2,1,0:T(8,128)(2,1)} %all_to_all.40.qkv, bf16[16,2,32,128]{3,2,1,0:T(8,128)(2,1)} %copy-done.19, f32[2,32,2048]{2,1,0:T(8,128)} %get-tuple-element.54.mixed, f32[2,1,2048]{2,1,0:T(1,128)} %get-tuple-element.55.total, ...), custom_call_target="tpu_custom_call" | custom-call | flops 17179869184 | bytes 1048576 | tf_op jit(solution)/shard_map/attend_backward/pallas_call | solution.py:268
  108.4 8.3 %all-to-all-start.3 = ((bf16[16,2,96,128]{3,2,1,0:T(8,128)(2,1)}), bf16[16,2,96,128]{3,2,1,0:T(8,128)(2,1)S(1)}, u32[]{:S(2)}, u32[]{:S(2)}) async-start(bf16[16,2,96,128]{3,2,1,0:T(8,128)(2,1)} %attend_backward.1), calls=%async_computation.3 | async-start | bytes 1572864 | tf_op jit(solution)/shard_map/all_to_all | solution.py:571
  116.7 3.0 %add_convert_fusion = bf16[16,3,4,16,128]{4,3,2,1,0:T(8,128)(2,1)} fusion(bf16[16,3,4,16,128]{4,3,2,1,0:T(8,128)(2,1)} %collective-permute-done.13, bf16[16,3,4,16,128]{4,3,2,1,0:T(8,128)(2,1)} %collective-permute-done.11, bf16[16,3,4,16,128]{4,3,2,1,0:T(8,128)(2,1)S(1)} %collective-permute-done.9, bf16[16,3,4,16,128]{4,3,2,1,0:T(8,128)(2,1)S(1)} %collective-permute-done.7, ...), kind=kLoop, calls=%fused_computation | loop fusion | flops 3932160 | bytes 4718592 | tf_op jit(solution)/shard_map/convert_element_type | solution.py:579
  119.8 11.1 %all-to-all-done.3.dqkv = bf16[16,2,96,128]{3,2,1,0:T(8,128)(2,1)S(1)} async-done(((bf16[16,2,96,128]{3,2,1,0:T(8,128)(2,1)}), bf16[16,2,96,128]{3,2,1,0:T(8,128)(2,1)S(1)}, u32[]{:S(2)}, u32[]{:S(2)}) %all-to-all-start.3) | async-done | bytes 786464 | tf_op jit(solution)/shard_map/all_to_all | solution.py:571
  130.8 3.6 %all-to-all-start.4 = ((bf16[16,3,4,16,128]{4,3,2,1,0:T(8,128)(2,1)}), bf16[16,3,4,16,128]{4,3,2,1,0:T(8,128)(2,1)S(1)}, u32[]{:S(2)}, u32[]{:S(2)}) async-start(bf16[16,3,4,16,128]{4,3,2,1,0:T(8,128)(2,1)} %add_convert_fusion), calls=%async_computation.4 | async-start | bytes 1572864 | tf_op jit(solution)/shard_map/all_to_all | solution.py:571
  134.5 5.2 %projection_backward.1 = (f32[256,512]{1,0:T(8,128)}, bf16[16,5,16,128]{3,2,1,0:T(8,128)(2,1)}, bf16[16,5,16,128]{3,2,1,0:T(8,128)(2,1)}, bf16[16,5,16,128]{3,2,...) custom-call(s32[1]{0:T(128)} %bitcast.place, ...), custom_call_target="tpu_custom_call" | custom-call | flops 805306368 | bytes 1048576 | tf_op jit(solution)/shard_map/projection_backward/pallas_call | solution.py:456
  139.6 1.1 collective-permute-start.1
  141.3 0.9 collective-permute-done.1
  142.2 1.1 add_convert_fusion.7
  143.7 3.4 %all-to-all-done.4 = bf16[16,3,4,16,128]{4,3,2,1,0:T(8,128)(2,1)S(1)} async-done(((bf16[16,3,4,16,128]{4,3,2,1,0:T(8,128)(2,1)}), bf16[16,3,4,16,128]{4,3,2,1,0:T(8,128)(2,1)S(1)}, u32[]{:S(2)}, u32[]{:S(2)}) %all-to-all-start.4) | async-done | bytes 786464 | tf_op jit(solution)/shard_map/all_to_all | solution.py:571
  147.3 1.1 broadcast_in_dim.4
  148.4 3.9 %all-to-all-start.5 = ((bf16[16,3,4,16,128]{4,3,2,1,0:T(8,128)(2,1)}), bf16[16,3,4,16,128]{4,3,2,1,0:T(8,128)(2,1)S(1)}, u32[]{:S(2)}, u32[]{:S(2)}) async-start(bf16[16,3,4,16,128]{4,3,2,1,0:T(8,128)(2,1)} %broadcast_in_dim.4), calls=%async_computation.5 | async-start | bytes 1572864 | tf_op jit(solution)/shard_map/all_to_all | solution.py:571
  153.0 2.7 %collective-permute-start.6 = (bf16[16,5,16,128]{3,2,1,0:T(8,128)(2,1)S(1)}, bf16[16,5,16,128]{3,2,1,0:T(8,128)(2,1)S(1)}, u32[]{:S(2)}, u32[]{:S(2)}) collective-permute-start(bf16[16,5,16,128]{3,2,1,0:T(8,128)(2,1)S(1)} %add_convert_fusion.5), channel_id=1, source_target_pairs={{0,6},{2,0},{4,2},{6,4},{1,7},{3,1},{5,3},{7,5},{8,14},{10,8},{12,... | collective-permute-start | bytes 983048 | tf_op jit(solution)/shard_map/ppermute | solution.py:583
  155.7 7.1 %all-to-all-done.5.refs_0_ = bf16[16,3,4,16,128]{4,3,2,1,0:T(8,128)(2,1)S(1)} async-done(((bf16[16,3,4,16,128]{4,3,2,1,0:T(8,128)(2,1)}), bf16[16,3,4,16,128]{4,3,2,1,0:T(8,128)(2,1)S(1)}, u32[]{:S(2)}, u32[]{:S(2)}) %all-to-all-start.5) | async-done | bytes 786464 | tf_op jit(solution)/shard_map/all_to_all | solution.py:571
  163.2 5.0 %collective-permute-start.24 = (bf16[16,3,4,16,128]{4,3,2,1,0:T(8,128)(2,1)S(1)}, bf16[16,3,4,16,128]{4,3,2,1,0:T(8,128)(2,1)S(1)}, u32[]{:S(2)}, u32[]{:S(2)}) collective-permute-start(bf16[16,3,4,16,128]{4,3,2,1,0:T(8,128)(2,1)S(1)} %all-to-all-done.5.refs_0_), channel_id=1, source_target_pairs={{0,4},{2,6},{4,0},{6,2},{1,5},{3,7},{5,1},{7,3},{8,12},{10,14},{12... | collective-permute-start | bytes 2359304 | tf_op jit(solution)/shard_map/ppermute | solution.py:583
  168.2 2.0 collective-permute-done.6
  170.2 2.0 add_convert_fusion.4
  172.2 6.9 %all-to-all-start.6 = ((bf16[16,5,16,128]{3,2,1,0:T(8,128)(2,1)}), bf16[16,5,16,128]{3,2,1,0:T(8,128)(2,1)S(1)}, u32[]{:S(2)}, u32[]{:S(2)}) async-start(bf16[16,5,16,128]{3,2,1,0:T(8,128)(2,1)} %add_convert_fusion.4), calls=%async_computation.6 | async-start | bytes 655360 | tf_op jit(solution)/shard_map/all_to_all | solution.py:571
  179.2 4.0 %collective-permute-start.26 = (bf16[16,3,4,16,128]{4,3,2,1,0:T(8,128)(2,1)S(1)}, bf16[16,3,4,16,128]{4,3,2,1,0:T(8,128)(2,1)S(1)}, u32[]{:S(2)}, u32[]{:S(2)}) collective-permute-start(bf16[16,3,4,16,128]{4,3,2,1,0:T(8,128)(2,1)S(1)} %all-to-all-done.5.refs_0_), channel_id=1, source_target_pairs={{0,6},{2,0},{4,2},{6,4},{1,7},{3,1},{5,3},{7,5},{8,14},{10,8},{12,... | collective-permute-start | bytes 2359304 | tf_op jit(solution)/shard_map/ppermute | solution.py:583
  183.2 3.7 %all-to-all-done.6 = bf16[16,5,16,128]{3,2,1,0:T(8,128)(2,1)S(1)} async-done(((bf16[16,5,16,128]{3,2,1,0:T(8,128)(2,1)}), bf16[16,5,16,128]{3,2,1,0:T(8,128)(2,1)S(1)}, u32[]{:S(2)}, u32[]{:S(2)}) %all-to-all-start.6) | async-done | bytes 327712 | tf_op jit(solution)/shard_map/all_to_all | solution.py:571
  187.0 10.8 %all_to_all.42.refs_0_ = bf16[16,4,16,128]{3,2,1,0:T(8,128)(2,1)S(1)} all-to-all(bf16[16,4,16,128]{3,2,1,0:T(8,128)(2,1)S(1)} %broadcast_in_dim.5), channel_id=1, replica_groups=mesh['x'=4,'zh'=2,'c'=2,'y'=4,'zl'=2] {'x','zh','zl'}, dimensions={0} | all-to-all | bytes 524288 | tf_op jit(solution)/shard_map/all_to_all | solution.py:571
  197.8 4.3 %collective-permute-start.14 = (bf16[16,4,16,128]{3,2,1,0:T(8,128)(2,1)S(1)}, bf16[16,4,16,128]{3,2,1,0:T(8,128)(2,1)S(1)}, u32[]{:S(2)}, u32[]{:S(2)}) collective-permute-start(bf16[16,4,16,128]{3,2,1,0:T(8,128)(2,1)S(1)} %all_to_all.42.refs_0_), channel_id=1, source_target_pairs={{0,2},{2,4},{4,6},{6,0},{1,3},{3,5},{5,7},{7,1},{8,10},{10,12},{12... | collective-permute-start | bytes 786440 | tf_op jit(solution)/shard_map/ppermute | solution.py:583
  202.1 1.2 collective-permute-start.15
  203.3 1.2 collective-permute-start.16
  204.5 3.8 %collective-permute-start.17 = (bf16[16,4,16,128]{3,2,1,0:T(8,128)(2,1)S(1)}, bf16[16,4,16,128]{3,2,1,0:T(8,128)(2,1)S(1)}, u32[]{:S(2)}, u32[]{:S(2)}) collective-permute-start(bf16[16,4,16,128]{3,2,1,0:T(8,128)(2,1)S(1)} %all_to_all.42.refs_0_), channel_id=1, source_target_pairs={{0,8},{8,0},{1,9},{9,1},{2,10},{10,2},{3,11},{11,3},{4,12},{12,4},... | collective-permute-start | bytes 786440 | tf_op jit(solution)/shard_map/ppermute | solution.py:598
  208.2 4.7 %collective-permute-start.18 = (bf16[16,4,16,128]{3,2,1,0:T(8,128)(2,1)S(1)}, bf16[16,4,16,128]{3,2,1,0:T(8,128)(2,1)S(1)}, u32[]{:S(2)}, u32[]{:S(2)}) collective-permute-start(bf16[16,4,16,128]{3,2,1,0:T(8,128)(2,1)S(1)} %collective-permute-done.14.refs_1_), channel_id=1, source_target_pairs={{0,8},{8,0},{1,9},{9,1},{2,10},{10,2},{3,11},{11,3},{4,12},{12,4},... | collective-permute-start | bytes 786440 | tf_op jit(solution)/shard_map/ppermute | solution.py:598
  213.1 0.8 copy-done.10
  213.8 2.3 collective-permute-start.23
  216.8 2.4 %collective-permute-done.19.refs_6_ = bf16[16,4,16,128]{3,2,1,0:T(8,128)(2,1)S(1)} collective-permute-done((bf16[16,4,16,128]{3,2,1,0:T(8,128)(2,1)S(1)}, bf16[16,4,16,128]{3,2,1,0:T(8,128)(2,1)S(1)}, u32[]{:S(2)}, u32[]{:S(2)}) %collective-permute-start.19) | collective-permute-done | bytes 262176 | tf_op jit(solution)/shard_map/ppermute | solution.py:598
  219.2 0.7 copy-done.18
  220.3 0.6 fusion
  220.9 4.9 %unpack_feed_forward.2 = (f32[2,256,2048]{2,1,0:T(8,128)}, f32[2,256,2048]{2,1,0:T(8,128)}, f32[4,2,256,512]{3,2,1,0:T(8,128)}) custom-call(s32[1]{0:T(128)} %bitcast.place, bf16[16,3,4,16,128]{4,3,2,1,0:T(8,128)(2,1)} %copy-done.1, bf16[16,3,4,16,128]{4,3,2,1,0:T(8,128)(2,1)} %collective-permute-done.22.refs_1_, bf16[16,3,4,16,128]{4,3,2,1,0:T(8,128)(2,1)} %copy-done.9, ...), custom_call_target="tpu_custom_call" | custom-call | flops 1048576 | bytes 9437184 | tf_op jit(solution)/shard_map/unpack_feed_forward/pallas_call | solution.py:508
  225.9 3.8 %unpack_projections.1 = (f32[512,512]{1,0:T(8,128)}, f32[512,512]{1,0:T(8,128)}, f32[512,512]{1,0:T(8,128)}, f32[512,512]{1,0:T(8,128)}) custom-call(s32[1]{0:T(128)} %bitcast.place, bf16[16,4,16,128]{3,2,1,0:T(8,128)(2,1)} %copy-done.2, bf16[16,4,16,128]{3,2,1,0:T(8,128)(2,1)} %copy-done.14, bf16[16,4,16,128]{3,2,1,0:T(8,128)(2,1)} %copy-done.15, ...), custom_call_target="tpu_custom_call" | custom-call | flops 1048576 | bytes 6291456 | tf_op jit(solution)/shard_map/unpack_projections/pallas_call | solution.py:546
  229.8 0.8 copy-done.3
  231.2 4.9 %unpack_feed_forward.3 = (f32[2,256,2048]{2,1,0:T(8,128)}, f32[2,256,2048]{2,1,0:T(8,128)}, f32[4,2,256,512]{3,2,1,0:T(8,128)}) custom-call(s32[1]{0:T(128)} %bitcast.place, bf16[16,3,4,16,128]{4,3,2,1,0:T(8,128)(2,1)} %copy-done.3, bf16[16,3,4,16,128]{4,3,2,1,0:T(8,128)(2,1)} %copy-done.4, ...), custom_call_target="tpu_custom_call", output_to_operand_aliasing={{0}: (5, {}), {1}: (6, {}), {2}: (7, {})} | custom-call | flops 1048576 | bytes 9437184 | tf_op jit(solution)/shard_map/unpack_feed_forward/pallas_call | solution.py:508
  (84 shorter events, 5.2 us)
Async XLA Ops:
  66.9 8.5 %copy-start.8 = (bf16[16,3,4,16,128]{4,3,2,1,0:T(8,128)(2,1)S(1)}, bf16[16,3,4,16,128]{4,3,2,1,0:T(8,128)(2,1)}, u32[]{:S(2)}) copy-start(bf16[16,3,4,16,128]{4,3,2,1,0:T(8,128)(2,1)} %get-tuple-element.71) | copy-start | bytes 2359300
  66.9 4.8 %collective-permute-start.8 = (bf16[16,3,4,16,128]{4,3,2,1,0:T(8,128)(2,1)}, bf16[16,3,4,16,128]{4,3,2,1,0:T(8,128)(2,1)S(1)}, u32[]{:S(2)}, u32[]{:S(2)}) collective-permute-start(bf16[16,3,4,16,128]{4,3,2,1,0:T(8,128)(2,1)} %get-tuple-element.70), channel_id=1, source_target_pairs={{0,8},{8,0},{1,9},{9,1},{2,10},{10,2},{3,11},{11,3},{4,12},{12,4},... | collective-permute-start | bytes 2359304 | tf_op jit(solution)/shard_map/ppermute | solution.py:587
  67.4 8.0 %collective-permute-start.10 = (bf16[16,3,4,16,128]{4,3,2,1,0:T(8,128)(2,1)}, bf16[16,3,4,16,128]{4,3,2,1,0:T(8,128)(2,1)}, u32[]{:S(2)}, u32[]{:S(2)}) collective-permute-start(bf16[16,3,4,16,128]{4,3,2,1,0:T(8,128)(2,1)} %get-tuple-element.72), channel_id=1, source_target_pairs={{0,8},{8,0},{1,9},{9,1},{2,10},{10,2},{3,11},{11,3},{4,12},{12,4},... | collective-permute-start | bytes 2359304 | tf_op jit(solution)/shard_map/ppermute | solution.py:587
  67.5 12.8 %collective-permute-start.12 = (bf16[16,3,4,16,128]{4,3,2,1,0:T(8,128)(2,1)}, bf16[16,3,4,16,128]{4,3,2,1,0:T(8,128)(2,1)S(1)}, u32[]{:S(2)}, u32[]{:S(2)}) collective-permute-start(bf16[16,3,4,16,128]{4,3,2,1,0:T(8,128)(2,1)} %get-tuple-element.74), channel_id=1, source_target_pairs={{0,8},{8,0},{1,9},{9,1},{2,10},{10,2},{3,11},{11,3},{4,12},{12,4},... | collective-permute-start | bytes 2359304 | tf_op jit(solution)/shard_map/ppermute | solution.py:587
  67.9 48.8 %collective-permute-start.7 = (bf16[16,3,4,16,128]{4,3,2,1,0:T(8,128)(2,1)}, bf16[16,3,4,16,128]{4,3,2,1,0:T(8,128)(2,1)S(1)}, u32[]{:S(2)}, u32[]{:S(2)}) collective-permute-start(bf16[16,3,4,16,128]{4,3,2,1,0:T(8,128)(2,1)} %get-tuple-element.68), channel_id=1, source_target_pairs={{0,8},{8,0},{1,9},{9,1},{2,10},{10,2},{3,11},{11,3},{4,12},{12,4},... | collective-permute-start | bytes 2359304 | tf_op jit(solution)/shard_map/ppermute | solution.py:587
  68.0 14.5 %all-to-all-start.2 = ((bf16[16,2,32,128]{3,2,1,0:T(8,128)(2,1)}), bf16[16,2,32,128]{3,2,1,0:T(8,128)(2,1)S(1)}, u32[]{:S(2)}, u32[]{:S(2)}) async-start(bf16[16,2,32,128]{3,2,1,0:T(8,128)(2,1)} %get-tuple-element.53), calls=%async_computation.2 | async-start | bytes 524288 | tf_op jit(solution)/shard_map/all_to_all | solution.py:571
  74.0 6.2 %copy-start.7 = (bf16[16,3,4,16,128]{4,3,2,1,0:T(8,128)(2,1)S(1)}, bf16[16,3,4,16,128]{4,3,2,1,0:T(8,128)(2,1)}, u32[]{:S(2)}) copy-start(bf16[16,3,4,16,128]{4,3,2,1,0:T(8,128)(2,1)} %get-tuple-element.73) | copy-start | bytes 2359300
  74.0 42.6 %collective-permute-start.9 = (bf16[16,3,4,16,128]{4,3,2,1,0:T(8,128)(2,1)}, bf16[16,3,4,16,128]{4,3,2,1,0:T(8,128)(2,1)S(1)}, u32[]{:S(2)}, u32[]{:S(2)}) collective-permute-start(bf16[16,3,4,16,128]{4,3,2,1,0:T(8,128)(2,1)} %add_convert_fusion.3), channel_id=1, source_target_pairs={{0,2},{2,4},{4,6},{6,0},{1,3},{3,5},{5,7},{7,1},{8,10},{10,12},{12... | collective-permute-start | bytes 2359304 | tf_op jit(solution)/shard_map/ppermute | solution.py:583
  77.7 39.0 %collective-permute-start.11 = (bf16[16,3,4,16,128]{4,3,2,1,0:T(8,128)(2,1)}, bf16[16,3,4,16,128]{4,3,2,1,0:T(8,128)(2,1)}, u32[]{:S(2)}, u32[]{:S(2)}) collective-permute-start(bf16[16,3,4,16,128]{4,3,2,1,0:T(8,128)(2,1)} %add_convert_fusion.2), channel_id=1, source_target_pairs={{0,4},{2,6},{4,0},{6,2},{1,5},{3,7},{5,1},{7,3},{8,12},{10,14},{12... | collective-permute-start | bytes 2359304 | tf_op jit(solution)/shard_map/ppermute | solution.py:583
  81.5 35.2 %collective-permute-start.13 = (bf16[16,3,4,16,128]{4,3,2,1,0:T(8,128)(2,1)}, bf16[16,3,4,16,128]{4,3,2,1,0:T(8,128)(2,1)}, u32[]{:S(2)}, u32[]{:S(2)}) collective-permute-start(bf16[16,3,4,16,128]{4,3,2,1,0:T(8,128)(2,1)} %add_convert_fusion.1), channel_id=1, source_target_pairs={{0,6},{2,0},{4,2},{6,4},{1,7},{3,1},{5,3},{7,5},{8,14},{10,8},{12,... | collective-permute-start | bytes 2359304 | tf_op jit(solution)/shard_map/ppermute | solution.py:583
  108.4 8.3 %copy-start.6 = (bf16[16,3,4,16,128]{4,3,2,1,0:T(8,128)(2,1)S(1)}, bf16[16,3,4,16,128]{4,3,2,1,0:T(8,128)(2,1)}, u32[]{:S(2)}) copy-start(bf16[16,3,4,16,128]{4,3,2,1,0:T(8,128)(2,1)} %get-tuple-element.67) | copy-start | bytes 2359300
  108.4 22.4 %all-to-all-start.3 = ((bf16[16,2,96,128]{3,2,1,0:T(8,128)(2,1)}), bf16[16,2,96,128]{3,2,1,0:T(8,128)(2,1)S(1)}, u32[]{:S(2)}, u32[]{:S(2)}) async-start(bf16[16,2,96,128]{3,2,1,0:T(8,128)(2,1)} %attend_backward.1), calls=%async_computation.3 | async-start | bytes 1572864 | tf_op jit(solution)/shard_map/all_to_all | solution.py:571
  130.8 3.6 %copy-start = (bf16[16,2,96,128]{3,2,1,0:T(8,128)(2,1)}, bf16[16,2,96,128]{3,2,1,0:T(8,128)(2,1)S(1)}, u32[]{:S(2)}) copy-start(bf16[16,2,96,128]{3,2,1,0:T(8,128)(2,1)S(1)} %all-to-all-done.3.dqkv) | copy-start | bytes 2359300
  130.8 16.4 %all-to-all-start.4 = ((bf16[16,3,4,16,128]{4,3,2,1,0:T(8,128)(2,1)}), bf16[16,3,4,16,128]{4,3,2,1,0:T(8,128)(2,1)S(1)}, u32[]{:S(2)}, u32[]{:S(2)}) async-start(bf16[16,3,4,16,128]{4,3,2,1,0:T(8,128)(2,1)} %add_convert_fusion), calls=%async_computation.4 | async-start | bytes 1572864 | tf_op jit(solution)/shard_map/all_to_all | solution.py:571
  139.6 2.6 %collective-permute-start.1 = (bf16[16,5,16,128]{3,2,1,0:T(8,128)(2,1)}, bf16[16,5,16,128]{3,2,1,0:T(8,128)(2,1)S(1)}, u32[]{:S(2)}, u32[]{:S(2)}) collective-permute-start(bf16[16,5,16,128]{3,2,1,0:T(8,128)(2,1)} %get-tuple-element.62), channel_id=1, source_target_pairs={{0,8},{8,0},{1,9},{9,1},{2,10},{10,2},{3,11},{11,3},{4,12},{12,4},... | collective-permute-start | bytes 983048 | tf_op jit(solution)/shard_map/ppermute | solution.py:587
  140.7 11.6 %collective-permute-start.3 = (bf16[16,5,16,128]{3,2,1,0:T(8,128)(2,1)}, bf16[16,5,16,128]{3,2,1,0:T(8,128)(2,1)S(1)}, u32[]{:S(2)}, u32[]{:S(2)}) collective-permute-start(bf16[16,5,16,128]{3,2,1,0:T(8,128)(2,1)} %get-tuple-element.64), channel_id=1, source_target_pairs={{0,8},{8,0},{1,9},{9,1},{2,10},{10,2},{3,11},{11,3},{4,12},{12,4},... | collective-permute-start | bytes 983048 | tf_op jit(solution)/shard_map/ppermute | solution.py:587
  140.8 12.1 %collective-permute-start.5 = (bf16[16,5,16,128]{3,2,1,0:T(8,128)(2,1)}, bf16[16,5,16,128]{3,2,1,0:T(8,128)(2,1)S(1)}, u32[]{:S(2)}, u32[]{:S(2)}) collective-permute-start(bf16[16,5,16,128]{3,2,1,0:T(8,128)(2,1)} %get-tuple-element.66), channel_id=1, source_target_pairs={{0,8},{8,0},{1,9},{9,1},{2,10},{10,2},{3,11},{11,3},{4,12},{12,4},... | collective-permute-start | bytes 983048 | tf_op jit(solution)/shard_map/ppermute | solution.py:587
  141.2 21.9 %collective-permute-start = (bf16[16,5,16,128]{3,2,1,0:T(8,128)(2,1)}, bf16[16,5,16,128]{3,2,1,0:T(8,128)(2,1)S(1)}, u32[]{:S(2)}, u32[]{:S(2)}) collective-permute-start(bf16[16,5,16,128]{3,2,1,0:T(8,128)(2,1)} %get-tuple-element.60), channel_id=1, source_target_pairs={{0,8},{8,0},{1,9},{9,1},{2,10},{10,2},{3,11},{11,3},{4,12},{12,4},... | collective-permute-start | bytes 983048 | tf_op jit(solution)/shard_map/ppermute | solution.py:587
  143.3 9.1 %copy-start.12 = (bf16[16,5,16,128]{3,2,1,0:T(8,128)(2,1)S(1)}, bf16[16,5,16,128]{3,2,1,0:T(8,128)(2,1)}, u32[]{:S(2)}) copy-start(bf16[16,5,16,128]{3,2,1,0:T(8,128)(2,1)} %get-tuple-element.63) | copy-start | bytes 983044
  143.3 24.9 %collective-permute-start.2 = (bf16[16,5,16,128]{3,2,1,0:T(8,128)(2,1)S(1)}, bf16[16,5,16,128]{3,2,1,0:T(8,128)(2,1)}, u32[]{:S(2)}, u32[]{:S(2)}) collective-permute-start(bf16[16,5,16,128]{3,2,1,0:T(8,128)(2,1)S(1)} %add_convert_fusion.7), channel_id=1, source_target_pairs={{0,2},{2,4},{4,6},{6,0},{1,3},{3,5},{5,7},{7,1},{8,10},{10,12},{12... | collective-permute-start | bytes 983048 | tf_op jit(solution)/shard_map/ppermute | solution.py:583
  147.3 5.6 %copy-start.11 = (bf16[16,5,16,128]{3,2,1,0:T(8,128)(2,1)S(1)}, bf16[16,5,16,128]{3,2,1,0:T(8,128)(2,1)}, u32[]{:S(2)}) copy-start(bf16[16,5,16,128]{3,2,1,0:T(8,128)(2,1)} %get-tuple-element.65) | copy-start | bytes 983044
  148.4 21.8 %copy-start.13 = (bf16[16,5,16,128]{3,2,1,0:T(8,128)(2,1)S(1)}, bf16[16,5,16,128]{3,2,1,0:T(8,128)(2,1)}, u32[]{:S(2)}) copy-start(bf16[16,5,16,128]{3,2,1,0:T(8,128)(2,1)} %get-tuple-element.59) | copy-start | bytes 983044
  148.4 14.4 %all-to-all-start.5 = ((bf16[16,3,4,16,128]{4,3,2,1,0:T(8,128)(2,1)}), bf16[16,3,4,16,128]{4,3,2,1,0:T(8,128)(2,1)S(1)}, u32[]{:S(2)}, u32[]{:S(2)}) async-start(bf16[16,3,4,16,128]{4,3,2,1,0:T(8,128)(2,1)} %broadcast_in_dim.4), calls=%async_computation.5 | async-start | bytes 1572864 | tf_op jit(solution)/shard_map/all_to_all | solution.py:571
  152.4 15.8 %collective-permute-start.4 = (bf16[16,5,16,128]{3,2,1,0:T(8,128)(2,1)S(1)}, bf16[16,5,16,128]{3,2,1,0:T(8,128)(2,1)}, u32[]{:S(2)}, u32[]{:S(2)}) collective-permute-start(bf16[16,5,16,128]{3,2,1,0:T(8,128)(2,1)S(1)} %add_convert_fusion.6), channel_id=1, source_target_pairs={{0,4},{2,6},{4,0},{6,2},{1,5},{3,7},{5,1},{7,3},{8,12},{10,14},{12... | collective-permute-start | bytes 983048 | tf_op jit(solution)/shard_map/ppermute | solution.py:583
  153.0 17.2 %collective-permute-start.6 = (bf16[16,5,16,128]{3,2,1,0:T(8,128)(2,1)S(1)}, bf16[16,5,16,128]{3,2,1,0:T(8,128)(2,1)S(1)}, u32[]{:S(2)}, u32[]{:S(2)}) collective-permute-start(bf16[16,5,16,128]{3,2,1,0:T(8,128)(2,1)S(1)} %add_convert_fusion.5), channel_id=1, source_target_pairs={{0,6},{2,0},{4,2},{6,4},{1,7},{3,1},{5,3},{7,5},{8,14},{10,8},{12,... | collective-permute-start | bytes 983048 | tf_op jit(solution)/shard_map/ppermute | solution.py:583
  162.8 50.2 %copy-start.1 = (bf16[16,3,4,16,128]{4,3,2,1,0:T(8,128)(2,1)}, bf16[16,3,4,16,128]{4,3,2,1,0:T(8,128)(2,1)S(1)}, u32[]{:S(2)}) copy-start(bf16[16,3,4,16,128]{4,3,2,1,0:T(8,128)(2,1)S(1)} %all-to-all-done.5.refs_0_) | copy-start | bytes 2359300
  162.8 40.5 %collective-permute-start.22 = (bf16[16,3,4,16,128]{4,3,2,1,0:T(8,128)(2,1)S(1)}, bf16[16,3,4,16,128]{4,3,2,1,0:T(8,128)(2,1)}, u32[]{:S(2)}, u32[]{:S(2)}) collective-permute-start(bf16[16,3,4,16,128]{4,3,2,1,0:T(8,128)(2,1)S(1)} %all-to-all-done.5.refs_0_), channel_id=1, source_target_pairs={{0,2},{2,4},{4,6},{6,0},{1,3},{3,5},{5,7},{7,1},{8,10},{10,12},{12... | collective-permute-start | bytes 2359304 | tf_op jit(solution)/shard_map/ppermute | solution.py:583
  163.2 41.3 %collective-permute-start.24 = (bf16[16,3,4,16,128]{4,3,2,1,0:T(8,128)(2,1)S(1)}, bf16[16,3,4,16,128]{4,3,2,1,0:T(8,128)(2,1)S(1)}, u32[]{:S(2)}, u32[]{:S(2)}) collective-permute-start(bf16[16,3,4,16,128]{4,3,2,1,0:T(8,128)(2,1)S(1)} %all-to-all-done.5.refs_0_), channel_id=1, source_target_pairs={{0,4},{2,6},{4,0},{6,2},{1,5},{3,7},{5,1},{7,3},{8,12},{10,14},{12... | collective-permute-start | bytes 2359304 | tf_op jit(solution)/shard_map/ppermute | solution.py:583
  172.2 14.6 %all-to-all-start.6 = ((bf16[16,5,16,128]{3,2,1,0:T(8,128)(2,1)}), bf16[16,5,16,128]{3,2,1,0:T(8,128)(2,1)S(1)}, u32[]{:S(2)}, u32[]{:S(2)}) async-start(bf16[16,5,16,128]{3,2,1,0:T(8,128)(2,1)} %add_convert_fusion.4), calls=%async_computation.6 | async-start | bytes 655360 | tf_op jit(solution)/shard_map/all_to_all | solution.py:571
  179.2 33.8 %collective-permute-start.26 = (bf16[16,3,4,16,128]{4,3,2,1,0:T(8,128)(2,1)S(1)}, bf16[16,3,4,16,128]{4,3,2,1,0:T(8,128)(2,1)S(1)}, u32[]{:S(2)}, u32[]{:S(2)}) collective-permute-start(bf16[16,3,4,16,128]{4,3,2,1,0:T(8,128)(2,1)S(1)} %all-to-all-done.5.refs_0_), channel_id=1, source_target_pairs={{0,6},{2,0},{4,2},{6,4},{1,7},{3,1},{5,3},{7,5},{8,14},{10,8},{12,... | collective-permute-start | bytes 2359304 | tf_op jit(solution)/shard_map/ppermute | solution.py:583
  197.8 28.1 %copy-start.2 = (bf16[16,4,16,128]{3,2,1,0:T(8,128)(2,1)}, bf16[16,4,16,128]{3,2,1,0:T(8,128)(2,1)S(1)}, u32[]{:S(2)}) copy-start(bf16[16,4,16,128]{3,2,1,0:T(8,128)(2,1)S(1)} %all_to_all.42.refs_0_) | copy-start | bytes 786436
  197.8 10.4 %collective-permute-start.14 = (bf16[16,4,16,128]{3,2,1,0:T(8,128)(2,1)S(1)}, bf16[16,4,16,128]{3,2,1,0:T(8,128)(2,1)S(1)}, u32[]{:S(2)}, u32[]{:S(2)}) collective-permute-start(bf16[16,4,16,128]{3,2,1,0:T(8,128)(2,1)S(1)} %all_to_all.42.refs_0_), channel_id=1, source_target_pairs={{0,2},{2,4},{4,6},{6,0},{1,3},{3,5},{5,7},{7,1},{8,10},{10,12},{12... | collective-permute-start | bytes 786440 | tf_op jit(solution)/shard_map/ppermute | solution.py:583
  202.1 11.8 %collective-permute-start.15 = (bf16[16,4,16,128]{3,2,1,0:T(8,128)(2,1)S(1)}, bf16[16,4,16,128]{3,2,1,0:T(8,128)(2,1)S(1)}, u32[]{:S(2)}, u32[]{:S(2)}) collective-permute-start(bf16[16,4,16,128]{3,2,1,0:T(8,128)(2,1)S(1)} %all_to_all.42.refs_0_), channel_id=1, source_target_pairs={{0,4},{2,6},{4,0},{6,2},{1,5},{3,7},{5,1},{7,3},{8,12},{10,14},{12... | collective-permute-start | bytes 786440 | tf_op jit(solution)/shard_map/ppermute | solution.py:583
  203.3 12.9 %collective-permute-start.16 = (bf16[16,4,16,128]{3,2,1,0:T(8,128)(2,1)S(1)}, bf16[16,4,16,128]{3,2,1,0:T(8,128)(2,1)}, u32[]{:S(2)}, u32[]{:S(2)}) collective-permute-start(bf16[16,4,16,128]{3,2,1,0:T(8,128)(2,1)S(1)} %all_to_all.42.refs_0_), channel_id=1, source_target_pairs={{0,6},{2,0},{4,2},{6,4},{1,7},{3,1},{5,3},{7,5},{8,14},{10,8},{12,... | collective-permute-start | bytes 786440 | tf_op jit(solution)/shard_map/ppermute | solution.py:583
  204.5 8.5 %copy-start.9 = (bf16[16,3,4,16,128]{4,3,2,1,0:T(8,128)(2,1)}, bf16[16,3,4,16,128]{4,3,2,1,0:T(8,128)(2,1)S(1)}, u32[]{:S(2)}) copy-start(bf16[16,3,4,16,128]{4,3,2,1,0:T(8,128)(2,1)S(1)} %collective-permute-done.24.refs_2_) | copy-start | bytes 2359300
  204.5 11.8 %collective-permute-start.17 = (bf16[16,4,16,128]{3,2,1,0:T(8,128)(2,1)S(1)}, bf16[16,4,16,128]{3,2,1,0:T(8,128)(2,1)S(1)}, u32[]{:S(2)}, u32[]{:S(2)}) collective-permute-start(bf16[16,4,16,128]{3,2,1,0:T(8,128)(2,1)S(1)} %all_to_all.42.refs_0_), channel_id=1, source_target_pairs={{0,8},{8,0},{1,9},{9,1},{2,10},{10,2},{3,11},{11,3},{4,12},{12,4},... | collective-permute-start | bytes 786440 | tf_op jit(solution)/shard_map/ppermute | solution.py:598
  208.2 17.6 %copy-start.14 = (bf16[16,4,16,128]{3,2,1,0:T(8,128)(2,1)}, bf16[16,4,16,128]{3,2,1,0:T(8,128)(2,1)S(1)}, u32[]{:S(2)}) copy-start(bf16[16,4,16,128]{3,2,1,0:T(8,128)(2,1)S(1)} %collective-permute-done.14.refs_1_) | copy-start | bytes 786436
  208.2 8.5 %collective-permute-start.18 = (bf16[16,4,16,128]{3,2,1,0:T(8,128)(2,1)S(1)}, bf16[16,4,16,128]{3,2,1,0:T(8,128)(2,1)S(1)}, u32[]{:S(2)}, u32[]{:S(2)}) collective-permute-start(bf16[16,4,16,128]{3,2,1,0:T(8,128)(2,1)S(1)} %collective-permute-done.14.refs_1_), channel_id=1, source_target_pairs={{0,8},{8,0},{1,9},{9,1},{2,10},{10,2},{3,11},{11,3},{4,12},{12,4},... | collective-permute-start | bytes 786440 | tf_op jit(solution)/shard_map/ppermute | solution.py:598
  213.0 16.8 %collective-permute-start.21 = (bf16[16,3,4,16,128]{4,3,2,1,0:T(8,128)(2,1)S(1)}, bf16[16,3,4,16,128]{4,3,2,1,0:T(8,128)(2,1)S(1)}, u32[]{:S(2)}, u32[]{:S(2)}) collective-permute-start(bf16[16,3,4,16,128]{4,3,2,1,0:T(8,128)(2,1)S(1)} %all-to-all-done.5.refs_0_), channel_id=1, source_target_pairs={{0,8},{8,0},{1,9},{9,1},{2,10},{10,2},{3,11},{11,3},{4,12},{12,4},... | collective-permute-start | bytes 2359304 | tf_op jit(solution)/shard_map/ppermute | solution.py:598
  213.8 12.0 %copy-start.15 = (bf16[16,4,16,128]{3,2,1,0:T(8,128)(2,1)}, bf16[16,4,16,128]{3,2,1,0:T(8,128)(2,1)S(1)}, u32[]{:S(2)}) copy-start(bf16[16,4,16,128]{3,2,1,0:T(8,128)(2,1)S(1)} %collective-permute-done.15.refs_2_) | copy-start | bytes 786436
  213.8 15.9 %collective-permute-start.23 = (bf16[16,3,4,16,128]{4,3,2,1,0:T(8,128)(2,1)}, bf16[16,3,4,16,128]{4,3,2,1,0:T(8,128)(2,1)S(1)}, u32[]{:S(2)}, u32[]{:S(2)}) collective-permute-start(bf16[16,3,4,16,128]{4,3,2,1,0:T(8,128)(2,1)} %collective-permute-done.22.refs_1_), channel_id=1, source_target_pairs={{0,8},{8,0},{1,9},{9,1},{2,10},{10,2},{3,11},{11,3},{4,12},{12,4},... | collective-permute-start | bytes 2359304 | tf_op jit(solution)/shard_map/ppermute | solution.py:598
  216.2 13.6 %collective-permute-start.25 = (bf16[16,3,4,16,128]{4,3,2,1,0:T(8,128)(2,1)}, bf16[16,3,4,16,128]{4,3,2,1,0:T(8,128)(2,1)S(1)}, u32[]{:S(2)}, u32[]{:S(2)}) collective-permute-start(bf16[16,3,4,16,128]{4,3,2,1,0:T(8,128)(2,1)} %copy-done.9), channel_id=1, source_target_pairs={{0,8},{8,0},{1,9},{9,1},{2,10},{10,2},{3,11},{11,3},{4,12},{12,4},... | collective-permute-start | bytes 2359304 | tf_op jit(solution)/shard_map/ppermute | solution.py:598
  216.3 2.9 %copy-start.16 = (bf16[16,4,16,128]{3,2,1,0:T(8,128)(2,1)}, bf16[16,4,16,128]{3,2,1,0:T(8,128)(2,1)S(1)}, u32[]{:S(2)}) copy-start(bf16[16,4,16,128]{3,2,1,0:T(8,128)(2,1)S(1)} %collective-permute-done.17.refs_4_) | copy-start | bytes 786436
  216.3 13.5 %collective-permute-start.27 = (bf16[16,3,4,16,128]{4,3,2,1,0:T(8,128)(2,1)}, bf16[16,3,4,16,128]{4,3,2,1,0:T(8,128)(2,1)}, u32[]{:S(2)}, u32[]{:S(2)}) collective-permute-start(bf16[16,3,4,16,128]{4,3,2,1,0:T(8,128)(2,1)} %copy-done.10), channel_id=1, source_target_pairs={{0,8},{8,0},{1,9},{9,1},{2,10},{10,2},{3,11},{11,3},{4,12},{12,4},... | collective-permute-start | bytes 2359304 | tf_op jit(solution)/shard_map/ppermute | solution.py:598
  216.7 2.5 %copy-start.17 = (bf16[16,4,16,128]{3,2,1,0:T(8,128)(2,1)}, bf16[16,4,16,128]{3,2,1,0:T(8,128)(2,1)S(1)}, u32[]{:S(2)}) copy-start(bf16[16,4,16,128]{3,2,1,0:T(8,128)(2,1)S(1)} %collective-permute-done.18.refs_5_) | copy-start | bytes 786436
  216.7 2.5 %collective-permute-start.19 = (bf16[16,4,16,128]{3,2,1,0:T(8,128)(2,1)S(1)}, bf16[16,4,16,128]{3,2,1,0:T(8,128)(2,1)S(1)}, u32[]{:S(2)}, u32[]{:S(2)}) collective-permute-start(bf16[16,4,16,128]{3,2,1,0:T(8,128)(2,1)S(1)} %collective-permute-done.15.refs_2_), channel_id=1, source_target_pairs={{0,8},{8,0},{1,9},{9,1},{2,10},{10,2},{3,11},{11,3},{4,12},{12,4},... | collective-permute-start | bytes 786440 | tf_op jit(solution)/shard_map/ppermute | solution.py:598
  219.9 5.9 %collective-permute-start.20 = (bf16[16,4,16,128]{3,2,1,0:T(8,128)(2,1)}, bf16[16,4,16,128]{3,2,1,0:T(8,128)(2,1)}, u32[]{:S(2)}, u32[]{:S(2)}) collective-permute-start(bf16[16,4,16,128]{3,2,1,0:T(8,128)(2,1)} %collective-permute-done.16.refs_3_), channel_id=1, source_target_pairs={{0,8},{8,0},{1,9},{9,1},{2,10},{10,2},{3,11},{11,3},{4,12},{12,4},... | collective-permute-start | bytes 786440 | tf_op jit(solution)/shard_map/ppermute | solution.py:598
  229.7 1.4 copy-start.5
  (5 other events, 4.3 us)

commit v3 on v2

--- a/solution.py
+++ b/solution.py
@@ -136,11 +136,15 @@
     return jnp.concatenate([kt, kt, extra, zeros], 0).T
 
 
-TQ = 1024
+TQ = 512
 TB = 512
-
-
-def attend_kernel(lengths, qkv, out, mixed, total, kaug, qaug, vaug):
+KB = 512
+
+
+KC = 256
+
+
+def attend_kernel(lengths, qkv, out, mixed, total, kaug, qaug, vaug, one, two):
     for w in range(2):
         kt = gather_rows(qkv, w, 32, 32)
         kaug[...] = key_rows(kt, lengths[w])
@@ -153,21 +157,35 @@
             [gather_rows(qkv, w, 64, 32), jnp.where(row == 0, 1.0, 0.0).astype(BF)], 0
         )
 
-        def tile(t, carry):
+        def scores(t, ref, keys):
+            s = mm(kaug[keys, :], qaug[:, pl.ds(pl.multiple_of(t * TQ, TQ), TQ)])
+            ref[keys, :] = s
+            return jnp.max(s, 0, keepdims=True)
+
+        def tile(t, now, later, peak):
             cols = pl.ds(pl.multiple_of(t * TQ, TQ), TQ)
-            st = mm(kaug[...], qaug[:, cols])
-            peak = jnp.max(st, 0, keepdims=True)
-            p = jnp.exp2(st - peak).astype(BF)
-            o = mm(vaug[...], p)
+            after = lax.rem(t + 1, LENGTH // TQ)
+            next_peak = jnp.full((1, TQ), masked_score, F32)
+            o = jnp.zeros((48, TQ), F32)
+            for c in range(LENGTH // KC):
+                keys = slice(c * KC, (c + 1) * KC)
+                next_peak = jnp.maximum(next_peak, scores(after, later, keys))
+                p = jnp.exp2(now[keys, :] - peak).astype(BF)
+                o = o + mm(vaug[:, keys], p)
             norm = o[32:33]
             ot = o[:32] / norm
             mixed[w, :, cols] = ot
             total[w, :, cols] = peak + jnp.log2(norm)
             for j in range(TQ // 128):
                 out[t * (TQ // 128) + j, w] = ot[:, j * 128 : (j + 1) * 128].astype(BF)
-            return carry
-
-        lax.fori_loop(0, LENGTH // TQ, tile, 0)
+            return next_peak
+
+        peak = scores(0, one, slice(0, LENGTH))
+
+        def pair(k, peak):
+            return tile(2 * k + 1, two, one, tile(2 * k, one, two, peak))
+
+        lax.fori_loop(0, LENGTH // TQ // 2, pair, peak)
 
 
 SMEM = pl.BlockSpec(memory_space=pltpu.SMEM)
@@ -188,6 +206,8 @@
             pltpu.VMEM((LENGTH, 128), BF),
             pltpu.VMEM((128, LENGTH), BF),
             pltpu.VMEM((48, LENGTH), BF),
+            pltpu.VMEM((LENGTH, TQ), F32),
+            pltpu.VMEM((LENGTH, TQ), F32),
         ],
         cost_estimate=cost(1 << 34),
         compiler_params=pltpu.CompilerParams(vmem_limit_bytes=VMEM_LIMIT),
@@ -196,72 +216,76 @@
 
 
 def attend_back_kernel(
-    lengths, qkv, dot_in, mixed, total, cosine, sine, out, kaug, qaug, vaug, doaug, right, dkv
+    lengths, qkv, dot_in, mixed, total, cosine, sine, out, rows, kaug, vaug, keys, dkt, dvt, one, two
 ):
-    for w in range(2):
+    row = lax.broadcasted_iota(jnp.int32, (16, LENGTH), 0)
+
+    def rows_of(*values):
+        block = jnp.zeros((16, LENGTH), F32)
+        for n, v in enumerate(values):
+            block = jnp.where(row == n, v, block)
+        return block.astype(BF)
+
+    def zeros(n):
+        return jnp.zeros((n, LENGTH), BF)
+
+    def window(w, carry):
+        qt = gather_rows(qkv, w, 0, 32)
         kt = gather_rows(qkv, w, 32, 32)
-        kaug[...] = key_rows(kt, lengths[w])
-        qt = gather_rows(qkv, w, 0, 32)
+        do = gather_rows(dot_in, w, 0, 32)
         hi, lo = split2(qt.astype(F32) * score_scale)
-        row = lax.broadcasted_iota(jnp.int32, (16, LENGTH), 0)
-
-        def rows_of(first, second, third, fourth):
-            return jnp.where(
-                row == 0,
-                first,
-                jnp.where(
-                    row == 1, second, jnp.where(row == 2, third, jnp.where(row == 3, fourth, 0.0))
-                ),
-            ).astype(BF)
-
-        l1, l2, l3 = (v.astype(F32) for v in split3(-total[w]))
-        qaug[...] = jnp.concatenate(
-            [hi, lo, rows_of(1.0, l1, l2, l3), jnp.zeros((48, LENGTH), BF)], 0
+        less = [v.astype(F32) for v in split3(-total[w])]
+        delta = jnp.sum(do.astype(F32) * mixed[w], 0, keepdims=True)
+        off = [v.astype(F32) for v in split3(-delta)]
+        rows[...] = jnp.concatenate([hi, lo, rows_of(1.0, *less), do, rows_of(*off)], 0).T
+        place = lax.broadcasted_iota(jnp.int32, (16, LENGTH), 1)
+        mask = jnp.where(place < lengths[w], 0.0, masked_score)
+        kaug[...] = jnp.concatenate([kt, kt, rows_of(mask, 1.0, 1.0, 1.0), zeros(48)], 0)
+        vaug[...] = jnp.concatenate(
+            [zeros(80), gather_rows(qkv, w, 64, 32), rows_of(1.0, 1.0, 1.0)], 0
         )
-        do = gather_rows(dot_in, w, 0, 32)
-        delta = jnp.sum(do.astype(F32) * mixed[w], 0, keepdims=True)
-        d1, d2, d3 = (v.astype(F32) for v in split3(-delta))
-        doaug[...] = jnp.concatenate(
-            [do, rows_of(d1, d2, d3, 0.0), jnp.zeros((80, LENGTH), BF)], 0
-        )
-        vaug[...] = jnp.concatenate(
-            [
-                gather_rows(qkv, w, 64, 32),
-                jnp.where(row < 3, 1.0, 0.0).astype(BF),
-                jnp.zeros((80, LENGTH), BF),
-            ],
-            0,
-        ).T
-        right[...] = jnp.concatenate([qt, do, jnp.zeros((64, LENGTH), BF)], 0).T
-        dkv[...] = jnp.zeros_like(dkv)
-        lane = lax.broadcasted_iota(jnp.int32, (TB, 128), 1)
-
-        def tile(t, carry):
-            cols = pl.ds(pl.multiple_of(t * TB, TB), TB)
-            st = mm(kaug[...], qaug[:, cols])
-            probs = jnp.exp2(st)
-            ds = (probs * mm(vaug[...], doaug[:, cols])).astype(BF)
-            both = jnp.concatenate([ds, probs.astype(BF)], 1)
-            r = right[cols, :]
-            zero = jnp.zeros_like(r)
-            pair = jnp.concatenate(
-                [jnp.where(lane < 32, r, zero), jnp.where(lane < 32, zero, r)], 0
-            )
-            dkv[...] += mm(both, pair)
-            dq = mm(kt, ds) * inv_root
-            dq = rotate(dq, cosine[:, cols], -sine[:, cols])
-            dq = dq.astype(BF)
-            for j in range(TB // 128):
-                out[t * (TB // 128) + j, w, 0:32, :] = dq[:, j * 128 : (j + 1) * 128]
-            return carry
-
-        lax.fori_loop(0, LENGTH // TB, tile, 0)
-        back = dkv[...].T
-        dk = rotate(back[:32] * inv_root, cosine[...], -sine[...]).astype(BF)
-        dv = back[32:64].astype(BF)
+        keys[...] = jnp.concatenate([kt, zeros(96)], 0).T
+        dkt[...] = jnp.zeros_like(dkt)
+        dvt[...] = jnp.zeros_like(dvt)
+
+        def weights(t, ref, at):
+            r = rows[t * TB : (t + 1) * TB, :]
+            probs = jnp.exp2(mm(r, kaug[:, at]))
+            ref[0, :, at] = (probs * mm(r, vaug[:, at])).astype(BF)
+            ref[1, :, at] = probs.astype(BF)
+
+        def tile(t, now, later):
+            blocks = range(t * (TB // 128), (t + 1) * (TB // 128))
+            q = jnp.concatenate([qkv[j, w, 0:32, :] for j in blocks], 1)
+            do_t = jnp.concatenate([dot_in[j, w] for j in blocks], 1)
+            dq = jnp.zeros((TB, 128), F32)
+            for c in range(LENGTH // KB):
+                at = slice(c * KB, (c + 1) * KB)
+                if later is not None:
+                    weights(t + 1, later, at)
+                ds = now[0, :, at]
+                dq = dq + mm(ds, keys[at, :])
+                dkt[:, at] += mm(q, ds)
+                dvt[:, at] += mm(do_t, now[1, :, at])
+            cols = slice(t * TB, (t + 1) * TB)
+            dq = rotate((dq * inv_root).T[:32], cosine[:, cols], -sine[:, cols])
+            for j, s in enumerate(blocks):
+                out[s, w, 0:32, :] = dq[:, j * 128 : (j + 1) * 128].astype(BF)
+
+        tiles = LENGTH // TB
+        for c in range(LENGTH // KB):
+            weights(0, one, slice(c * KB, (c + 1) * KB))
+        for t in range(tiles):
+            now, later = ((one, two), (two, one))[t % 2]
+            tile(t, now, later if t + 1 < tiles else None)
+        dk = rotate(dkt[...] * inv_root, cosine[...], -sine[...]).astype(BF)
+        dv = dvt[...].astype(BF)
         for s in range(HEADS):
             out[s, w, 32:64, :] = dk[:, s * 128 : (s + 1) * 128]
             out[s, w, 64:96, :] = dv[:, s * 128 : (s + 1) * 128]
+        return carry
+
+    lax.fori_loop(0, 2, window, 0)
 
 
 def attend_back_call(lengths, qkv, do, mixed, total, cos, sin):
@@ -273,10 +297,12 @@
         scratch_shapes=[
             pltpu.VMEM((LENGTH, 128), BF),
             pltpu.VMEM((128, LENGTH), BF),
-            pltpu.VMEM((LENGTH, 128), BF),
             pltpu.VMEM((128, LENGTH), BF),
             pltpu.VMEM((LENGTH, 128), BF),
-            pltpu.VMEM((LENGTH, 128), F32),
+            pltpu.VMEM((HEAD_DIM, LENGTH), F32),
+            pltpu.VMEM((HEAD_DIM, LENGTH), F32),
+            pltpu.VMEM((2, TB, LENGTH), BF),
+            pltpu.VMEM((2, TB, LENGTH), BF),
         ],
         cost_estimate=cost(1 << 34),
         compiler_params=pltpu.CompilerParams(vmem_limit_bytes=VMEM_LIMIT),
@@ -465,80 +491,78 @@
     )(place, tok, dres, dqkv, wq, wk, wv, gain, bias, gwout, vecs)
 
 
-def put_pieces(number, core, refs, write):
-    for d, ref in enumerate(refs):
-        write(ref, core, pl.multiple_of((y_of(number) + 4 - d) % 4 * 64, 64))
-
-
-def wide_rows(ref, n, out, start):
+def unpack_ff_kernel(place, *refs):
+    pieces = refs[:8]
+    gwg, gwu, gwd, parts, arrived = refs[8:]
+    step = pl.program_id(0)
+    copies = [
+        pltpu.make_async_copy(piece, parts.at[k], arrived.at[k]) for k, piece in enumerate(pieces)
+    ]
+
+    @pl.when(step == 0)
+    def begin():
+        for copy in copies:
+            copy.start()
+
+    for k, copy in enumerate(copies):
+        pl.when(step == k)(copy.wait)
     for j in range(4):
-        rows = pl.ds(start + j * 16, 16)
-        for i in range(4):
-            for l in range(4):
+        rows = slice(j * 16, j * 16 + 16)
+        for l in range(4):
+            for i in range(4):
                 lo = i * 512 + l * 128
-                out[0, rows, lo : lo + 128] = ref[4 * j + l, n, i].astype(F32)
-
-
-def unpack_ff_kernel(place, *refs):
-    gwg, gwu, gwd = refs[-3:]
-    number = place[0]
-
-    def write(ref, core, start):
-        wide_rows(ref, 0, gwg, start)
-        wide_rows(ref, 1, gwu, start)
-        for j in range(4):
-            rows = pl.ds(start + j * 16, 16)
-            for i in range(4):
-                for l in range(4):
-                    gwd[i, 0, rows, l * 128 : (l + 1) * 128] = ref[4 * j + l, 2, i].astype(F32)
-
-    put_pieces(number, None, refs[:4], write)
-
-
-def unpack_ff_call(place, pieces, other, before):
+                gwg[0, rows, lo : lo + 128] = parts[step, 4 * j + l, 0, i].astype(F32)
+                gwu[0, rows, lo : lo + 128] = parts[step, 4 * j + l, 1, i].astype(F32)
+                gwd[i, 0, rows, l * 128 : (l + 1) * 128] = parts[step, 4 * j + l, 2, i].astype(F32)
+
+
+def unpack_ff_call(place, pieces):
     def spec(block, axis):
-        def index(i, p):
+        def index(k, p):
             at = [0] * len(block)
-            at[axis] = (core_of(p[0]) + other) % 2
+            at[axis] = (core_of(p[0]) + k // 4) % 2 * 4 + (y_of(p[0]) + 4 - k % 4) % 4
             return tuple(at)
 
         return pl.BlockSpec(block, index)
 
-    shapes = ((2, 256, 2048), (2, 256, 2048), (4, 2, 256, 512))
     return pl.pallas_call(
         unpack_ff_kernel,
         grid_spec=pltpu.PrefetchScalarGridSpec(
             num_scalar_prefetch=1,
-            grid=(1,),
-            in_specs=[whole(*pieces[0].shape)] * 4
-            + [pl.BlockSpec(memory_space=pl.ANY)] * len(before),
+            grid=(8,),
+            in_specs=[pl.BlockSpec(memory_space=pl.ANY)] * 8,
             out_specs=(
-                spec((1, 256, 2048), 0),
-                spec((1, 256, 2048), 0),
-                spec((4, 1, 256, 512), 1),
+                spec((1, 64, 2048), 0),
+                spec((1, 64, 2048), 0),
+                spec((4, 1, 64, 512), 1),
             ),
+            scratch_shapes=[
+                pltpu.VMEM((8,) + pieces[0].shape, BF),
+                pltpu.SemaphoreType.DMA((8,)),
+            ],
         ),
-        out_shape=tuple(jax.ShapeDtypeStruct(shape, F32) for shape in shapes),
-        input_output_aliases={5 + k: k for k in range(3)} if before else {},
-        cost_estimate=cost(1 << 20, 9 << 20),
+        out_shape=(
+            jax.ShapeDtypeStruct((8, 64, 2048), F32),
+            jax.ShapeDtypeStruct((8, 64, 2048), F32),
+            jax.ShapeDtypeStruct((4, 8, 64, 512), F32),
+        ),
+        cost_estimate=cost(1 << 20, 18 << 20),
         compiler_params=pltpu.CompilerParams(vmem_limit_bytes=VMEM_LIMIT),
         name="unpack_feed_forward",
-    )(place, *pieces, *before)
+    )(place, *pieces)
 
 
 def unpack_kernel(place, *refs):
     outs = refs[-4:]
-    number = place[0]
-
-    def write(ref, core, start):
-        for n, g in enumerate(outs):
-            for j in range(4):
-                rows = pl.ds(pl.multiple_of(core * 256 + start + j * 16, 16), 16)
-                for l in range(4):
-                    g[rows, l * 128 : (l + 1) * 128] = ref[4 * j + l, n].astype(F32)
-
-    put_pieces(number, core_of(number), refs[:4], write)
-    put_pieces(number, 1 - core_of(number), refs[4:8], write)
+    core, y = core_of(place[0]), y_of(place[0])
+    for d in range(4):
+        start = (y + 4 - d) % 4 * 64
+        for ref, c in ((refs[d], core), (refs[4 + d], 1 - core)):
+            for n, g in enumerate(outs):
+                for j in range(4):
+                    rows = pl.ds(pl.multiple_of(c * 256 + start + j * 16, 16), 16)
+                    for l in range(4):
+                        g[rows, l * 128 : (l + 1) * 128] = ref[4 * j + l, n].astype(F32)
 
 
 def unpack_call(place, mine, others):
@@ -563,7 +587,7 @@
 
 SEQ = ("x", "zh", "c")
 WIN = ("y", "zl")
-REST = ("x", "zh", "zl")
+REST = ("zl", "zh", "x")
 SWAP = [(0, 1), (1, 0)]
 
 
@@ -630,7 +654,7 @@
     )
     ff = spread(ff, REST, 16)
     mine, others = collect(ff)
-    gwg, gwu, gwd = unpack_ff_call(place, others, 1, unpack_ff_call(place, mine, 0, ()))
+    gwg, gwu, gwd = unpack_ff_call(place, mine + others)
     part = reduce_rest(after(reduce_y(pieces), ff))
     four = part[4].reshape(4, 4, 128).transpose(1, 0, 2).reshape(4, width).astype(F32)
     gwq, gwk, gwv, gwout = unpack_call(place, *collect(spread(part[:4], REST, 16)))

time: 237 us -> 225 us (0.949)
  Pallas kernels: 73.1 us -> 62 us
    pallas_call x1, Pallas kernels: 25.2 us -> 20.4 us  [attend_back_call(): pl.pallas_call(attend_back_kernel, out_shape=jax.ShapeDtypeStruct((HEADS,...]
    pallas_call x2 -> x1, Pallas kernels: 9.88 us -> 6.66 us  [unpack_ff_call(): pl.pallas_call(unpack_ff_kernel, grid_spec=pltpu.PrefetchScalarGridSpec(n...]
    pallas_call x1, Pallas kernels: 13.9 us -> 10.9 us  [attend_call(): pl.pallas_call(attend_kernel, out_shape=(jax.ShapeDtypeStruct((HEADS, 2,...]
  transfers between devices with their start and end apart: 33 -> 33, of which waited for: 7 -> 9; matrix products, arithmetic and copies ran while one was open for 6% -> 6% of each run, Pallas kernels for 17% -> 13%
where the time goes in v3:
time: 225 us; the launch traced here: 224 us
  starting transfers between devices  66 us (29%)
  Pallas kernels  62 us (28%)
  blocking collectives  47.2 us (21%)
  waiting for transfers between devices  31.9 us (14%)
  other arithmetic  12.6 us (6%)
  local copies, waits for them, and re-layouts  3.17 us (1%)
    all_to_all x3, blocking collectives, exchange(): return lax.all_to_all(x, axes, 0, 0, tiled=True)  47.2 us
    all_to_all x5, starting transfers between devices, exchange(): return lax.all_to_all(x, axes, 0, 0, tiled=True)  27 us
    all_to_all x5, waiting for transfers between devices, exchange(): return lax.all_to_all(x, axes, 0, 0, tiled=True)  26.1 us
    ppermute x12, starting transfers between devices, along_y(): return lax.ppermute(x, 'y', [(i, (i + d) % 4) for i in range(4)])  23.3 us
    pallas_call x1, Pallas kernels, attend_back_call(): pl.pallas_call(attend_back_kernel, out_shape=jax.ShapeDtypeStruct((HEADS,...  20.4 us
    ppermute x8, starting transfers between devices, collect(): return (mine, [lax.ppermute(m, 'c', SWAP) for m in mine])  12.6 us
    convert_element_type x8, other arithmetic, add_up(): return sum((t.astype(F32) for t in terms)).astype(BF)  12.4 us
    pallas_call x1, Pallas kernels, ff_call(): pl.pallas_call(ff_kernel, grid_spec=pltpu.PrefetchScalarGridSpec(num_scal...  11.9 us
  transfers between devices with their start and end apart: 33, of which 9 were waited for; matrix products, arithmetic and copies ran while one was open for 6% of the time, Pallas kernels for 13%

profile of v3, /device:TPU:1, one launch (start us, length us, event | category | flops | bytes accessed | tf_op | source)
XLA Modules:
  0.0 224.0 jit_solution(14158886877740235831)
XLA Ops:
  0.7 3.2 %qkv_forward.1 = bf16[16,2,96,128]{3,2,1,0:T(8,128)(2,1)} custom-call(s32[1]{0:T(128)} %bitcast.place, bf16[256,512]{1,0:T(8,128)(2,1)} %bitcast.21, f32[1,512]{1,0:T(1,128)} %bitcast.25, f32[1,512]{1,0:T(1,128)} %bitcast.27, bf16[512,512]{1,0:T(8,128)(2,1)} %wq.3, bf16[512,512]{1,0:T(8,128)(2,1)} %wk.3, bf16[512,512]{1,0:T(8,128)(2,1)} %wv.3, ...), custom_call_target="tpu_custom_call" | custom-call | flops 402653184 | bytes 1048576 | tf_op jit(solution)/shard_map/qkv_forward/pallas_call | solution.py:96
  3.9 23.7 %all_to_all.40.qkv = bf16[16,2,96,128]{3,2,1,0:T(8,128)(2,1)} all-to-all(bf16[16,2,96,128]{3,2,1,0:T(8,128)(2,1)} %qkv_forward.1), channel_id=1, replica_groups=mesh['x'=4,'zh'=2,'c'=2,'y'=4,'zl'=2] {'x','zh','c'}, dimensions={0} | all-to-all | bytes 1572864 | tf_op jit(solution)/shard_map/all_to_all | solution.py:595
  27.6 10.9 %attend_forward.1 = (bf16[16,2,32,128]{3,2,1,0:T(8,128)(2,1)}, f32[2,32,2048]{2,1,0:T(8,128)}, f32[2,1,2048]{2,1,0:T(1,128)}) custom-call(s32[2]{0:T(128)} %lengths.3, bf16[16,2,96,128]{3,2,1,0:T(8,128)(2,1)} %all_to_all.40.qkv), custom_call_target="tpu_custom_call" | custom-call | flops 17179869184 | bytes 1048576 | tf_op jit(solution)/shard_map/attend_forward/pallas_call | solution.py:196
  38.5 13.4 %all_to_all.41.ob = bf16[16,2,32,128]{3,2,1,0:T(8,128)(2,1)} all-to-all(bf16[16,2,32,128]{3,2,1,0:T(8,128)(2,1)} %get-tuple-element.47), channel_id=1, replica_groups=mesh['x'=4,'zh'=2,'c'=2,'y'=4,'zl'=2] {'x','zh','c'}, dimensions={0} | all-to-all | bytes 524288 | tf_op jit(solution)/shard_map/all_to_all | solution.py:595
  51.9 11.9 %feed_forward.1 = (f32[256,512]{1,0:T(8,128)}, bf16[16,3,4,16,128]{4,3,2,1,0:T(8,128)(2,1)}, bf16[16,3,4,16,128]{4,3,2,1,0:T(8,128)(2,1)}, bf16[16,3,4,16,128]{4...) custom-call(s32[1]{0:T(128)} %bitcast.place, ...), custom_call_target="tpu_custom_call" | custom-call | flops 4831838208 | bytes 1048576 | tf_op jit(solution)/shard_map/feed_forward/pallas_call | solution.py:402
  63.8 0.5 collective-permute-start.8
  64.9 3.7 %all-to-all-start.2 = ((bf16[16,2,32,128]{3,2,1,0:T(8,128)(2,1)}), bf16[16,2,32,128]{3,2,1,0:T(8,128)(2,1)S(1)}, u32[]{:S(2)}, u32[]{:S(2)}) async-start(bf16[16,2,32,128]{3,2,1,0:T(8,128)(2,1)} %get-tuple-element.50), calls=%async_computation.2 | async-start | bytes 524288 | tf_op jit(solution)/shard_map/all_to_all | solution.py:595
  68.7 2.3 %add_convert_fusion.3 = bf16[16,3,4,16,128]{4,3,2,1,0:T(8,128)(2,1)} fusion(bf16[16,3,4,16,128]{4,3,2,1,0:T(8,128)(2,1)S(1)} %collective-permute-done.8, bf16[16,3,4,16,128]{4,3,2,1,0:T(8,128)(2,1)} %get-tuple-element.66), kind=kLoop, calls=%fused_computation.3 | loop fusion | flops 1572864 | bytes 2359296 | tf_op jit(solution)/shard_map/convert_element_type | solution.py:603
  71.0 1.3 collective-permute-start.9
  72.3 2.3 %add_convert_fusion.2 = bf16[16,3,4,16,128]{4,3,2,1,0:T(8,128)(2,1)} fusion(bf16[16,3,4,16,128]{4,3,2,1,0:T(8,128)(2,1)} %collective-permute-done.10, bf16[16,3,4,16,128]{4,3,2,1,0:T(8,128)(2,1)S(1)} %copy-done.8), kind=kLoop, calls=%fused_computation.2 | loop fusion | flops 1572864 | bytes 2359296 | tf_op jit(solution)/shard_map/convert_element_type | solution.py:603
  74.6 2.6 %collective-permute-start.11 = (bf16[16,3,4,16,128]{4,3,2,1,0:T(8,128)(2,1)}, bf16[16,3,4,16,128]{4,3,2,1,0:T(8,128)(2,1)}, u32[]{:S(2)}, u32[]{:S(2)}) collective-permute-start(bf16[16,3,4,16,128]{4,3,2,1,0:T(8,128)(2,1)} %add_convert_fusion.2), channel_id=1, source_target_pairs={{0,4},{2,6},{4,0},{6,2},{1,5},{3,7},{5,1},{7,3},{8,12},{10,14},{12... | collective-permute-start | bytes 2359304 | tf_op jit(solution)/shard_map/ppermute | solution.py:607
  77.2 1.2 add_convert_fusion.1
  78.4 1.1 collective-permute-start.13
  79.5 0.7 copy-done.17
  80.2 20.4 %attend_backward.1 = bf16[16,2,96,128]{3,2,1,0:T(8,128)(2,1)} custom-call(s32[2]{0:T(128)} %lengths.3, bf16[16,2,96,128]{3,2,1,0:T(8,128)(2,1)} %all_to_all.40.qkv, bf16[16,2,32,128]{3,2,1,0:T(8,128)(2,1)} %copy-done.17, f32[2,32,2048]{2,1,0:T(8,128)} %get-tuple-element.51.mixed, f32[2,1,2048]{2,1,0:T(1,128)} %get-tuple-element.52.total, ...), custom_call_target="tpu_custom_call" | custom-call | flops 17179869184 | bytes 1048576 | tf_op jit(solution)/shard_map/attend_backward/pallas_call | solution.py:292
  100.5 8.3 %all-to-all-start.3 = ((bf16[16,2,96,128]{3,2,1,0:T(8,128)(2,1)}), bf16[16,2,96,128]{3,2,1,0:T(8,128)(2,1)S(1)}, u32[]{:S(2)}, u32[]{:S(2)}) async-start(bf16[16,2,96,128]{3,2,1,0:T(8,128)(2,1)} %attend_backward.1), calls=%async_computation.3 | async-start | bytes 1572864 | tf_op jit(solution)/shard_map/all_to_all | solution.py:595
  108.8 0.7 collective-permute-done.11
  109.5 1.6 collective-permute-done.13
  111.2 3.0 %add_convert_fusion = bf16[16,3,4,16,128]{4,3,2,1,0:T(8,128)(2,1)} fusion(bf16[16,3,4,16,128]{4,3,2,1,0:T(8,128)(2,1)} %collective-permute-done.13, bf16[16,3,4,16,128]{4,3,2,1,0:T(8,128)(2,1)} %collective-permute-done.11, bf16[16,3,4,16,128]{4,3,2,1,0:T(8,128)(2,1)S(1)} %collective-permute-done.9, bf16[16,3,4,16,128]{4,3,2,1,0:T(8,128)(2,1)S(1)} %collective-permute-done.7, ...), kind=kLoop, calls=%fused_computation | loop fusion | flops 3932160 | bytes 4718592 | tf_op jit(solution)/shard_map/convert_element_type | solution.py:603
  114.2 8.8 %all-to-all-done.3.dqkv = bf16[16,2,96,128]{3,2,1,0:T(8,128)(2,1)S(1)} async-done(((bf16[16,2,96,128]{3,2,1,0:T(8,128)(2,1)}), bf16[16,2,96,128]{3,2,1,0:T(8,128)(2,1)S(1)}, u32[]{:S(2)}, u32[]{:S(2)}) %all-to-all-start.3) | async-done | bytes 786464 | tf_op jit(solution)/shard_map/all_to_all | solution.py:595
  123.0 3.6 %all-to-all-start.4 = ((bf16[16,3,4,16,128]{4,3,2,1,0:T(8,128)(2,1)}), bf16[16,3,4,16,128]{4,3,2,1,0:T(8,128)(2,1)S(1)}, u32[]{:S(2)}, u32[]{:S(2)}) async-start(bf16[16,3,4,16,128]{4,3,2,1,0:T(8,128)(2,1)} %add_convert_fusion), calls=%async_computation.4 | async-start | bytes 1572864 | tf_op jit(solution)/shard_map/all_to_all | solution.py:595
  126.6 5.2 %projection_backward.1 = (f32[256,512]{1,0:T(8,128)}, bf16[16,5,16,128]{3,2,1,0:T(8,128)(2,1)}, bf16[16,5,16,128]{3,2,1,0:T(8,128)(2,1)}, bf16[16,5,16,128]{3,2,...) custom-call(s32[1]{0:T(128)} %bitcast.place, ...), custom_call_target="tpu_custom_call" | custom-call | flops 805306368 | bytes 1048576 | tf_op jit(solution)/shard_map/projection_backward/pallas_call | solution.py:482
  131.8 1.1 collective-permute-start.1
  133.7 0.6 collective-permute-done.1
  134.3 1.1 add_convert_fusion.7
  135.9 4.2 %all-to-all-done.4 = bf16[16,3,4,16,128]{4,3,2,1,0:T(8,128)(2,1)S(1)} async-done(((bf16[16,3,4,16,128]{4,3,2,1,0:T(8,128)(2,1)}), bf16[16,3,4,16,128]{4,3,2,1,0:T(8,128)(2,1)S(1)}, u32[]{:S(2)}, u32[]{:S(2)}) %all-to-all-start.4) | async-done | bytes 786464 | tf_op jit(solution)/shard_map/all_to_all | solution.py:595
  140.3 1.1 broadcast_in_dim.4
  141.3 3.6 %all-to-all-start.5 = ((bf16[16,3,4,16,128]{4,3,2,1,0:T(8,128)(2,1)}), bf16[16,3,4,16,128]{4,3,2,1,0:T(8,128)(2,1)S(1)}, u32[]{:S(2)}, u32[]{:S(2)}) async-start(bf16[16,3,4,16,128]{4,3,2,1,0:T(8,128)(2,1)} %broadcast_in_dim.4), calls=%async_computation.5 | async-start | bytes 1572864 | tf_op jit(solution)/shard_map/all_to_all | solution.py:595
  145.3 2.8 %collective-permute-start.6 = (bf16[16,5,16,128]{3,2,1,0:T(8,128)(2,1)S(1)}, bf16[16,5,16,128]{3,2,1,0:T(8,128)(2,1)}, u32[]{:S(2)}, u32[]{:S(2)}) collective-permute-start(bf16[16,5,16,128]{3,2,1,0:T(8,128)(2,1)S(1)} %add_convert_fusion.5), channel_id=1, source_target_pairs={{0,6},{2,0},{4,2},{6,4},{1,7},{3,1},{5,3},{7,5},{8,14},{10,8},{12,... | collective-permute-start | bytes 983048 | tf_op jit(solution)/shard_map/ppermute | solution.py:607
  148.1 9.2 %all-to-all-done.5.refs_0_ = bf16[16,3,4,16,128]{4,3,2,1,0:T(8,128)(2,1)S(1)} async-done(((bf16[16,3,4,16,128]{4,3,2,1,0:T(8,128)(2,1)}), bf16[16,3,4,16,128]{4,3,2,1,0:T(8,128)(2,1)S(1)}, u32[]{:S(2)}, u32[]{:S(2)}) %all-to-all-start.5) | async-done | bytes 786464 | tf_op jit(solution)/shard_map/all_to_all | solution.py:595
  157.7 3.4 %collective-permute-start.22 = (bf16[16,3,4,16,128]{4,3,2,1,0:T(8,128)(2,1)S(1)}, bf16[16,3,4,16,128]{4,3,2,1,0:T(8,128)(2,1)S(1)}, u32[]{:S(2)}, u32[]{:S(2)}) collective-permute-start(bf16[16,3,4,16,128]{4,3,2,1,0:T(8,128)(2,1)S(1)} %all-to-all-done.5.refs_0_), channel_id=1, source_target_pairs={{0,4},{2,6},{4,0},{6,2},{1,5},{3,7},{5,1},{7,3},{8,12},{10,14},{12... | collective-permute-start | bytes 2359304 | tf_op jit(solution)/shard_map/ppermute | solution.py:607
  161.2 2.3 %add_convert_fusion.4 = bf16[16,5,16,128]{3,2,1,0:T(8,128)(2,1)} fusion(bf16[16,5,16,128]{3,2,1,0:T(8,128)(2,1)} %collective-permute-done.6, bf16[16,5,16,128]{3,2,1,0:T(8,128)(2,1)} %collective-permute-done.4, bf16[16,5,16,128]{3,2,1,0:T(8,128)(2,1)} %collective-permute-done.2, bf16[16,5,16,128]{3,2,1,0:T(8,128)(2,1)} %collective-permute-done, ...), kind=kLoop, calls=%fused_computation.4 | loop fusion | flops 1638400 | bytes 1966080 | tf_op jit(solution)/shard_map/convert_element_type | solution.py:603
  163.5 7.8 %all-to-all-start.6 = ((bf16[16,5,16,128]{3,2,1,0:T(8,128)(2,1)}), bf16[16,5,16,128]{3,2,1,0:T(8,128)(2,1)S(1)}, u32[]{:S(2)}, u32[]{:S(2)}) async-start(bf16[16,5,16,128]{3,2,1,0:T(8,128)(2,1)} %add_convert_fusion.4), calls=%async_computation.6 | async-start | bytes 655360 | tf_op jit(solution)/shard_map/all_to_all | solution.py:595
  171.2 4.1 %collective-permute-start.23 = (bf16[16,3,4,16,128]{4,3,2,1,0:T(8,128)(2,1)S(1)}, bf16[16,3,4,16,128]{4,3,2,1,0:T(8,128)(2,1)S(1)}, u32[]{:S(2)}, u32[]{:S(2)}) collective-permute-start(bf16[16,3,4,16,128]{4,3,2,1,0:T(8,128)(2,1)S(1)} %all-to-all-done.5.refs_0_), channel_id=1, source_target_pairs={{0,6},{2,0},{4,2},{6,4},{1,7},{3,1},{5,3},{7,5},{8,14},{10,8},{12,... | collective-permute-start | bytes 2359304 | tf_op jit(solution)/shard_map/ppermute | solution.py:607
  175.3 3.9 %all-to-all-done.6 = bf16[16,5,16,128]{3,2,1,0:T(8,128)(2,1)S(1)} async-done(((bf16[16,5,16,128]{3,2,1,0:T(8,128)(2,1)}), bf16[16,5,16,128]{3,2,1,0:T(8,128)(2,1)S(1)}, u32[]{:S(2)}, u32[]{:S(2)}) %all-to-all-start.6) | async-done | bytes 327712 | tf_op jit(solution)/shard_map/all_to_all | solution.py:595
  179.3 10.1 %all_to_all.42.refs_0_ = bf16[16,4,16,128]{3,2,1,0:T(8,128)(2,1)S(1)} all-to-all(bf16[16,4,16,128]{3,2,1,0:T(8,128)(2,1)S(1)} %broadcast_in_dim.5), channel_id=1, replica_groups=mesh['x'=4,'zh'=2,'c'=2,'y'=4,'zl'=2] {'zl','zh','x'}, dimensions={0} | all-to-all | bytes 524288 | tf_op jit(solution)/shard_map/all_to_all | solution.py:595
  189.5 4.7 %collective-permute-start.14 = (bf16[16,4,16,128]{3,2,1,0:T(8,128)(2,1)S(1)}, bf16[16,4,16,128]{3,2,1,0:T(8,128)(2,1)S(1)}, u32[]{:S(2)}, u32[]{:S(2)}) collective-permute-start(bf16[16,4,16,128]{3,2,1,0:T(8,128)(2,1)S(1)} %all_to_all.42.refs_0_), channel_id=1, source_target_pairs={{0,2},{2,4},{4,6},{6,0},{1,3},{3,5},{5,7},{7,1},{8,10},{10,12},{12... | collective-permute-start | bytes 786440 | tf_op jit(solution)/shard_map/ppermute | solution.py:607
  194.1 1.2 collective-permute-start.15
  195.4 1.2 collective-permute-start.16
  196.5 3.6 %collective-permute-start.17 = (bf16[16,4,16,128]{3,2,1,0:T(8,128)(2,1)S(1)}, bf16[16,4,16,128]{3,2,1,0:T(8,128)(2,1)S(1)}, u32[]{:S(2)}, u32[]{:S(2)}) collective-permute-start(bf16[16,4,16,128]{3,2,1,0:T(8,128)(2,1)S(1)} %all_to_all.42.refs_0_), channel_id=1, source_target_pairs={{0,8},{8,0},{1,9},{9,1},{2,10},{10,2},{3,11},{11,3},{4,12},{12,4},... | collective-permute-start | bytes 786440 | tf_op jit(solution)/shard_map/ppermute | solution.py:622
  200.2 4.7 %collective-permute-start.18 = (bf16[16,4,16,128]{3,2,1,0:T(8,128)(2,1)S(1)}, bf16[16,4,16,128]{3,2,1,0:T(8,128)(2,1)S(1)}, u32[]{:S(2)}, u32[]{:S(2)}) collective-permute-start(bf16[16,4,16,128]{3,2,1,0:T(8,128)(2,1)S(1)} %collective-permute-done.14.refs_1_), channel_id=1, source_target_pairs={{0,8},{8,0},{1,9},{9,1},{2,10},{10,2},{3,11},{11,3},{4,12},{12,4},... | collective-permute-start | bytes 786440 | tf_op jit(solution)/shard_map/ppermute | solution.py:622
  205.0 3.2 %collective-permute-start.25 = (bf16[16,3,4,16,128]{4,3,2,1,0:T(8,128)(2,1)S(1)}, bf16[16,3,4,16,128]{4,3,2,1,0:T(8,128)(2,1)}, u32[]{:S(2)}, u32[]{:S(2)}) collective-permute-start(bf16[16,3,4,16,128]{4,3,2,1,0:T(8,128)(2,1)S(1)} %collective-permute-done.21.refs_1_), channel_id=1, source_target_pairs={{0,8},{8,0},{1,9},{9,1},{2,10},{10,2},{3,11},{11,3},{4,12},{12,4},... | collective-permute-start | bytes 2359304 | tf_op jit(solution)/shard_map/ppermute | solution.py:622
  208.9 2.0 collective-permute-done.19.refs_6_
  210.9 0.7 copy-done.16
  212.0 0.6 fusion
  212.6 0.7 collective-permute-done.20.refs_7_
  213.3 3.8 %unpack_projections.1 = (f32[512,512]{1,0:T(8,128)}, f32[512,512]{1,0:T(8,128)}, f32[512,512]{1,0:T(8,128)}, f32[512,512]{1,0:T(8,128)}) custom-call(s32[1]{0:T(128)} %bitcast.place, bf16[16,4,16,128]{3,2,1,0:T(8,128)(2,1)} %copy-done.2, bf16[16,4,16,128]{3,2,1,0:T(8,128)(2,1)} %copy-done.11, bf16[16,4,16,128]{3,2,1,0:T(8,128)(2,1)} %copy-done.12, ...), custom_call_target="tpu_custom_call" | custom-call | flops 1048576 | bytes 6291456 | tf_op jit(solution)/shard_map/unpack_projections/pallas_call | solution.py:570
  217.2 6.7 %unpack_feed_forward.1 = (f32[8,64,2048]{2,1,0:T(8,128)}, f32[8,64,2048]{2,1,0:T(8,128)}, f32[4,8,64,512]{3,2,1,0:T(8,128)}) custom-call(s32[1]{0:T(128)} %bitcast.place, bf16[16,3,4,16,128]{4,3,2,1,0:T(8,128)(2,1)} %copy-done, bf16[16,3,4,16,128]{4,3,2,1,0:T(8,128)(2,1)} %copy-done.3, bf16[16,3,4,16,128]{4,3,2,1,0:T(8,128)(2,1)} %copy-done.4, ...), custom_call_target="tpu_custom_call" | custom-call | flops 1048576 | bytes 18874368 | tf_op jit(solution)/shard_map/unpack_feed_forward/pallas_call | solution.py:528
  (79 shorter events, 4.1 us)
Async XLA Ops:
  63.8 8.5 %copy-start.8 = (bf16[16,3,4,16,128]{4,3,2,1,0:T(8,128)(2,1)S(1)}, bf16[16,3,4,16,128]{4,3,2,1,0:T(8,128)(2,1)}, u32[]{:S(2)}) copy-start(bf16[16,3,4,16,128]{4,3,2,1,0:T(8,128)(2,1)} %get-tuple-element.68) | copy-start | bytes 2359300
  63.8 4.8 %collective-permute-start.8 = (bf16[16,3,4,16,128]{4,3,2,1,0:T(8,128)(2,1)}, bf16[16,3,4,16,128]{4,3,2,1,0:T(8,128)(2,1)S(1)}, u32[]{:S(2)}, u32[]{:S(2)}) collective-permute-start(bf16[16,3,4,16,128]{4,3,2,1,0:T(8,128)(2,1)} %get-tuple-element.67), channel_id=1, source_target_pairs={{0,8},{8,0},{1,9},{9,1},{2,10},{10,2},{3,11},{11,3},{4,12},{12,4},... | collective-permute-start | bytes 2359304 | tf_op jit(solution)/shard_map/ppermute | solution.py:611
  64.3 8.0 %collective-permute-start.10 = (bf16[16,3,4,16,128]{4,3,2,1,0:T(8,128)(2,1)}, bf16[16,3,4,16,128]{4,3,2,1,0:T(8,128)(2,1)}, u32[]{:S(2)}, u32[]{:S(2)}) collective-permute-start(bf16[16,3,4,16,128]{4,3,2,1,0:T(8,128)(2,1)} %get-tuple-element.69), channel_id=1, source_target_pairs={{0,8},{8,0},{1,9},{9,1},{2,10},{10,2},{3,11},{11,3},{4,12},{12,4},... | collective-permute-start | bytes 2359304 | tf_op jit(solution)/shard_map/ppermute | solution.py:611
  64.4 12.8 %collective-permute-start.12 = (bf16[16,3,4,16,128]{4,3,2,1,0:T(8,128)(2,1)}, bf16[16,3,4,16,128]{4,3,2,1,0:T(8,128)(2,1)S(1)}, u32[]{:S(2)}, u32[]{:S(2)}) collective-permute-start(bf16[16,3,4,16,128]{4,3,2,1,0:T(8,128)(2,1)} %get-tuple-element.71), channel_id=1, source_target_pairs={{0,8},{8,0},{1,9},{9,1},{2,10},{10,2},{3,11},{11,3},{4,12},{12,4},... | collective-permute-start | bytes 2359304 | tf_op jit(solution)/shard_map/ppermute | solution.py:611
  64.8 44.0 %collective-permute-start.7 = (bf16[16,3,4,16,128]{4,3,2,1,0:T(8,128)(2,1)}, bf16[16,3,4,16,128]{4,3,2,1,0:T(8,128)(2,1)S(1)}, u32[]{:S(2)}, u32[]{:S(2)}) collective-permute-start(bf16[16,3,4,16,128]{4,3,2,1,0:T(8,128)(2,1)} %get-tuple-element.65), channel_id=1, source_target_pairs={{0,8},{8,0},{1,9},{9,1},{2,10},{10,2},{3,11},{11,3},{4,12},{12,4},... | collective-permute-start | bytes 2359304 | tf_op jit(solution)/shard_map/ppermute | solution.py:611
  64.9 14.5 %all-to-all-start.2 = ((bf16[16,2,32,128]{3,2,1,0:T(8,128)(2,1)}), bf16[16,2,32,128]{3,2,1,0:T(8,128)(2,1)S(1)}, u32[]{:S(2)}, u32[]{:S(2)}) async-start(bf16[16,2,32,128]{3,2,1,0:T(8,128)(2,1)} %get-tuple-element.50), calls=%async_computation.2 | async-start | bytes 524288 | tf_op jit(solution)/shard_map/all_to_all | solution.py:595
  71.0 6.2 %copy-start.7 = (bf16[16,3,4,16,128]{4,3,2,1,0:T(8,128)(2,1)S(1)}, bf16[16,3,4,16,128]{4,3,2,1,0:T(8,128)(2,1)}, u32[]{:S(2)}) copy-start(bf16[16,3,4,16,128]{4,3,2,1,0:T(8,128)(2,1)} %get-tuple-element.70) | copy-start | bytes 2359300
  71.0 37.8 %collective-permute-start.9 = (bf16[16,3,4,16,128]{4,3,2,1,0:T(8,128)(2,1)}, bf16[16,3,4,16,128]{4,3,2,1,0:T(8,128)(2,1)S(1)}, u32[]{:S(2)}, u32[]{:S(2)}) collective-permute-start(bf16[16,3,4,16,128]{4,3,2,1,0:T(8,128)(2,1)} %add_convert_fusion.3), channel_id=1, source_target_pairs={{0,2},{2,4},{4,6},{6,0},{1,3},{3,5},{5,7},{7,1},{8,10},{10,12},{12... | collective-permute-start | bytes 2359304 | tf_op jit(solution)/shard_map/ppermute | solution.py:607
  74.6 34.9 %collective-permute-start.11 = (bf16[16,3,4,16,128]{4,3,2,1,0:T(8,128)(2,1)}, bf16[16,3,4,16,128]{4,3,2,1,0:T(8,128)(2,1)}, u32[]{:S(2)}, u32[]{:S(2)}) collective-permute-start(bf16[16,3,4,16,128]{4,3,2,1,0:T(8,128)(2,1)} %add_convert_fusion.2), channel_id=1, source_target_pairs={{0,4},{2,6},{4,0},{6,2},{1,5},{3,7},{5,1},{7,3},{8,12},{10,14},{12... | collective-permute-start | bytes 2359304 | tf_op jit(solution)/shard_map/ppermute | solution.py:607
  78.4 32.8 %collective-permute-start.13 = (bf16[16,3,4,16,128]{4,3,2,1,0:T(8,128)(2,1)}, bf16[16,3,4,16,128]{4,3,2,1,0:T(8,128)(2,1)}, u32[]{:S(2)}, u32[]{:S(2)}) collective-permute-start(bf16[16,3,4,16,128]{4,3,2,1,0:T(8,128)(2,1)} %add_convert_fusion.1), channel_id=1, source_target_pairs={{0,6},{2,0},{4,2},{6,4},{1,7},{3,1},{5,3},{7,5},{8,14},{10,8},{12,... | collective-permute-start | bytes 2359304 | tf_op jit(solution)/shard_map/ppermute | solution.py:607
  100.5 10.6 %copy-start.6 = (bf16[16,3,4,16,128]{4,3,2,1,0:T(8,128)(2,1)S(1)}, bf16[16,3,4,16,128]{4,3,2,1,0:T(8,128)(2,1)}, u32[]{:S(2)}) copy-start(bf16[16,3,4,16,128]{4,3,2,1,0:T(8,128)(2,1)} %get-tuple-element.64) | copy-start | bytes 2359300
  100.5 22.4 %all-to-all-start.3 = ((bf16[16,2,96,128]{3,2,1,0:T(8,128)(2,1)}), bf16[16,2,96,128]{3,2,1,0:T(8,128)(2,1)S(1)}, u32[]{:S(2)}, u32[]{:S(2)}) async-start(bf16[16,2,96,128]{3,2,1,0:T(8,128)(2,1)} %attend_backward.1), calls=%async_computation.3 | async-start | bytes 1572864 | tf_op jit(solution)/shard_map/all_to_all | solution.py:595
  123.0 3.6 %copy-start.1 = (bf16[16,2,96,128]{3,2,1,0:T(8,128)(2,1)}, bf16[16,2,96,128]{3,2,1,0:T(8,128)(2,1)S(1)}, u32[]{:S(2)}) copy-start(bf16[16,2,96,128]{3,2,1,0:T(8,128)(2,1)S(1)} %all-to-all-done.3.dqkv) | copy-start | bytes 2359300
  123.0 17.2 %all-to-all-start.4 = ((bf16[16,3,4,16,128]{4,3,2,1,0:T(8,128)(2,1)}), bf16[16,3,4,16,128]{4,3,2,1,0:T(8,128)(2,1)S(1)}, u32[]{:S(2)}, u32[]{:S(2)}) async-start(bf16[16,3,4,16,128]{4,3,2,1,0:T(8,128)(2,1)} %add_convert_fusion), calls=%async_computation.4 | async-start | bytes 1572864 | tf_op jit(solution)/shard_map/all_to_all | solution.py:595
  131.8 2.6 %collective-permute-start.1 = (bf16[16,5,16,128]{3,2,1,0:T(8,128)(2,1)}, bf16[16,5,16,128]{3,2,1,0:T(8,128)(2,1)S(1)}, u32[]{:S(2)}, u32[]{:S(2)}) collective-permute-start(bf16[16,5,16,128]{3,2,1,0:T(8,128)(2,1)} %get-tuple-element.59), channel_id=1, source_target_pairs={{0,8},{8,0},{1,9},{9,1},{2,10},{10,2},{3,11},{11,3},{4,12},{12,4},... | collective-permute-start | bytes 983048 | tf_op jit(solution)/shard_map/ppermute | solution.py:611
  132.9 12.1 %collective-permute-start.3 = (bf16[16,5,16,128]{3,2,1,0:T(8,128)(2,1)}, bf16[16,5,16,128]{3,2,1,0:T(8,128)(2,1)S(1)}, u32[]{:S(2)}, u32[]{:S(2)}) collective-permute-start(bf16[16,5,16,128]{3,2,1,0:T(8,128)(2,1)} %get-tuple-element.61), channel_id=1, source_target_pairs={{0,8},{8,0},{1,9},{9,1},{2,10},{10,2},{3,11},{11,3},{4,12},{12,4},... | collective-permute-start | bytes 983048 | tf_op jit(solution)/shard_map/ppermute | solution.py:611
  133.2 12.0 %collective-permute-start.5 = (bf16[16,5,16,128]{3,2,1,0:T(8,128)(2,1)}, bf16[16,5,16,128]{3,2,1,0:T(8,128)(2,1)S(1)}, u32[]{:S(2)}, u32[]{:S(2)}) collective-permute-start(bf16[16,5,16,128]{3,2,1,0:T(8,128)(2,1)} %get-tuple-element.63), channel_id=1, source_target_pairs={{0,8},{8,0},{1,9},{9,1},{2,10},{10,2},{3,11},{11,3},{4,12},{12,4},... | collective-permute-start | bytes 983048 | tf_op jit(solution)/shard_map/ppermute | solution.py:611
  133.4 24.4 %collective-permute-start = (bf16[16,5,16,128]{3,2,1,0:T(8,128)(2,1)}, bf16[16,5,16,128]{3,2,1,0:T(8,128)(2,1)}, u32[]{:S(2)}, u32[]{:S(2)}) collective-permute-start(bf16[16,5,16,128]{3,2,1,0:T(8,128)(2,1)} %get-tuple-element.57), channel_id=1, source_target_pairs={{0,8},{8,0},{1,9},{9,1},{2,10},{10,2},{3,11},{11,3},{4,12},{12,4},... | collective-permute-start | bytes 983048 | tf_op jit(solution)/shard_map/ppermute | solution.py:611
  135.4 9.6 %copy-start.10 = (bf16[16,5,16,128]{3,2,1,0:T(8,128)(2,1)S(1)}, bf16[16,5,16,128]{3,2,1,0:T(8,128)(2,1)}, u32[]{:S(2)}) copy-start(bf16[16,5,16,128]{3,2,1,0:T(8,128)(2,1)} %get-tuple-element.60) | copy-start | bytes 983044
  135.4 25.7 %collective-permute-start.2 = (bf16[16,5,16,128]{3,2,1,0:T(8,128)(2,1)S(1)}, bf16[16,5,16,128]{3,2,1,0:T(8,128)(2,1)}, u32[]{:S(2)}, u32[]{:S(2)}) collective-permute-start(bf16[16,5,16,128]{3,2,1,0:T(8,128)(2,1)S(1)} %add_convert_fusion.7), channel_id=1, source_target_pairs={{0,2},{2,4},{4,6},{6,0},{1,3},{3,5},{5,7},{7,1},{8,10},{10,12},{12... | collective-permute-start | bytes 983048 | tf_op jit(solution)/shard_map/ppermute | solution.py:607
  140.2 5.0 %copy-start.9 = (bf16[16,5,16,128]{3,2,1,0:T(8,128)(2,1)S(1)}, bf16[16,5,16,128]{3,2,1,0:T(8,128)(2,1)}, u32[]{:S(2)}) copy-start(bf16[16,5,16,128]{3,2,1,0:T(8,128)(2,1)} %get-tuple-element.62) | copy-start | bytes 983044
  141.3 16.0 %all-to-all-start.5 = ((bf16[16,3,4,16,128]{4,3,2,1,0:T(8,128)(2,1)}), bf16[16,3,4,16,128]{4,3,2,1,0:T(8,128)(2,1)S(1)}, u32[]{:S(2)}, u32[]{:S(2)}) async-start(bf16[16,3,4,16,128]{4,3,2,1,0:T(8,128)(2,1)} %broadcast_in_dim.4), calls=%async_computation.5 | async-start | bytes 1572864 | tf_op jit(solution)/shard_map/all_to_all | solution.py:595
  145.1 16.1 %collective-permute-start.4 = (bf16[16,5,16,128]{3,2,1,0:T(8,128)(2,1)S(1)}, bf16[16,5,16,128]{3,2,1,0:T(8,128)(2,1)}, u32[]{:S(2)}, u32[]{:S(2)}) collective-permute-start(bf16[16,5,16,128]{3,2,1,0:T(8,128)(2,1)S(1)} %add_convert_fusion.6), channel_id=1, source_target_pairs={{0,4},{2,6},{4,0},{6,2},{1,5},{3,7},{5,1},{7,3},{8,12},{10,14},{12... | collective-permute-start | bytes 983048 | tf_op jit(solution)/shard_map/ppermute | solution.py:607
  145.3 15.8 %collective-permute-start.6 = (bf16[16,5,16,128]{3,2,1,0:T(8,128)(2,1)S(1)}, bf16[16,5,16,128]{3,2,1,0:T(8,128)(2,1)}, u32[]{:S(2)}, u32[]{:S(2)}) collective-permute-start(bf16[16,5,16,128]{3,2,1,0:T(8,128)(2,1)S(1)} %add_convert_fusion.5), channel_id=1, source_target_pairs={{0,6},{2,0},{4,2},{6,4},{1,7},{3,1},{5,3},{7,5},{8,14},{10,8},{12,... | collective-permute-start | bytes 983048 | tf_op jit(solution)/shard_map/ppermute | solution.py:607
  157.3 47.6 %copy-start = (bf16[16,3,4,16,128]{4,3,2,1,0:T(8,128)(2,1)}, bf16[16,3,4,16,128]{4,3,2,1,0:T(8,128)(2,1)S(1)}, u32[]{:S(2)}) copy-start(bf16[16,3,4,16,128]{4,3,2,1,0:T(8,128)(2,1)S(1)} %all-to-all-done.5.refs_0_) | copy-start | bytes 2359300
  157.3 38.0 %collective-permute-start.21 = (bf16[16,3,4,16,128]{4,3,2,1,0:T(8,128)(2,1)S(1)}, bf16[16,3,4,16,128]{4,3,2,1,0:T(8,128)(2,1)S(1)}, u32[]{:S(2)}, u32[]{:S(2)}) collective-permute-start(bf16[16,3,4,16,128]{4,3,2,1,0:T(8,128)(2,1)S(1)} %all-to-all-done.5.refs_0_), channel_id=1, source_target_pairs={{0,2},{2,4},{4,6},{6,0},{1,3},{3,5},{5,7},{7,1},{8,10},{10,12},{12... | collective-permute-start | bytes 2359304 | tf_op jit(solution)/shard_map/ppermute | solution.py:607
  157.7 38.8 %collective-permute-start.22 = (bf16[16,3,4,16,128]{4,3,2,1,0:T(8,128)(2,1)S(1)}, bf16[16,3,4,16,128]{4,3,2,1,0:T(8,128)(2,1)S(1)}, u32[]{:S(2)}, u32[]{:S(2)}) collective-permute-start(bf16[16,3,4,16,128]{4,3,2,1,0:T(8,128)(2,1)S(1)} %all-to-all-done.5.refs_0_), channel_id=1, source_target_pairs={{0,4},{2,6},{4,0},{6,2},{1,5},{3,7},{5,1},{7,3},{8,12},{10,14},{12... | collective-permute-start | bytes 2359304 | tf_op jit(solution)/shard_map/ppermute | solution.py:607
  163.5 15.8 %all-to-all-start.6 = ((bf16[16,5,16,128]{3,2,1,0:T(8,128)(2,1)}), bf16[16,5,16,128]{3,2,1,0:T(8,128)(2,1)S(1)}, u32[]{:S(2)}, u32[]{:S(2)}) async-start(bf16[16,5,16,128]{3,2,1,0:T(8,128)(2,1)} %add_convert_fusion.4), calls=%async_computation.6 | async-start | bytes 655360 | tf_op jit(solution)/shard_map/all_to_all | solution.py:595
  171.2 33.7 %collective-permute-start.23 = (bf16[16,3,4,16,128]{4,3,2,1,0:T(8,128)(2,1)S(1)}, bf16[16,3,4,16,128]{4,3,2,1,0:T(8,128)(2,1)S(1)}, u32[]{:S(2)}, u32[]{:S(2)}) collective-permute-start(bf16[16,3,4,16,128]{4,3,2,1,0:T(8,128)(2,1)S(1)} %all-to-all-done.5.refs_0_), channel_id=1, source_target_pairs={{0,6},{2,0},{4,2},{6,4},{1,7},{3,1},{5,3},{7,5},{8,14},{10,8},{12,... | collective-permute-start | bytes 2359304 | tf_op jit(solution)/shard_map/ppermute | solution.py:607
  189.5 23.8 %copy-start.2 = (bf16[16,4,16,128]{3,2,1,0:T(8,128)(2,1)}, bf16[16,4,16,128]{3,2,1,0:T(8,128)(2,1)S(1)}, u32[]{:S(2)}) copy-start(bf16[16,4,16,128]{3,2,1,0:T(8,128)(2,1)S(1)} %all_to_all.42.refs_0_) | copy-start | bytes 786436
  189.5 10.7 %collective-permute-start.14 = (bf16[16,4,16,128]{3,2,1,0:T(8,128)(2,1)S(1)}, bf16[16,4,16,128]{3,2,1,0:T(8,128)(2,1)S(1)}, u32[]{:S(2)}, u32[]{:S(2)}) collective-permute-start(bf16[16,4,16,128]{3,2,1,0:T(8,128)(2,1)S(1)} %all_to_all.42.refs_0_), channel_id=1, source_target_pairs={{0,2},{2,4},{4,6},{6,0},{1,3},{3,5},{5,7},{7,1},{8,10},{10,12},{12... | collective-permute-start | bytes 786440 | tf_op jit(solution)/shard_map/ppermute | solution.py:607
  194.1 10.9 %collective-permute-start.15 = (bf16[16,4,16,128]{3,2,1,0:T(8,128)(2,1)S(1)}, bf16[16,4,16,128]{3,2,1,0:T(8,128)(2,1)S(1)}, u32[]{:S(2)}, u32[]{:S(2)}) collective-permute-start(bf16[16,4,16,128]{3,2,1,0:T(8,128)(2,1)S(1)} %all_to_all.42.refs_0_), channel_id=1, source_target_pairs={{0,4},{2,6},{4,0},{6,2},{1,5},{3,7},{5,1},{7,3},{8,12},{10,14},{12... | collective-permute-start | bytes 786440 | tf_op jit(solution)/shard_map/ppermute | solution.py:607
  195.4 21.8 %copy-start.3 = (bf16[16,3,4,16,128]{4,3,2,1,0:T(8,128)(2,1)}, bf16[16,3,4,16,128]{4,3,2,1,0:T(8,128)(2,1)S(1)}, u32[]{:S(2)}) copy-start(bf16[16,3,4,16,128]{4,3,2,1,0:T(8,128)(2,1)S(1)} %collective-permute-done.21.refs_1_) | copy-start | bytes 2359300
  195.4 12.9 %collective-permute-start.16 = (bf16[16,4,16,128]{3,2,1,0:T(8,128)(2,1)S(1)}, bf16[16,4,16,128]{3,2,1,0:T(8,128)(2,1)S(1)}, u32[]{:S(2)}, u32[]{:S(2)}) collective-permute-start(bf16[16,4,16,128]{3,2,1,0:T(8,128)(2,1)S(1)} %all_to_all.42.refs_0_), channel_id=1, source_target_pairs={{0,6},{2,0},{4,2},{6,4},{1,7},{3,1},{5,3},{7,5},{8,14},{10,8},{12,... | collective-permute-start | bytes 786440 | tf_op jit(solution)/shard_map/ppermute | solution.py:607
  196.5 20.6 %copy-start.4 = (bf16[16,3,4,16,128]{4,3,2,1,0:T(8,128)(2,1)}, bf16[16,3,4,16,128]{4,3,2,1,0:T(8,128)(2,1)S(1)}, u32[]{:S(2)}) copy-start(bf16[16,3,4,16,128]{4,3,2,1,0:T(8,128)(2,1)S(1)} %collective-permute-done.22.refs_2_) | copy-start | bytes 2359300
  196.5 11.8 %collective-permute-start.17 = (bf16[16,4,16,128]{3,2,1,0:T(8,128)(2,1)S(1)}, bf16[16,4,16,128]{3,2,1,0:T(8,128)(2,1)S(1)}, u32[]{:S(2)}, u32[]{:S(2)}) collective-permute-start(bf16[16,4,16,128]{3,2,1,0:T(8,128)(2,1)S(1)} %all_to_all.42.refs_0_), channel_id=1, source_target_pairs={{0,8},{8,0},{1,9},{9,1},{2,10},{10,2},{3,11},{11,3},{4,12},{12,4},... | collective-permute-start | bytes 786440 | tf_op jit(solution)/shard_map/ppermute | solution.py:622
  200.2 13.1 %copy-start.11 = (bf16[16,4,16,128]{3,2,1,0:T(8,128)(2,1)}, bf16[16,4,16,128]{3,2,1,0:T(8,128)(2,1)S(1)}, u32[]{:S(2)}) copy-start(bf16[16,4,16,128]{3,2,1,0:T(8,128)(2,1)S(1)} %collective-permute-done.14.refs_1_) | copy-start | bytes 786436
  200.2 8.6 %collective-permute-start.18 = (bf16[16,4,16,128]{3,2,1,0:T(8,128)(2,1)S(1)}, bf16[16,4,16,128]{3,2,1,0:T(8,128)(2,1)S(1)}, u32[]{:S(2)}, u32[]{:S(2)}) collective-permute-start(bf16[16,4,16,128]{3,2,1,0:T(8,128)(2,1)S(1)} %collective-permute-done.14.refs_1_), channel_id=1, source_target_pairs={{0,8},{8,0},{1,9},{9,1},{2,10},{10,2},{3,11},{11,3},{4,12},{12,4},... | collective-permute-start | bytes 786440 | tf_op jit(solution)/shard_map/ppermute | solution.py:622
  204.9 12.2 %copy-start.5 = (bf16[16,3,4,16,128]{4,3,2,1,0:T(8,128)(2,1)}, bf16[16,3,4,16,128]{4,3,2,1,0:T(8,128)(2,1)S(1)}, u32[]{:S(2)}) copy-start(bf16[16,3,4,16,128]{4,3,2,1,0:T(8,128)(2,1)S(1)} %collective-permute-done.23.refs_3_) | copy-start | bytes 2359300
  204.9 12.2 %collective-permute-start.24 = (bf16[16,3,4,16,128]{4,3,2,1,0:T(8,128)(2,1)S(1)}, bf16[16,3,4,16,128]{4,3,2,1,0:T(8,128)(2,1)}, u32[]{:S(2)}, u32[]{:S(2)}) collective-permute-start(bf16[16,3,4,16,128]{4,3,2,1,0:T(8,128)(2,1)S(1)} %all-to-all-done.5.refs_0_), channel_id=1, source_target_pairs={{0,8},{8,0},{1,9},{9,1},{2,10},{10,2},{3,11},{11,3},{4,12},{12,4},... | collective-permute-start | bytes 2359304 | tf_op jit(solution)/shard_map/ppermute | solution.py:622
  205.0 8.3 %copy-start.12 = (bf16[16,4,16,128]{3,2,1,0:T(8,128)(2,1)}, bf16[16,4,16,128]{3,2,1,0:T(8,128)(2,1)S(1)}, u32[]{:S(2)}) copy-start(bf16[16,4,16,128]{3,2,1,0:T(8,128)(2,1)S(1)} %collective-permute-done.15.refs_2_) | copy-start | bytes 786436
  205.0 12.1 %collective-permute-start.25 = (bf16[16,3,4,16,128]{4,3,2,1,0:T(8,128)(2,1)S(1)}, bf16[16,3,4,16,128]{4,3,2,1,0:T(8,128)(2,1)}, u32[]{:S(2)}, u32[]{:S(2)}) collective-permute-start(bf16[16,3,4,16,128]{4,3,2,1,0:T(8,128)(2,1)S(1)} %collective-permute-done.21.refs_1_), channel_id=1, source_target_pairs={{0,8},{8,0},{1,9},{9,1},{2,10},{10,2},{3,11},{11,3},{4,12},{12,4},... | collective-permute-start | bytes 2359304 | tf_op jit(solution)/shard_map/ppermute | solution.py:622
  208.2 2.7 %copy-start.13 = (bf16[16,4,16,128]{3,2,1,0:T(8,128)(2,1)}, bf16[16,4,16,128]{3,2,1,0:T(8,128)(2,1)S(1)}, u32[]{:S(2)}) copy-start(bf16[16,4,16,128]{3,2,1,0:T(8,128)(2,1)S(1)} %collective-permute-done.16.refs_3_) | copy-start | bytes 786436
  208.2 8.9 %collective-permute-start.26 = (bf16[16,3,4,16,128]{4,3,2,1,0:T(8,128)(2,1)S(1)}, bf16[16,3,4,16,128]{4,3,2,1,0:T(8,128)(2,1)}, u32[]{:S(2)}, u32[]{:S(2)}) collective-permute-start(bf16[16,3,4,16,128]{4,3,2,1,0:T(8,128)(2,1)S(1)} %collective-permute-done.22.refs_2_), channel_id=1, source_target_pairs={{0,8},{8,0},{1,9},{9,1},{2,10},{10,2},{3,11},{11,3},{4,12},{12,4},... | collective-permute-start | bytes 2359304 | tf_op jit(solution)/shard_map/ppermute | solution.py:622
  208.3 2.6 %copy-start.14 = (bf16[16,4,16,128]{3,2,1,0:T(8,128)(2,1)}, bf16[16,4,16,128]{3,2,1,0:T(8,128)(2,1)S(1)}, u32[]{:S(2)}) copy-start(bf16[16,4,16,128]{3,2,1,0:T(8,128)(2,1)S(1)} %collective-permute-done.17.refs_4_) | copy-start | bytes 786436
  208.3 8.8 %collective-permute-start.27 = (bf16[16,3,4,16,128]{4,3,2,1,0:T(8,128)(2,1)S(1)}, bf16[16,3,4,16,128]{4,3,2,1,0:T(8,128)(2,1)}, u32[]{:S(2)}, u32[]{:S(2)}) collective-permute-start(bf16[16,3,4,16,128]{4,3,2,1,0:T(8,128)(2,1)S(1)} %collective-permute-done.23.refs_3_), channel_id=1, source_target_pairs={{0,8},{8,0},{1,9},{9,1},{2,10},{10,2},{3,11},{11,3},{4,12},{12,4},... | collective-permute-start | bytes 2359304 | tf_op jit(solution)/shard_map/ppermute | solution.py:622
  208.8 2.1 collective-permute-start.19
  211.6 1.7 collective-permute-start.20
  (3 other events, 3.5 us)

commit v4 on v3

--- a/solution.py
+++ b/solution.py
@@ -342,108 +342,95 @@
 
 
 def ff_kernel(
-    place, tok, ob, wout, gain, bias, wg, wu, wd, cot,
+    place, tok, ob, wout, gain, bias, wg_all, wu_all, wd_all, cot,
     output, k0, k1, k2, k3, s0, s1, s2, s3, gwout, vecs, dres, dot_out,
-    res, h2, h2t, dh2, obt, mt,
+    h2t, dh2, obt, mt, wg_here, wu_here, wd_here, arrived,
 ):
     pieces = (k0, k1, k2, k3, s0, s1, s2, s3)
     core, y = core_of(place[0]), y_of(place[0])
-    step = pl.program_id(0)
-    last = pl.num_programs(0) - 1
-
-    @pl.when(step == 0)
-    def first():
-        for k in range(2):
-            obt[:, k * 128 : (k + 1) * 128] = ob[:, k].reshape(512, 128)
-        r = tok[...].astype(F32) + mm(obt[...].T, wout[...])
-        xhat, _ = normalize(r)
-        h = (xhat * gain[...] + bias[...]).astype(BF)
-        res[...] = r
-        h2[...] = h
-        mt[...] = h.T
-        h2t[...] = ordered(mt, core, y)
-        output[...] = r
-        dh2[...] = jnp.zeros_like(dh2)
-
-    gate = mm(h2[...], wg[...])
-    up = mm(h2[...], wu[...])
-    dm = mm_nt(cot[...], wd[...])
-    sg = jax.nn.sigmoid(gate)
-    act = gate * sg
-    m = (act * up).astype(BF)
-    dgate = (dm * up * (sg * (1.0 + gate - act))).astype(BF)
-    dup = (dm * act).astype(BF)
-    output[...] += mm(m, wd[...])
-    mt[...] = m.T
-    pack(pieces, (0, 0), mm(h2t[...], dgate))
-    pack(pieces, (1, 0), mm(h2t[...], dup))
-    pack(pieces, (2, 0), mm(ordered(mt, core, y), cot[...]))
-    dh2[...] += mm_nt(dgate, wg[...]) + mm_nt(dup, wu[...])
-
-    @pl.when(step == last)
-    def final():
-        xhat, rstd = normalize(res[...])
-        dh = dh2[...]
-        vecs[0:1] = jnp.sum(dh * xhat, 0, keepdims=True)
-        vecs[1:2] = jnp.sum(dh, 0, keepdims=True)
-        dr = cot[...].astype(F32) + norm_back(dh, gain[...], xhat, rstd)
-        dres[...] = dr
-        da = dr.astype(BF)
-        gwout[...] = mm(ordered(obt, core, y), da)
-        do = mm_nt(wout[...], da).astype(BF)
-        for k in range(2):
-            dot_out[:, k] = do[:, k * 128 : (k + 1) * 128].reshape(HEADS, HEAD_DIM, 128)
+    steps = wg_all.shape[1] // FC
+
+    def copies(i):
+        at = slice(i * FC, (i + 1) * FC)
+        return (
+            pltpu.make_async_copy(wg_all.at[:, at], wg_here.at[i], arrived.at[3 * i]),
+            pltpu.make_async_copy(wu_all.at[:, at], wu_here.at[i], arrived.at[3 * i + 1]),
+            pltpu.make_async_copy(wd_all.at[at, :], wd_here.at[i], arrived.at[3 * i + 2]),
+        )
+
+    for i in range(steps):
+        for copy in copies(i):
+            copy.start()
+    for k in range(2):
+        obt[:, k * 128 : (k + 1) * 128] = ob[:, k].reshape(512, 128)
+    r = tok[...].astype(F32) + mm(obt[...].T, wout[...])
+    xhat, rstd = normalize(r)
+    h2 = (xhat * gain[...] + bias[...]).astype(BF)
+    mt[...] = h2.T
+    h2t[...] = ordered(mt, core, y)
+    output[...] = r
+    for i in range(steps):
+        for copy in copies(i):
+            copy.wait()
+        wg, wu, wd = wg_here[i], wu_here[i], wd_here[i]
+        gate = mm(h2, wg)
+        up = mm(h2, wu)
+        dm = mm_nt(cot[...], wd)
+        sg = jax.nn.sigmoid(gate)
+        act = gate * sg
+        m = (act * up).astype(BF)
+        dgate = (dm * up * (sg * (1.0 + gate - act))).astype(BF)
+        dup = (dm * act).astype(BF)
+        output[...] += mm(m, wd)
+        mt[...] = m.T
+        pack(pieces, (0, i), mm(h2t[...], dgate))
+        pack(pieces, (1, i), mm(h2t[...], dup))
+        pack(pieces, (2, i), mm(ordered(mt, core, y), cot[...]))
+        part = mm_nt(dgate, wg) + mm_nt(dup, wu)
+        if i == 0:
+            dh2[...] = part
+        else:
+            dh2[...] += part
+    xhat, rstd = normalize(r)
+    dh = dh2[...]
+    vecs[0:1] = jnp.sum(dh * xhat, 0, keepdims=True)
+    vecs[1:2] = jnp.sum(dh, 0, keepdims=True)
+    dr = cot[...].astype(F32) + norm_back(dh, gain[...], xhat, rstd)
+    dres[...] = dr
+    da = dr.astype(BF)
+    gwout[...] = mm(ordered(obt, core, y), da).astype(BF)
+    do = mm_nt(wout[...], da).astype(BF)
+    for k in range(2):
+        dot_out[:, k] = do[:, k * 128 : (k + 1) * 128].reshape(HEADS, HEAD_DIM, 128)
 
 
 def ff_call(place, tok, ob, wout, gain, bias, wg, wu, wd, cot):
     rows, width = tok.shape
     ff = wg.shape[1]
-
+    steps = ff // FC
+    anywhere = pl.BlockSpec(memory_space=pl.ANY)
     return pl.pallas_call(
         ff_kernel,
-        grid_spec=pltpu.PrefetchScalarGridSpec(
-            num_scalar_prefetch=1,
-            grid=(ff // FC,),
-            in_specs=[
-                whole(rows, width),
-                whole(HEADS, 2, HEAD_DIM, 128),
-                whole(width, width),
-                whole(1, width),
-                whole(1, width),
-                pl.BlockSpec((width, FC), lambda i, c: (0, i)),
-                pl.BlockSpec((width, FC), lambda i, c: (0, i)),
-                pl.BlockSpec((FC, width), lambda i, c: (i, 0)),
-                whole(rows, width),
-            ],
-            out_specs=(
-                whole(rows, width),
-            )
-            + (pl.BlockSpec((16, 3, 1, 16, 128), lambda i, c: (0, 0, i, 0, 0)),) * 8
-            + (
-                whole(width, width),
-                whole(2, width),
-                whole(rows, width),
-                whole(HEADS, 2, HEAD_DIM, 128),
-            ),
-            scratch_shapes=[
-                pltpu.VMEM((rows, width), F32),
-                pltpu.VMEM((rows, width), BF),
-                pltpu.VMEM((width, rows), BF),
-                pltpu.VMEM((rows, width), F32),
-                pltpu.VMEM((width, rows), BF),
-                pltpu.VMEM((FC, rows), BF),
-            ],
-        ),
-        out_shape=(
-            jax.ShapeDtypeStruct((rows, width), F32),
-        )
+        in_specs=[SMEM] + [VM] * 5 + [anywhere] * 3 + [VM],
+        out_specs=(VM,) * 13,
+        out_shape=(jax.ShapeDtypeStruct((rows, width), F32),)
         + (jax.ShapeDtypeStruct((16, 3, 4, 16, 128), BF),) * 8
         + (
-            jax.ShapeDtypeStruct((width, width), F32),
+            jax.ShapeDtypeStruct((width, width), BF),
             jax.ShapeDtypeStruct((2, width), F32),
             jax.ShapeDtypeStruct((rows, width), F32),
             jax.ShapeDtypeStruct((HEADS, 2, HEAD_DIM, 128), BF),
         ),
+        scratch_shapes=[
+            pltpu.VMEM((width, rows), BF),
+            pltpu.VMEM((rows, width), F32),
+            pltpu.VMEM((width, rows), BF),
+            pltpu.VMEM((FC, rows), BF),
+            pltpu.VMEM((steps, width, FC), BF),
+            pltpu.VMEM((steps, width, FC), BF),
+            pltpu.VMEM((steps, FC, width), BF),
+            pltpu.SemaphoreType.DMA((3 * steps,)),
+        ],
         cost_estimate=cost(2 * rows * width * ff * 9),
         compiler_params=pltpu.CompilerParams(vmem_limit_bytes=VMEM_LIMIT),
         name="feed_forward",
@@ -619,7 +606,8 @@
 
 def collect(whole_piece):
     mine = [whole_piece] + [along_y(whole_piece, d) for d in (1, 2, 3)]
-    return mine, [lax.ppermute(m, "c", SWAP) for m in mine]
+    theirs = [lax.ppermute(m, "c", SWAP) for m in mine[::-1]]
+    return mine, theirs[::-1]
 
 
 def after(x, *others):

time: 225 us -> 225 us (level)
    all_to_all x5, waiting for transfers between devices: 26.1 us -> 30.2 us  [exchange(): return lax.all_to_all(x, axes, 0, 0, tiled=True)]
    ppermute x12, waiting for transfers between devices: 2.36 us -> 0.05 us  [along_y(): return lax.ppermute(x, 'y', [(i, (i + d) % 4) for i in range(4)])]
  transfers between devices with their start and end apart: 33 -> 33, of which waited for: 9 -> 7; matrix products, arithmetic and copies ran while one was open for 6% -> 6% of each run, Pallas kernels for 13% -> 13%
where the time goes in v4:
time: 225 us; the launch traced here: 224 us
  starting transfers between devices  64.5 us (29%)
  Pallas kernels  61.3 us (27%)
  blocking collectives  47.2 us (21%)
  waiting for transfers between devices  33.9 us (15%)
  other arithmetic  12.6 us (6%)
  local copies, waits for them, and re-layouts  3.17 us (1%)
    all_to_all x3, blocking collectives, exchange(): return lax.all_to_all(x, axes, 0, 0, tiled=True)  47.2 us
    all_to_all x5, waiting for transfers between devices, exchange(): return lax.all_to_all(x, axes, 0, 0, tiled=True)  30.2 us
    all_to_all x5, starting transfers between devices, exchange(): return lax.all_to_all(x, axes, 0, 0, tiled=True)  27 us
    ppermute x12, starting transfers between devices, along_y(): return lax.ppermute(x, 'y', [(i, (i + d) % 4) for i in range(4)])  21.1 us
    pallas_call x1, Pallas kernels, attend_back_call(): pl.pallas_call(attend_back_kernel, out_shape=jax.ShapeDtypeStruct((HEADS,...  20.4 us
    ppermute x8, starting transfers between devices, collect(): theirs = [lax.ppermute(m, 'c', SWAP) for m in mine[::-1]]  13.6 us
    convert_element_type x8, other arithmetic, add_up(): return sum((t.astype(F32) for t in terms)).astype(BF)  12.4 us
    pallas_call x1, Pallas kernels, ff_call(): pl.pallas_call(ff_kernel, in_specs=[SMEM] + [VM] * 5 + [anywhere] * 3 + [...  11.4 us
  transfers between devices with their start and end apart: 33, of which 7 were waited for; matrix products, arithmetic and copies ran while one was open for 6% of the time, Pallas kernels for 13%

profile of v4, /device:TPU:1, one launch (start us, length us, event | category | flops | bytes accessed | tf_op | source)
XLA Modules:
  0.0 223.9 jit_solution(18067049536305635477)
XLA Ops:
  0.7 3.2 %qkv_forward.1 = bf16[16,2,96,128]{3,2,1,0:T(8,128)(2,1)} custom-call(s32[1]{0:T(128)} %bitcast.place, bf16[256,512]{1,0:T(8,128)(2,1)} %bitcast.21, f32[1,512]{1,0:T(1,128)} %bitcast.25, f32[1,512]{1,0:T(1,128)} %bitcast.27, bf16[512,512]{1,0:T(8,128)(2,1)} %wq.3, bf16[512,512]{1,0:T(8,128)(2,1)} %wk.3, bf16[512,512]{1,0:T(8,128)(2,1)} %wv.3, ...), custom_call_target="tpu_custom_call" | custom-call | flops 402653184 | bytes 1048576 | tf_op jit(solution)/shard_map/qkv_forward/pallas_call | solution.py:96
  3.9 23.7 %all_to_all.40.qkv = bf16[16,2,96,128]{3,2,1,0:T(8,128)(2,1)} all-to-all(bf16[16,2,96,128]{3,2,1,0:T(8,128)(2,1)} %qkv_forward.1), channel_id=1, replica_groups=mesh['x'=4,'zh'=2,'c'=2,'y'=4,'zl'=2] {'x','zh','c'}, dimensions={0} | all-to-all | bytes 1572864 | tf_op jit(solution)/shard_map/all_to_all | solution.py:582
  27.6 10.9 %attend_forward.1 = (bf16[16,2,32,128]{3,2,1,0:T(8,128)(2,1)}, f32[2,32,2048]{2,1,0:T(8,128)}, f32[2,1,2048]{2,1,0:T(1,128)}) custom-call(s32[2]{0:T(128)} %lengths.3, bf16[16,2,96,128]{3,2,1,0:T(8,128)(2,1)} %all_to_all.40.qkv), custom_call_target="tpu_custom_call" | custom-call | flops 17179869184 | bytes 1048576 | tf_op jit(solution)/shard_map/attend_forward/pallas_call | solution.py:196
  38.5 13.4 %all_to_all.41.ob = bf16[16,2,32,128]{3,2,1,0:T(8,128)(2,1)} all-to-all(bf16[16,2,32,128]{3,2,1,0:T(8,128)(2,1)} %get-tuple-element.47), channel_id=1, replica_groups=mesh['x'=4,'zh'=2,'c'=2,'y'=4,'zl'=2] {'x','zh','c'}, dimensions={0} | all-to-all | bytes 524288 | tf_op jit(solution)/shard_map/all_to_all | solution.py:582
  51.9 11.4 %feed_forward.1 = (f32[256,512]{1,0:T(8,128)}, bf16[16,3,4,16,128]{4,3,2,1,0:T(8,128)(2,1)}, bf16[16,3,4,16,128]{4,3,2,1,0:T(8,128)(2,1)}, bf16[16,3,4,16,128]{4...) custom-call(s32[1]{0:T(128)} %bitcast.place, ...), custom_call_target="tpu_custom_call" | custom-call | flops 4831838208 | bytes 1048576 | tf_op jit(solution)/shard_map/feed_forward/pallas_call | solution.py:412
  63.2 0.5 collective-permute-start.10
  63.8 0.4 collective-permute-start.12
  64.3 3.7 %all-to-all-start.2 = ((bf16[16,2,32,128]{3,2,1,0:T(8,128)(2,1)}), bf16[16,2,32,128]{3,2,1,0:T(8,128)(2,1)S(1)}, u32[]{:S(2)}, u32[]{:S(2)}) async-start(bf16[16,2,32,128]{3,2,1,0:T(8,128)(2,1)} %get-tuple-element.50), calls=%async_computation.2 | async-start | bytes 524288 | tf_op jit(solution)/shard_map/all_to_all | solution.py:582
  68.1 2.3 %add_convert_fusion.2 = bf16[16,3,4,16,128]{4,3,2,1,0:T(8,128)(2,1)} fusion(bf16[16,3,4,16,128]{4,3,2,1,0:T(8,128)(2,1)S(1)} %collective-permute-done.10, bf16[16,3,4,16,128]{4,3,2,1,0:T(8,128)(2,1)} %get-tuple-element.68), kind=kLoop, calls=%fused_computation.2 | loop fusion | flops 1572864 | bytes 2359296 | tf_op jit(solution)/shard_map/convert_element_type | solution.py:590
  70.4 2.9 %collective-permute-start.11 = (bf16[16,3,4,16,128]{4,3,2,1,0:T(8,128)(2,1)}, bf16[16,3,4,16,128]{4,3,2,1,0:T(8,128)(2,1)S(1)}, u32[]{:S(2)}, u32[]{:S(2)}) collective-permute-start(bf16[16,3,4,16,128]{4,3,2,1,0:T(8,128)(2,1)} %add_convert_fusion.2), channel_id=1, source_target_pairs={{0,4},{2,6},{4,0},{6,2},{1,5},{3,7},{5,1},{7,3},{8,12},{10,14},{12... | collective-permute-start | bytes 2359304 | tf_op jit(solution)/shard_map/ppermute | solution.py:594
  73.3 2.3 %add_convert_fusion.3 = bf16[16,3,4,16,128]{4,3,2,1,0:T(8,128)(2,1)} fusion(bf16[16,3,4,16,128]{4,3,2,1,0:T(8,128)(2,1)} %collective-permute-done.8, bf16[16,3,4,16,128]{4,3,2,1,0:T(8,128)(2,1)S(1)} %copy-done.8), kind=kLoop, calls=%fused_computation.3 | loop fusion | flops 1572864 | bytes 2359296 | tf_op jit(solution)/shard_map/convert_element_type | solution.py:590
  75.6 0.4 collective-permute-start.9
  76.0 1.2 add_convert_fusion.1
  77.2 2.3 %collective-permute-start.13 = (bf16[16,3,4,16,128]{4,3,2,1,0:T(8,128)(2,1)}, bf16[16,3,4,16,128]{4,3,2,1,0:T(8,128)(2,1)}, u32[]{:S(2)}, u32[]{:S(2)}) collective-permute-start(bf16[16,3,4,16,128]{4,3,2,1,0:T(8,128)(2,1)} %add_convert_fusion.1), channel_id=1, source_target_pairs={{0,6},{2,0},{4,2},{6,4},{1,7},{3,1},{5,3},{7,5},{8,14},{10,8},{12,... | collective-permute-start | bytes 2359304 | tf_op jit(solution)/shard_map/ppermute | solution.py:594
  79.5 0.7 copy-done.17
  80.2 20.4 %attend_backward.1 = bf16[16,2,96,128]{3,2,1,0:T(8,128)(2,1)} custom-call(s32[2]{0:T(128)} %lengths.3, bf16[16,2,96,128]{3,2,1,0:T(8,128)(2,1)} %all_to_all.40.qkv, bf16[16,2,32,128]{3,2,1,0:T(8,128)(2,1)} %copy-done.17, f32[2,32,2048]{2,1,0:T(8,128)} %get-tuple-element.51.mixed, f32[2,1,2048]{2,1,0:T(1,128)} %get-tuple-element.52.total, ...), custom_call_target="tpu_custom_call" | custom-call | flops 17179869184 | bytes 1048576 | tf_op jit(solution)/shard_map/attend_backward/pallas_call | solution.py:292
  100.6 8.3 %all-to-all-start.3 = ((bf16[16,2,96,128]{3,2,1,0:T(8,128)(2,1)}), bf16[16,2,96,128]{3,2,1,0:T(8,128)(2,1)S(1)}, u32[]{:S(2)}, u32[]{:S(2)}) async-start(bf16[16,2,96,128]{3,2,1,0:T(8,128)(2,1)} %attend_backward.1), calls=%async_computation.3 | async-start | bytes 1572864 | tf_op jit(solution)/shard_map/all_to_all | solution.py:582
  108.9 3.0 %add_convert_fusion = bf16[16,3,4,16,128]{4,3,2,1,0:T(8,128)(2,1)} fusion(bf16[16,3,4,16,128]{4,3,2,1,0:T(8,128)(2,1)} %collective-permute-done.13, bf16[16,3,4,16,128]{4,3,2,1,0:T(8,128)(2,1)S(1)} %collective-permute-done.11, bf16[16,3,4,16,128]{4,3,2,1,0:T(8,128)(2,1)} %collective-permute-done.9, bf16[16,3,4,16,128]{4,3,2,1,0:T(8,128)(2,1)S(1)} %collective-permute-done.7, ...), kind=kLoop, calls=%fused_computation | loop fusion | flops 3932160 | bytes 4718592 | tf_op jit(solution)/shard_map/convert_element_type | solution.py:590
  111.9 11.1 %all-to-all-done.3.dqkv = bf16[16,2,96,128]{3,2,1,0:T(8,128)(2,1)S(1)} async-done(((bf16[16,2,96,128]{3,2,1,0:T(8,128)(2,1)}), bf16[16,2,96,128]{3,2,1,0:T(8,128)(2,1)S(1)}, u32[]{:S(2)}, u32[]{:S(2)}) %all-to-all-start.3) | async-done | bytes 786464 | tf_op jit(solution)/shard_map/all_to_all | solution.py:582
  123.0 3.6 %all-to-all-start.4 = ((bf16[16,3,4,16,128]{4,3,2,1,0:T(8,128)(2,1)}), bf16[16,3,4,16,128]{4,3,2,1,0:T(8,128)(2,1)S(1)}, u32[]{:S(2)}, u32[]{:S(2)}) async-start(bf16[16,3,4,16,128]{4,3,2,1,0:T(8,128)(2,1)} %add_convert_fusion), calls=%async_computation.4 | async-start | bytes 1572864 | tf_op jit(solution)/shard_map/all_to_all | solution.py:582
  126.6 5.0 %projection_backward.1 = (f32[256,512]{1,0:T(8,128)}, bf16[16,5,16,128]{3,2,1,0:T(8,128)(2,1)}, bf16[16,5,16,128]{3,2,1,0:T(8,128)(2,1)}, bf16[16,5,16,128]{3,2,...) custom-call(s32[1]{0:T(128)} %bitcast.place, ...), custom_call_target="tpu_custom_call" | custom-call | flops 805306368 | bytes 1048576 | tf_op jit(solution)/shard_map/projection_backward/pallas_call | solution.py:469
  131.6 1.1 collective-permute-start.1
  132.8 0.4 collective-permute-start.5
  133.3 0.9 collective-permute-done.1
  134.2 1.1 add_convert_fusion.7
  135.3 4.8 %all-to-all-done.4 = bf16[16,3,4,16,128]{4,3,2,1,0:T(8,128)(2,1)S(1)} async-done(((bf16[16,3,4,16,128]{4,3,2,1,0:T(8,128)(2,1)}), bf16[16,3,4,16,128]{4,3,2,1,0:T(8,128)(2,1)S(1)}, u32[]{:S(2)}, u32[]{:S(2)}) %all-to-all-start.4) | async-done | bytes 786464 | tf_op jit(solution)/shard_map/all_to_all | solution.py:582
  140.3 1.1 broadcast_in_dim.4
  141.4 3.6 %all-to-all-start.5 = ((bf16[16,3,4,16,128]{4,3,2,1,0:T(8,128)(2,1)}), bf16[16,3,4,16,128]{4,3,2,1,0:T(8,128)(2,1)S(1)}, u32[]{:S(2)}, u32[]{:S(2)}) async-start(bf16[16,3,4,16,128]{4,3,2,1,0:T(8,128)(2,1)} %broadcast_in_dim.4), calls=%async_computation.5 | async-start | bytes 1572864 | tf_op jit(solution)/shard_map/all_to_all | solution.py:582
  145.3 1.6 collective-permute-start.6
  146.9 10.5 %all-to-all-done.5.refs_0_ = bf16[16,3,4,16,128]{4,3,2,1,0:T(8,128)(2,1)S(1)} async-done(((bf16[16,3,4,16,128]{4,3,2,1,0:T(8,128)(2,1)}), bf16[16,3,4,16,128]{4,3,2,1,0:T(8,128)(2,1)S(1)}, u32[]{:S(2)}, u32[]{:S(2)}) %all-to-all-start.5) | async-done | bytes 786464 | tf_op jit(solution)/shard_map/all_to_all | solution.py:582
  157.4 3.6 %collective-permute-start.22 = (bf16[16,3,4,16,128]{4,3,2,1,0:T(8,128)(2,1)S(1)}, bf16[16,3,4,16,128]{4,3,2,1,0:T(8,128)(2,1)S(1)}, u32[]{:S(2)}, u32[]{:S(2)}) collective-permute-start(bf16[16,3,4,16,128]{4,3,2,1,0:T(8,128)(2,1)S(1)} %all-to-all-done.5.refs_0_), channel_id=1, source_target_pairs={{0,4},{2,6},{4,0},{6,2},{1,5},{3,7},{5,1},{7,3},{8,12},{10,14},{12... | collective-permute-start | bytes 2359304 | tf_op jit(solution)/shard_map/ppermute | solution.py:594
  161.0 2.3 %add_convert_fusion.4 = bf16[16,5,16,128]{3,2,1,0:T(8,128)(2,1)} fusion(bf16[16,5,16,128]{3,2,1,0:T(8,128)(2,1)} %collective-permute-done.6, bf16[16,5,16,128]{3,2,1,0:T(8,128)(2,1)} %collective-permute-done.4, bf16[16,5,16,128]{3,2,1,0:T(8,128)(2,1)} %collective-permute-done.2, bf16[16,5,16,128]{3,2,1,0:T(8,128)(2,1)} %collective-permute-done, ...), kind=kLoop, calls=%fused_computation.4 | loop fusion | flops 1638400 | bytes 1966080 | tf_op jit(solution)/shard_map/convert_element_type | solution.py:590
  163.3 7.8 %all-to-all-start.6 = ((bf16[16,5,16,128]{3,2,1,0:T(8,128)(2,1)}), bf16[16,5,16,128]{3,2,1,0:T(8,128)(2,1)S(1)}, u32[]{:S(2)}, u32[]{:S(2)}) async-start(bf16[16,5,16,128]{3,2,1,0:T(8,128)(2,1)} %add_convert_fusion.4), calls=%async_computation.6 | async-start | bytes 655360 | tf_op jit(solution)/shard_map/all_to_all | solution.py:582
  171.1 4.1 %collective-permute-start.23 = (bf16[16,3,4,16,128]{4,3,2,1,0:T(8,128)(2,1)S(1)}, bf16[16,3,4,16,128]{4,3,2,1,0:T(8,128)(2,1)S(1)}, u32[]{:S(2)}, u32[]{:S(2)}) collective-permute-start(bf16[16,3,4,16,128]{4,3,2,1,0:T(8,128)(2,1)S(1)} %all-to-all-done.5.refs_0_), channel_id=1, source_target_pairs={{0,6},{2,0},{4,2},{6,4},{1,7},{3,1},{5,3},{7,5},{8,14},{10,8},{12,... | collective-permute-start | bytes 2359304 | tf_op jit(solution)/shard_map/ppermute | solution.py:594
  175.2 3.9 %all-to-all-done.6 = bf16[16,5,16,128]{3,2,1,0:T(8,128)(2,1)S(1)} async-done(((bf16[16,5,16,128]{3,2,1,0:T(8,128)(2,1)}), bf16[16,5,16,128]{3,2,1,0:T(8,128)(2,1)S(1)}, u32[]{:S(2)}, u32[]{:S(2)}) %all-to-all-start.6) | async-done | bytes 327712 | tf_op jit(solution)/shard_map/all_to_all | solution.py:582
  179.2 10.1 %all_to_all.42.refs_0_ = bf16[16,4,16,128]{3,2,1,0:T(8,128)(2,1)S(1)} all-to-all(bf16[16,4,16,128]{3,2,1,0:T(8,128)(2,1)S(1)} %broadcast_in_dim.5), channel_id=1, replica_groups=mesh['x'=4,'zh'=2,'c'=2,'y'=4,'zl'=2] {'zl','zh','x'}, dimensions={0} | all-to-all | bytes 524288 | tf_op jit(solution)/shard_map/all_to_all | solution.py:582
  189.3 3.7 %collective-permute-start.14 = (bf16[16,4,16,128]{3,2,1,0:T(8,128)(2,1)S(1)}, bf16[16,4,16,128]{3,2,1,0:T(8,128)(2,1)S(1)}, u32[]{:S(2)}, u32[]{:S(2)}) collective-permute-start(bf16[16,4,16,128]{3,2,1,0:T(8,128)(2,1)S(1)} %all_to_all.42.refs_0_), channel_id=1, source_target_pairs={{0,2},{2,4},{4,6},{6,0},{1,3},{3,5},{5,7},{7,1},{8,10},{10,12},{12... | collective-permute-start | bytes 786440 | tf_op jit(solution)/shard_map/ppermute | solution.py:594
  193.0 2.2 collective-permute-start.15
  195.4 3.6 %collective-permute-start.17 = (bf16[16,4,16,128]{3,2,1,0:T(8,128)(2,1)S(1)}, bf16[16,4,16,128]{3,2,1,0:T(8,128)(2,1)S(1)}, u32[]{:S(2)}, u32[]{:S(2)}) collective-permute-start(bf16[16,4,16,128]{3,2,1,0:T(8,128)(2,1)S(1)} %all_to_all.42.refs_0_), channel_id=1, source_target_pairs={{0,8},{8,0},{1,9},{9,1},{2,10},{10,2},{3,11},{11,3},{4,12},{12,4},... | collective-permute-start | bytes 786440 | tf_op jit(solution)/shard_map/ppermute | solution.py:609
  199.0 5.7 %collective-permute-start.18 = (bf16[16,4,16,128]{3,2,1,0:T(8,128)(2,1)S(1)}, bf16[16,4,16,128]{3,2,1,0:T(8,128)(2,1)S(1)}, u32[]{:S(2)}, u32[]{:S(2)}) collective-permute-start(bf16[16,4,16,128]{3,2,1,0:T(8,128)(2,1)S(1)} %collective-permute-done.14.refs_1_), channel_id=1, source_target_pairs={{0,8},{8,0},{1,9},{9,1},{2,10},{10,2},{3,11},{11,3},{4,12},{12,4},... | collective-permute-start | bytes 786440 | tf_op jit(solution)/shard_map/ppermute | solution.py:609
  204.9 3.2 %collective-permute-start.25 = (bf16[16,3,4,16,128]{4,3,2,1,0:T(8,128)(2,1)S(1)}, bf16[16,3,4,16,128]{4,3,2,1,0:T(8,128)(2,1)}, u32[]{:S(2)}, u32[]{:S(2)}) collective-permute-start(bf16[16,3,4,16,128]{4,3,2,1,0:T(8,128)(2,1)S(1)} %collective-permute-done.21.refs_1_), channel_id=1, source_target_pairs={{0,8},{8,0},{1,9},{9,1},{2,10},{10,2},{3,11},{11,3},{4,12},{12,4},... | collective-permute-start | bytes 2359304 | tf_op jit(solution)/shard_map/ppermute | solution.py:609
  208.2 0.4 collective-permute-start.27
  208.7 2.0 collective-permute-done.19.refs_6_
  210.8 0.7 copy-done.16
  211.8 0.6 fusion
  212.4 0.7 collective-permute-done.20.refs_7_
  213.1 3.8 %unpack_projections.1 = (f32[512,512]{1,0:T(8,128)}, f32[512,512]{1,0:T(8,128)}, f32[512,512]{1,0:T(8,128)}, f32[512,512]{1,0:T(8,128)}) custom-call(s32[1]{0:T(128)} %bitcast.place, bf16[16,4,16,128]{3,2,1,0:T(8,128)(2,1)} %copy-done.2, bf16[16,4,16,128]{3,2,1,0:T(8,128)(2,1)} %copy-done.11, bf16[16,4,16,128]{3,2,1,0:T(8,128)(2,1)} %copy-done.12, ...), custom_call_target="tpu_custom_call" | custom-call | flops 1048576 | bytes 6291456 | tf_op jit(solution)/shard_map/unpack_projections/pallas_call | solution.py:557
  217.0 6.7 %unpack_feed_forward.1 = (f32[8,64,2048]{2,1,0:T(8,128)}, f32[8,64,2048]{2,1,0:T(8,128)}, f32[4,8,64,512]{3,2,1,0:T(8,128)}) custom-call(s32[1]{0:T(128)} %bitcast.place, bf16[16,3,4,16,128]{4,3,2,1,0:T(8,128)(2,1)} %copy-done, bf16[16,3,4,16,128]{4,3,2,1,0:T(8,128)(2,1)} %copy-done.3, bf16[16,3,4,16,128]{4,3,2,1,0:T(8,128)(2,1)} %copy-done.4, ...), custom_call_target="tpu_custom_call" | custom-call | flops 1048576 | bytes 18874368 | tf_op jit(solution)/shard_map/unpack_feed_forward/pallas_call | solution.py:515
  (79 shorter events, 1.9 us)
Async XLA Ops:
  63.2 10.1 %copy-start.8 = (bf16[16,3,4,16,128]{4,3,2,1,0:T(8,128)(2,1)S(1)}, bf16[16,3,4,16,128]{4,3,2,1,0:T(8,128)(2,1)}, u32[]{:S(2)}) copy-start(bf16[16,3,4,16,128]{4,3,2,1,0:T(8,128)(2,1)} %get-tuple-element.66) | copy-start | bytes 2359300
  63.2 4.8 %collective-permute-start.10 = (bf16[16,3,4,16,128]{4,3,2,1,0:T(8,128)(2,1)}, bf16[16,3,4,16,128]{4,3,2,1,0:T(8,128)(2,1)S(1)}, u32[]{:S(2)}, u32[]{:S(2)}) collective-permute-start(bf16[16,3,4,16,128]{4,3,2,1,0:T(8,128)(2,1)} %get-tuple-element.69), channel_id=1, source_target_pairs={{0,8},{8,0},{1,9},{9,1},{2,10},{10,2},{3,11},{11,3},{4,12},{12,4},... | collective-permute-start | bytes 2359304 | tf_op jit(solution)/shard_map/ppermute | solution.py:598
  63.7 9.6 %collective-permute-start.8 = (bf16[16,3,4,16,128]{4,3,2,1,0:T(8,128)(2,1)}, bf16[16,3,4,16,128]{4,3,2,1,0:T(8,128)(2,1)}, u32[]{:S(2)}, u32[]{:S(2)}) collective-permute-start(bf16[16,3,4,16,128]{4,3,2,1,0:T(8,128)(2,1)} %get-tuple-element.67), channel_id=1, source_target_pairs={{0,8},{8,0},{1,9},{9,1},{2,10},{10,2},{3,11},{11,3},{4,12},{12,4},... | collective-permute-start | bytes 2359304 | tf_op jit(solution)/shard_map/ppermute | solution.py:598
  63.8 12.2 %collective-permute-start.12 = (bf16[16,3,4,16,128]{4,3,2,1,0:T(8,128)(2,1)}, bf16[16,3,4,16,128]{4,3,2,1,0:T(8,128)(2,1)S(1)}, u32[]{:S(2)}, u32[]{:S(2)}) collective-permute-start(bf16[16,3,4,16,128]{4,3,2,1,0:T(8,128)(2,1)} %get-tuple-element.71), channel_id=1, source_target_pairs={{0,8},{8,0},{1,9},{9,1},{2,10},{10,2},{3,11},{11,3},{4,12},{12,4},... | collective-permute-start | bytes 2359304 | tf_op jit(solution)/shard_map/ppermute | solution.py:598
  64.2 44.6 %collective-permute-start.7 = (bf16[16,3,4,16,128]{4,3,2,1,0:T(8,128)(2,1)}, bf16[16,3,4,16,128]{4,3,2,1,0:T(8,128)(2,1)S(1)}, u32[]{:S(2)}, u32[]{:S(2)}) collective-permute-start(bf16[16,3,4,16,128]{4,3,2,1,0:T(8,128)(2,1)} %get-tuple-element.65), channel_id=1, source_target_pairs={{0,8},{8,0},{1,9},{9,1},{2,10},{10,2},{3,11},{11,3},{4,12},{12,4},... | collective-permute-start | bytes 2359304 | tf_op jit(solution)/shard_map/ppermute | solution.py:598
  64.3 15.1 %all-to-all-start.2 = ((bf16[16,2,32,128]{3,2,1,0:T(8,128)(2,1)}), bf16[16,2,32,128]{3,2,1,0:T(8,128)(2,1)S(1)}, u32[]{:S(2)}, u32[]{:S(2)}) async-start(bf16[16,2,32,128]{3,2,1,0:T(8,128)(2,1)} %get-tuple-element.50), calls=%async_computation.2 | async-start | bytes 524288 | tf_op jit(solution)/shard_map/all_to_all | solution.py:582
  70.4 5.6 %copy-start.7 = (bf16[16,3,4,16,128]{4,3,2,1,0:T(8,128)(2,1)S(1)}, bf16[16,3,4,16,128]{4,3,2,1,0:T(8,128)(2,1)}, u32[]{:S(2)}) copy-start(bf16[16,3,4,16,128]{4,3,2,1,0:T(8,128)(2,1)} %get-tuple-element.70) | copy-start | bytes 2359300
  70.4 38.4 %collective-permute-start.11 = (bf16[16,3,4,16,128]{4,3,2,1,0:T(8,128)(2,1)}, bf16[16,3,4,16,128]{4,3,2,1,0:T(8,128)(2,1)S(1)}, u32[]{:S(2)}, u32[]{:S(2)}) collective-permute-start(bf16[16,3,4,16,128]{4,3,2,1,0:T(8,128)(2,1)} %add_convert_fusion.2), channel_id=1, source_target_pairs={{0,4},{2,6},{4,0},{6,2},{1,5},{3,7},{5,1},{7,3},{8,12},{10,14},{12... | collective-permute-start | bytes 2359304 | tf_op jit(solution)/shard_map/ppermute | solution.py:594
  75.6 33.2 %collective-permute-start.9 = (bf16[16,3,4,16,128]{4,3,2,1,0:T(8,128)(2,1)}, bf16[16,3,4,16,128]{4,3,2,1,0:T(8,128)(2,1)}, u32[]{:S(2)}, u32[]{:S(2)}) collective-permute-start(bf16[16,3,4,16,128]{4,3,2,1,0:T(8,128)(2,1)} %add_convert_fusion.3), channel_id=1, source_target_pairs={{0,2},{2,4},{4,6},{6,0},{1,3},{3,5},{5,7},{7,1},{8,10},{10,12},{12... | collective-permute-start | bytes 2359304 | tf_op jit(solution)/shard_map/ppermute | solution.py:594
  77.2 31.6 %collective-permute-start.13 = (bf16[16,3,4,16,128]{4,3,2,1,0:T(8,128)(2,1)}, bf16[16,3,4,16,128]{4,3,2,1,0:T(8,128)(2,1)}, u32[]{:S(2)}, u32[]{:S(2)}) collective-permute-start(bf16[16,3,4,16,128]{4,3,2,1,0:T(8,128)(2,1)} %add_convert_fusion.1), channel_id=1, source_target_pairs={{0,6},{2,0},{4,2},{6,4},{1,7},{3,1},{5,3},{7,5},{8,14},{10,8},{12,... | collective-permute-start | bytes 2359304 | tf_op jit(solution)/shard_map/ppermute | solution.py:594
  100.6 8.3 %copy-start.6 = (bf16[16,3,4,16,128]{4,3,2,1,0:T(8,128)(2,1)S(1)}, bf16[16,3,4,16,128]{4,3,2,1,0:T(8,128)(2,1)}, u32[]{:S(2)}) copy-start(bf16[16,3,4,16,128]{4,3,2,1,0:T(8,128)(2,1)} %get-tuple-element.64) | copy-start | bytes 2359300
  100.6 22.4 %all-to-all-start.3 = ((bf16[16,2,96,128]{3,2,1,0:T(8,128)(2,1)}), bf16[16,2,96,128]{3,2,1,0:T(8,128)(2,1)S(1)}, u32[]{:S(2)}, u32[]{:S(2)}) async-start(bf16[16,2,96,128]{3,2,1,0:T(8,128)(2,1)} %attend_backward.1), calls=%async_computation.3 | async-start | bytes 1572864 | tf_op jit(solution)/shard_map/all_to_all | solution.py:582
  123.0 3.6 %copy-start.1 = (bf16[16,2,96,128]{3,2,1,0:T(8,128)(2,1)}, bf16[16,2,96,128]{3,2,1,0:T(8,128)(2,1)S(1)}, u32[]{:S(2)}) copy-start(bf16[16,2,96,128]{3,2,1,0:T(8,128)(2,1)S(1)} %all-to-all-done.3.dqkv) | copy-start | bytes 2359300
  123.0 17.2 %all-to-all-start.4 = ((bf16[16,3,4,16,128]{4,3,2,1,0:T(8,128)(2,1)}), bf16[16,3,4,16,128]{4,3,2,1,0:T(8,128)(2,1)S(1)}, u32[]{:S(2)}, u32[]{:S(2)}) async-start(bf16[16,3,4,16,128]{4,3,2,1,0:T(8,128)(2,1)} %add_convert_fusion), calls=%async_computation.4 | async-start | bytes 1572864 | tf_op jit(solution)/shard_map/all_to_all | solution.py:582
  131.6 2.6 %collective-permute-start.1 = (bf16[16,5,16,128]{3,2,1,0:T(8,128)(2,1)}, bf16[16,5,16,128]{3,2,1,0:T(8,128)(2,1)S(1)}, u32[]{:S(2)}, u32[]{:S(2)}) collective-permute-start(bf16[16,5,16,128]{3,2,1,0:T(8,128)(2,1)} %get-tuple-element.59), channel_id=1, source_target_pairs={{0,8},{8,0},{1,9},{9,1},{2,10},{10,2},{3,11},{11,3},{4,12},{12,4},... | collective-permute-start | bytes 983048 | tf_op jit(solution)/shard_map/ppermute | solution.py:598
  132.7 12.3 %collective-permute-start.3 = (bf16[16,5,16,128]{3,2,1,0:T(8,128)(2,1)}, bf16[16,5,16,128]{3,2,1,0:T(8,128)(2,1)S(1)}, u32[]{:S(2)}, u32[]{:S(2)}) collective-permute-start(bf16[16,5,16,128]{3,2,1,0:T(8,128)(2,1)} %get-tuple-element.61), channel_id=1, source_target_pairs={{0,8},{8,0},{1,9},{9,1},{2,10},{10,2},{3,11},{11,3},{4,12},{12,4},... | collective-permute-start | bytes 983048 | tf_op jit(solution)/shard_map/ppermute | solution.py:598
  132.8 12.4 %collective-permute-start.5 = (bf16[16,5,16,128]{3,2,1,0:T(8,128)(2,1)}, bf16[16,5,16,128]{3,2,1,0:T(8,128)(2,1)S(1)}, u32[]{:S(2)}, u32[]{:S(2)}) collective-permute-start(bf16[16,5,16,128]{3,2,1,0:T(8,128)(2,1)} %get-tuple-element.63), channel_id=1, source_target_pairs={{0,8},{8,0},{1,9},{9,1},{2,10},{10,2},{3,11},{11,3},{4,12},{12,4},... | collective-permute-start | bytes 983048 | tf_op jit(solution)/shard_map/ppermute | solution.py:598
  133.2 24.1 %collective-permute-start = (bf16[16,5,16,128]{3,2,1,0:T(8,128)(2,1)}, bf16[16,5,16,128]{3,2,1,0:T(8,128)(2,1)}, u32[]{:S(2)}, u32[]{:S(2)}) collective-permute-start(bf16[16,5,16,128]{3,2,1,0:T(8,128)(2,1)} %get-tuple-element.57), channel_id=1, source_target_pairs={{0,8},{8,0},{1,9},{9,1},{2,10},{10,2},{3,11},{11,3},{4,12},{12,4},... | collective-permute-start | bytes 983048 | tf_op jit(solution)/shard_map/ppermute | solution.py:598
  135.2 9.7 %copy-start.10 = (bf16[16,5,16,128]{3,2,1,0:T(8,128)(2,1)S(1)}, bf16[16,5,16,128]{3,2,1,0:T(8,128)(2,1)}, u32[]{:S(2)}) copy-start(bf16[16,5,16,128]{3,2,1,0:T(8,128)(2,1)} %get-tuple-element.60) | copy-start | bytes 983044
  135.3 25.7 %collective-permute-start.2 = (bf16[16,5,16,128]{3,2,1,0:T(8,128)(2,1)S(1)}, bf16[16,5,16,128]{3,2,1,0:T(8,128)(2,1)}, u32[]{:S(2)}, u32[]{:S(2)}) collective-permute-start(bf16[16,5,16,128]{3,2,1,0:T(8,128)(2,1)S(1)} %add_convert_fusion.7), channel_id=1, source_target_pairs={{0,2},{2,4},{4,6},{6,0},{1,3},{3,5},{5,7},{7,1},{8,10},{10,12},{12... | collective-permute-start | bytes 983048 | tf_op jit(solution)/shard_map/ppermute | solution.py:594
  140.3 4.9 %copy-start.9 = (bf16[16,5,16,128]{3,2,1,0:T(8,128)(2,1)S(1)}, bf16[16,5,16,128]{3,2,1,0:T(8,128)(2,1)}, u32[]{:S(2)}) copy-start(bf16[16,5,16,128]{3,2,1,0:T(8,128)(2,1)} %get-tuple-element.62) | copy-start | bytes 983044
  141.4 16.0 %all-to-all-start.5 = ((bf16[16,3,4,16,128]{4,3,2,1,0:T(8,128)(2,1)}), bf16[16,3,4,16,128]{4,3,2,1,0:T(8,128)(2,1)S(1)}, u32[]{:S(2)}, u32[]{:S(2)}) async-start(bf16[16,3,4,16,128]{4,3,2,1,0:T(8,128)(2,1)} %broadcast_in_dim.4), calls=%async_computation.5 | async-start | bytes 1572864 | tf_op jit(solution)/shard_map/all_to_all | solution.py:582
  145.1 15.9 %collective-permute-start.4 = (bf16[16,5,16,128]{3,2,1,0:T(8,128)(2,1)S(1)}, bf16[16,5,16,128]{3,2,1,0:T(8,128)(2,1)}, u32[]{:S(2)}, u32[]{:S(2)}) collective-permute-start(bf16[16,5,16,128]{3,2,1,0:T(8,128)(2,1)S(1)} %add_convert_fusion.6), channel_id=1, source_target_pairs={{0,4},{2,6},{4,0},{6,2},{1,5},{3,7},{5,1},{7,3},{8,12},{10,14},{12... | collective-permute-start | bytes 983048 | tf_op jit(solution)/shard_map/ppermute | solution.py:594
  145.3 15.7 %collective-permute-start.6 = (bf16[16,5,16,128]{3,2,1,0:T(8,128)(2,1)S(1)}, bf16[16,5,16,128]{3,2,1,0:T(8,128)(2,1)}, u32[]{:S(2)}, u32[]{:S(2)}) collective-permute-start(bf16[16,5,16,128]{3,2,1,0:T(8,128)(2,1)S(1)} %add_convert_fusion.5), channel_id=1, source_target_pairs={{0,6},{2,0},{4,2},{6,4},{1,7},{3,1},{5,3},{7,5},{8,14},{10,8},{12,... | collective-permute-start | bytes 983048 | tf_op jit(solution)/shard_map/ppermute | solution.py:594
  157.4 47.4 %copy-start = (bf16[16,3,4,16,128]{4,3,2,1,0:T(8,128)(2,1)}, bf16[16,3,4,16,128]{4,3,2,1,0:T(8,128)(2,1)S(1)}, u32[]{:S(2)}) copy-start(bf16[16,3,4,16,128]{4,3,2,1,0:T(8,128)(2,1)S(1)} %all-to-all-done.5.refs_0_) | copy-start | bytes 2359300
  157.4 37.8 %collective-permute-start.21 = (bf16[16,3,4,16,128]{4,3,2,1,0:T(8,128)(2,1)S(1)}, bf16[16,3,4,16,128]{4,3,2,1,0:T(8,128)(2,1)S(1)}, u32[]{:S(2)}, u32[]{:S(2)}) collective-permute-start(bf16[16,3,4,16,128]{4,3,2,1,0:T(8,128)(2,1)S(1)} %all-to-all-done.5.refs_0_), channel_id=1, source_target_pairs={{0,2},{2,4},{4,6},{6,0},{1,3},{3,5},{5,7},{7,1},{8,10},{10,12},{12... | collective-permute-start | bytes 2359304 | tf_op jit(solution)/shard_map/ppermute | solution.py:594
  157.4 38.0 %collective-permute-start.22 = (bf16[16,3,4,16,128]{4,3,2,1,0:T(8,128)(2,1)S(1)}, bf16[16,3,4,16,128]{4,3,2,1,0:T(8,128)(2,1)S(1)}, u32[]{:S(2)}, u32[]{:S(2)}) collective-permute-start(bf16[16,3,4,16,128]{4,3,2,1,0:T(8,128)(2,1)S(1)} %all-to-all-done.5.refs_0_), channel_id=1, source_target_pairs={{0,4},{2,6},{4,0},{6,2},{1,5},{3,7},{5,1},{7,3},{8,12},{10,14},{12... | collective-permute-start | bytes 2359304 | tf_op jit(solution)/shard_map/ppermute | solution.py:594
  163.3 15.8 %all-to-all-start.6 = ((bf16[16,5,16,128]{3,2,1,0:T(8,128)(2,1)}), bf16[16,5,16,128]{3,2,1,0:T(8,128)(2,1)S(1)}, u32[]{:S(2)}, u32[]{:S(2)}) async-start(bf16[16,5,16,128]{3,2,1,0:T(8,128)(2,1)} %add_convert_fusion.4), calls=%async_computation.6 | async-start | bytes 655360 | tf_op jit(solution)/shard_map/all_to_all | solution.py:582
  171.1 33.7 %collective-permute-start.23 = (bf16[16,3,4,16,128]{4,3,2,1,0:T(8,128)(2,1)S(1)}, bf16[16,3,4,16,128]{4,3,2,1,0:T(8,128)(2,1)S(1)}, u32[]{:S(2)}, u32[]{:S(2)}) collective-permute-start(bf16[16,3,4,16,128]{4,3,2,1,0:T(8,128)(2,1)S(1)} %all-to-all-done.5.refs_0_), channel_id=1, source_target_pairs={{0,6},{2,0},{4,2},{6,4},{1,7},{3,1},{5,3},{7,5},{8,14},{10,8},{12,... | collective-permute-start | bytes 2359304 | tf_op jit(solution)/shard_map/ppermute | solution.py:594
  189.3 23.8 %copy-start.2 = (bf16[16,4,16,128]{3,2,1,0:T(8,128)(2,1)}, bf16[16,4,16,128]{3,2,1,0:T(8,128)(2,1)S(1)}, u32[]{:S(2)}) copy-start(bf16[16,4,16,128]{3,2,1,0:T(8,128)(2,1)S(1)} %all_to_all.42.refs_0_) | copy-start | bytes 786436
  189.3 9.7 %collective-permute-start.14 = (bf16[16,4,16,128]{3,2,1,0:T(8,128)(2,1)S(1)}, bf16[16,4,16,128]{3,2,1,0:T(8,128)(2,1)S(1)}, u32[]{:S(2)}, u32[]{:S(2)}) collective-permute-start(bf16[16,4,16,128]{3,2,1,0:T(8,128)(2,1)S(1)} %all_to_all.42.refs_0_), channel_id=1, source_target_pairs={{0,2},{2,4},{4,6},{6,0},{1,3},{3,5},{5,7},{7,1},{8,10},{10,12},{12... | collective-permute-start | bytes 786440 | tf_op jit(solution)/shard_map/ppermute | solution.py:594
  193.0 11.9 %collective-permute-start.15 = (bf16[16,4,16,128]{3,2,1,0:T(8,128)(2,1)S(1)}, bf16[16,4,16,128]{3,2,1,0:T(8,128)(2,1)S(1)}, u32[]{:S(2)}, u32[]{:S(2)}) collective-permute-start(bf16[16,4,16,128]{3,2,1,0:T(8,128)(2,1)S(1)} %all_to_all.42.refs_0_), channel_id=1, source_target_pairs={{0,4},{2,6},{4,0},{6,2},{1,5},{3,7},{5,1},{7,3},{8,12},{10,14},{12... | collective-permute-start | bytes 786440 | tf_op jit(solution)/shard_map/ppermute | solution.py:594
  195.2 21.8 %copy-start.3 = (bf16[16,3,4,16,128]{4,3,2,1,0:T(8,128)(2,1)}, bf16[16,3,4,16,128]{4,3,2,1,0:T(8,128)(2,1)S(1)}, u32[]{:S(2)}) copy-start(bf16[16,3,4,16,128]{4,3,2,1,0:T(8,128)(2,1)S(1)} %collective-permute-done.21.refs_1_) | copy-start | bytes 2359300
  195.2 12.9 %collective-permute-start.16 = (bf16[16,4,16,128]{3,2,1,0:T(8,128)(2,1)S(1)}, bf16[16,4,16,128]{3,2,1,0:T(8,128)(2,1)S(1)}, u32[]{:S(2)}, u32[]{:S(2)}) collective-permute-start(bf16[16,4,16,128]{3,2,1,0:T(8,128)(2,1)S(1)} %all_to_all.42.refs_0_), channel_id=1, source_target_pairs={{0,6},{2,0},{4,2},{6,4},{1,7},{3,1},{5,3},{7,5},{8,14},{10,8},{12,... | collective-permute-start | bytes 786440 | tf_op jit(solution)/shard_map/ppermute | solution.py:594
  195.4 21.6 %copy-start.4 = (bf16[16,3,4,16,128]{4,3,2,1,0:T(8,128)(2,1)}, bf16[16,3,4,16,128]{4,3,2,1,0:T(8,128)(2,1)S(1)}, u32[]{:S(2)}) copy-start(bf16[16,3,4,16,128]{4,3,2,1,0:T(8,128)(2,1)S(1)} %collective-permute-done.22.refs_2_) | copy-start | bytes 2359300
  195.4 12.8 %collective-permute-start.17 = (bf16[16,4,16,128]{3,2,1,0:T(8,128)(2,1)S(1)}, bf16[16,4,16,128]{3,2,1,0:T(8,128)(2,1)S(1)}, u32[]{:S(2)}, u32[]{:S(2)}) collective-permute-start(bf16[16,4,16,128]{3,2,1,0:T(8,128)(2,1)S(1)} %all_to_all.42.refs_0_), channel_id=1, source_target_pairs={{0,8},{8,0},{1,9},{9,1},{2,10},{10,2},{3,11},{11,3},{4,12},{12,4},... | collective-permute-start | bytes 786440 | tf_op jit(solution)/shard_map/ppermute | solution.py:609
  199.0 14.1 %copy-start.11 = (bf16[16,4,16,128]{3,2,1,0:T(8,128)(2,1)}, bf16[16,4,16,128]{3,2,1,0:T(8,128)(2,1)S(1)}, u32[]{:S(2)}) copy-start(bf16[16,4,16,128]{3,2,1,0:T(8,128)(2,1)S(1)} %collective-permute-done.14.refs_1_) | copy-start | bytes 786436
  199.0 9.6 %collective-permute-start.18 = (bf16[16,4,16,128]{3,2,1,0:T(8,128)(2,1)S(1)}, bf16[16,4,16,128]{3,2,1,0:T(8,128)(2,1)S(1)}, u32[]{:S(2)}, u32[]{:S(2)}) collective-permute-start(bf16[16,4,16,128]{3,2,1,0:T(8,128)(2,1)S(1)} %collective-permute-done.14.refs_1_), channel_id=1, source_target_pairs={{0,8},{8,0},{1,9},{9,1},{2,10},{10,2},{3,11},{11,3},{4,12},{12,4},... | collective-permute-start | bytes 786440 | tf_op jit(solution)/shard_map/ppermute | solution.py:609
  204.8 12.2 %copy-start.5 = (bf16[16,3,4,16,128]{4,3,2,1,0:T(8,128)(2,1)}, bf16[16,3,4,16,128]{4,3,2,1,0:T(8,128)(2,1)S(1)}, u32[]{:S(2)}) copy-start(bf16[16,3,4,16,128]{4,3,2,1,0:T(8,128)(2,1)S(1)} %collective-permute-done.23.refs_3_) | copy-start | bytes 2359300
  204.8 12.2 %collective-permute-start.24 = (bf16[16,3,4,16,128]{4,3,2,1,0:T(8,128)(2,1)S(1)}, bf16[16,3,4,16,128]{4,3,2,1,0:T(8,128)(2,1)}, u32[]{:S(2)}, u32[]{:S(2)}) collective-permute-start(bf16[16,3,4,16,128]{4,3,2,1,0:T(8,128)(2,1)S(1)} %all-to-all-done.5.refs_0_), channel_id=1, source_target_pairs={{0,8},{8,0},{1,9},{9,1},{2,10},{10,2},{3,11},{11,3},{4,12},{12,4},... | collective-permute-start | bytes 2359304 | tf_op jit(solution)/shard_map/ppermute | solution.py:609
  204.9 8.3 %copy-start.12 = (bf16[16,4,16,128]{3,2,1,0:T(8,128)(2,1)}, bf16[16,4,16,128]{3,2,1,0:T(8,128)(2,1)S(1)}, u32[]{:S(2)}) copy-start(bf16[16,4,16,128]{3,2,1,0:T(8,128)(2,1)S(1)} %collective-permute-done.15.refs_2_) | copy-start | bytes 786436
  204.9 12.1 %collective-permute-start.25 = (bf16[16,3,4,16,128]{4,3,2,1,0:T(8,128)(2,1)S(1)}, bf16[16,3,4,16,128]{4,3,2,1,0:T(8,128)(2,1)}, u32[]{:S(2)}, u32[]{:S(2)}) collective-permute-start(bf16[16,3,4,16,128]{4,3,2,1,0:T(8,128)(2,1)S(1)} %collective-permute-done.21.refs_1_), channel_id=1, source_target_pairs={{0,8},{8,0},{1,9},{9,1},{2,10},{10,2},{3,11},{11,3},{4,12},{12,4},... | collective-permute-start | bytes 2359304 | tf_op jit(solution)/shard_map/ppermute | solution.py:609
  208.1 2.7 %copy-start.13 = (bf16[16,4,16,128]{3,2,1,0:T(8,128)(2,1)}, bf16[16,4,16,128]{3,2,1,0:T(8,128)(2,1)S(1)}, u32[]{:S(2)}) copy-start(bf16[16,4,16,128]{3,2,1,0:T(8,128)(2,1)S(1)} %collective-permute-done.16.refs_3_) | copy-start | bytes 786436
  208.1 8.9 %collective-permute-start.26 = (bf16[16,3,4,16,128]{4,3,2,1,0:T(8,128)(2,1)S(1)}, bf16[16,3,4,16,128]{4,3,2,1,0:T(8,128)(2,1)}, u32[]{:S(2)}, u32[]{:S(2)}) collective-permute-start(bf16[16,3,4,16,128]{4,3,2,1,0:T(8,128)(2,1)S(1)} %collective-permute-done.22.refs_2_), channel_id=1, source_target_pairs={{0,8},{8,0},{1,9},{9,1},{2,10},{10,2},{3,11},{11,3},{4,12},{12,4},... | collective-permute-start | bytes 2359304 | tf_op jit(solution)/shard_map/ppermute | solution.py:609
  208.2 2.6 %copy-start.14 = (bf16[16,4,16,128]{3,2,1,0:T(8,128)(2,1)}, bf16[16,4,16,128]{3,2,1,0:T(8,128)(2,1)S(1)}, u32[]{:S(2)}) copy-start(bf16[16,4,16,128]{3,2,1,0:T(8,128)(2,1)S(1)} %collective-permute-done.17.refs_4_) | copy-start | bytes 786436
  208.2 8.8 %collective-permute-start.27 = (bf16[16,3,4,16,128]{4,3,2,1,0:T(8,128)(2,1)S(1)}, bf16[16,3,4,16,128]{4,3,2,1,0:T(8,128)(2,1)}, u32[]{:S(2)}, u32[]{:S(2)}) collective-permute-start(bf16[16,3,4,16,128]{4,3,2,1,0:T(8,128)(2,1)S(1)} %collective-permute-done.23.refs_3_), channel_id=1, source_target_pairs={{0,8},{8,0},{1,9},{9,1},{2,10},{10,2},{3,11},{11,3},{4,12},{12,4},... | collective-permute-start | bytes 2359304 | tf_op jit(solution)/shard_map/ppermute | solution.py:609
  208.6 2.1 collective-permute-start.19
  211.4 1.7 collective-permute-start.20
  (3 other events, 3.5 us)
